TPU v7x, 256 devices: a whole 4x4x8 slice. The times are simulated.
256 devices in a mesh: ctx: 32 (over y, x, core), mp: 8 (over z).
Axes of the slice: x: 4, y: 4, z: 8, core: 2. Of those that a mesh axis runs over, the one named last changes fastest.
Arguments:
- clip_store: bfloat16 [64, 512, 5120], P('ctx', None, 'mp'), may hold values from -96 to 96
- text_tokens: bfloat16 [4, 512, 5120], P(None, 'ctx', 'mp'), may hold values from -96 to 96
- candidates: int32 [4, 4], replicated, may hold values from 0 to 63, as said below
- clip_slot: int32 [64], replicated, may hold values from 0 to 63, as said below
- text_positions: int32 [4, 512], replicated, may hold values from 2048 to 2814, as said below
- block_order: int32 [64], replicated, may hold values from 0 to 63, as said below
- w_query: bfloat16 [5120, 5120], P(None, 'mp'), may hold values from -0.078125 to 0.078125
- b_query: bfloat16 [5120], P('mp'), may hold values from -6 to 6
- key_value_weight: bfloat16 [5120, 2, 1024], P(None, None, 'mp'), may hold values from -0.078125 to 0.078125
- value_offset_bias: bfloat16 [1024], P('mp'), may hold values from -3 to 3
Outputs:
- attended: bfloat16 [4, 64, 40, 5120], P(None, 'ctx', None, 'mp')
Inputs may be any that keep to these rules, and one draw needn't show every extreme that they name: `candidates`: the 16 candidate clips lie on distinct store shards: the values clip_slot[c] // 2 differ for all of them. `clip_slot`: a permutation of the store rows. `text_positions`: along each query's text tokens the positions rise by 1 or 2 from 2048. `block_order`: a permutation; slots 2 i and 2 i + 1 hold blocks c and 63 - c for some c.
All inputs are finite; a program needn't handle non-finite values.
Results may differ from a plain program's by a relative error of at most 0.017.
The roundings to bfloat16 on the way count: a program that leaves them out, or rounds other values in their place, can miss the bound.
Values may be sent and summed in bfloat16 or wider, within the bound.
No kernel may reach another device: no remote copies, remote signals or barrier semaphores. Data moves between devices by JAX's collectives and lax.ppermute only.
A program may use at most 64 MiB of HBM per device.

v0:
```python
import math

import jax
import jax.numpy as jnp
from jax import lax
from jax.sharding import PartitionSpec as P

HEAD_SIZE = 128


NEG_FILL = -1e30
ROPE_BASE = 1000000.0


def broadcast(block, axis, owner):
    block = jnp.where(lax.axis_index(axis) == owner, block, jnp.zeros_like(block))
    return lax.psum(block, axis)


def apply_rotation(value_rows, positions, head_dim):
    half_dim = head_dim // 2
    frequency = ROPE_BASE ** (-(jnp.arange(half_dim, dtype=jnp.float32) * 2.0) / head_dim)
    angles = positions.astype(jnp.float32)[..., None] * frequency
    angles = jnp.concatenate([angles, angles], axis=-1)
    cosine = jnp.cos(angles)[..., None, :]
    sine_table = jnp.sin(angles)[..., None, :]
    first_half = value_rows[..., :half_dim]
    second = value_rows[..., half_dim:]
    turned = jnp.concatenate([-second, first_half], axis=-1)
    return value_rows * cosine + turned * sine_table


def per_device(
    clip_store,
    text_tokens,
    candidates,
    clip_slot,
    text_positions,
    block_order,
    w_query,
    b_query,
    key_value_weight,
    value_offset_bias,
):
    my_index = lax.axis_index("ctx")
    clips_here, clip_len, feat_here = clip_store.shape
    seq_count, cand_count = candidates.shape
    text_len = text_positions.shape[1]
    block_count = block_order.shape[0]
    visual_len = cand_count * clip_len
    block_len = (visual_len + text_len) // block_count
    model_width = w_query.shape[0]
    my_blocks = lax.dynamic_slice_in_dim(block_order, 2 * my_index, 2)
    offsets = jnp.arange(block_len, dtype=jnp.int32)
    row_pos = my_blocks[:, None] * block_len + offsets[None, :]
    seq_ids = jnp.arange(seq_count, dtype=jnp.int32)
    cand_slots = jnp.take(clip_slot, candidates.reshape(-1))
    token_rows = jnp.zeros((seq_count, 2, block_len, feat_here), clip_store.dtype)

    def fetch_one(entry_number, current):
        seq_here = entry_number // cand_count
        part_here = entry_number % cand_count
        store_slot = cand_slots[entry_number]
        held_clip = lax.dynamic_index_in_dim(clip_store, store_slot % clips_here, 0, keepdims=False)
        fetched = broadcast(held_clip, "ctx", store_slot // clips_here)
        offset_in = row_pos - part_here * clip_len
        inside = (offset_in >= 0) & (offset_in < clip_len)
        picked = jnp.take(fetched, jnp.clip(offset_in, 0, clip_len - 1), axis=0)
        keep_mask = inside[None, :, :, None] & (seq_ids == seq_here)[:, None, None, None]
        return jnp.where(keep_mask, picked[None], current)

    token_rows = lax.fori_loop(0, seq_count * cand_count, fetch_one, token_rows)
    text_index = row_pos - visual_len
    piece = lax.all_gather(text_tokens, "ctx", axis=1, tiled=True)
    piece_len = piece.shape[1]
    offset_in = text_index
    inside = (offset_in >= 0) & (offset_in < piece_len)
    picked = jnp.take(piece, jnp.clip(offset_in, 0, piece_len - 1).reshape(-1), axis=1)
    picked = picked.reshape(seq_count, 2, block_len, feat_here)
    token_rows = jnp.where(inside[None, :, :, None], picked, token_rows)
    kv_flat = key_value_weight.reshape(model_width, -1)
    query_cols = w_query.shape[1]
    kv_cols = kv_flat.shape[1]
    row_count = seq_count * 2 * block_len
    piece = lax.all_gather(token_rows, "mp", axis=3, tiled=True)
    piece_len = piece.shape[3]
    flat_piece = piece.reshape(row_count, piece_len)
    query_sum = jnp.dot(flat_piece, w_query, preferred_element_type=jnp.float32)
    kv_sum = jnp.dot(flat_piece, kv_flat, preferred_element_type=jnp.float32)
    text_at = jnp.take(
        text_positions, jnp.clip(text_index, 0, text_len - 1).reshape(-1), axis=1
    ).reshape(seq_count, 2, block_len)
    rotary_positions = jnp.where(row_pos[None] < visual_len, row_pos[None], text_at)
    heads_here = query_cols // HEAD_SIZE
    kv_here = kv_cols // (2 * HEAD_SIZE)
    heads_per_group = heads_here // kv_here
    query_full = (query_sum + b_query.astype(jnp.float32)).reshape(
        seq_count, 2 * block_len, heads_here, HEAD_SIZE
    )
    query_vectors = apply_rotation(
        query_full, rotary_positions.reshape(seq_count, 2 * block_len), HEAD_SIZE
    ).astype(jnp.bfloat16)
    key_full = kv_sum[:, : kv_here * HEAD_SIZE].reshape(seq_count, 2, block_len, kv_here, HEAD_SIZE)
    rotated_key_rows = (
        apply_rotation(key_full, rotary_positions, HEAD_SIZE)
        .astype(jnp.bfloat16)
        .reshape(seq_count, 2, block_len, kv_here * HEAD_SIZE)
    )
    value_rows = (kv_sum[:, kv_here * HEAD_SIZE :] + value_offset_bias.astype(jnp.float32)).astype(
        jnp.bfloat16
    )
    value_rows = value_rows.reshape(seq_count, 2, block_len, kv_here * HEAD_SIZE)
    query_rows = query_vectors.reshape(
        seq_count, 2 * block_len, kv_here, heads_per_group, HEAD_SIZE
    )
    query_pos = row_pos.reshape(-1)
    score_scale = 1.0 / math.sqrt(HEAD_SIZE)

    def attend_block(carry_state, inputs):
        key_block, value_block, key_pos = inputs
        run_max, run_sum, accumulated = carry_state
        scores = (
            jnp.einsum(
                "sqkgd,snkd->skgqn", query_rows, key_block, preferred_element_type=jnp.float32
            )
            * score_scale
        )
        allowed = key_pos[None, :] <= query_pos[:, None]
        scores = jnp.where(allowed, scores, NEG_FILL)
        new_max = jnp.maximum(run_max, jnp.max(scores, axis=-1))
        weights = jnp.where(allowed, jnp.exp(scores - new_max[..., None]), 0.0)
        shrink = jnp.exp(run_max - new_max)
        run_sum = run_sum * shrink + jnp.sum(weights, axis=-1)
        accumulated = accumulated * shrink[..., None] + jnp.einsum(
            "skgqn,snkd->skgqd",
            weights.astype(jnp.bfloat16),
            value_block,
            preferred_element_type=jnp.float32,
        )
        return ((new_max, run_sum, accumulated), None)

    stat_shape = (seq_count, kv_here, heads_per_group, 2 * block_len)
    carry_state = (
        jnp.full(stat_shape, NEG_FILL, jnp.float32),
        jnp.zeros(stat_shape, jnp.float32),
        jnp.zeros(stat_shape + (HEAD_SIZE,), jnp.float32),
    )
    fold_carry_state = carry_state
    key_piece = lax.all_gather(rotated_key_rows, "ctx", axis=1, tiled=True)
    value_piece = lax.all_gather(value_rows, "ctx", axis=1, tiled=True)
    piece_len = key_piece.shape[1]
    group_len = math.gcd(piece_len, 16)
    step_count = piece_len // group_len
    slot_ids = jnp.arange(piece_len, dtype=jnp.int32)
    key_pos = (jnp.take(block_order, slot_ids)[:, None] * block_len + offsets[None, :]).reshape(
        step_count, group_len * block_len
    )
    key_blocks = jnp.moveaxis(
        key_piece.reshape(seq_count, step_count, group_len * block_len, kv_here, HEAD_SIZE), 1, 0
    )
    value_blocks = jnp.moveaxis(
        value_piece.reshape(seq_count, step_count, group_len * block_len, kv_here, HEAD_SIZE), 1, 0
    )
    fold_carry_state, unused = lax.scan(
        attend_block, fold_carry_state, (key_blocks, value_blocks, key_pos)
    )
    carry_state = fold_carry_state
    run_max, run_sum, accumulated = carry_state
    head_outputs = accumulated / run_sum[..., None]
    head_outputs = jnp.transpose(head_outputs, (0, 3, 1, 2, 4)).reshape(
        seq_count, 2, block_len, heads_here * HEAD_SIZE
    )
    return head_outputs.astype(jnp.bfloat16)


def solution(mesh):
    placed = (
        P("ctx", None, "mp"),
        P(None, "ctx", "mp"),
        P(),
        P(),
        P(),
        P(),
        P(None, "mp"),
        P("mp"),
        P(None, None, "mp"),
        P("mp"),
    )
    return jax.shard_map(
        per_device,
        mesh=mesh,
        in_specs=placed,
        out_specs=P(None, "ctx", None, "mp"),
        check_vma=False,
    )
```

profile of v0, /device:TPU:1, one launch (start us, length us, event | category | flops | bytes accessed | tf_op | source)
XLA Modules:
  0.0 2191.3 jit_solution(12570384522665391096)
XLA Ops:
  11.4 52.3 %all-gather.5.cloned.1.call-done = bf16[4,512,640]{2,0,1:T(4,128)(2,1)} async-done(((bf16[4,16,640]{2,0,1:T(4,128)(2,1)}), bf16[4,512,640]{2,0,1:T(4,128)(2,1)}) %all-gather.5.cloned.1.call-update) | async-done | bytes 2621456 | tf_op jit(solution)/shard_map/all_gather | solution.py:74
  66.4 1924.6 %while.32 = (s32[]{:T(128)}, bf16[4,2,40,640]{3,2,1,0:T(8,128)(2,1)S(1)}, s32[16]{0:T(128)S(1)}, bf16[2,512,640]{2,1,0:T(8,128)(2,1)}, s32[2]{0:T(128)S(1)}, /*i...) while((s32[]{:T(128)}, ...), condition=%wide.region_2.3_spmd.clone, body=%wide.region_0.0_spmd.clone.sunk | while | flops 1118990 | bytes 6581361 | solution.py:72
  72.0 111.9 %all-reduce.2.cloned.1.call-done = bf16[512,640]{1,0:T(8,128)(2,1)} async-done(((bf16[512,640]{1,0:T(8,128)(2,1)}), bf16[512,640]{1,0:T(8,128)(2,1)}) %all-reduce.2.cloned.1.call-update) | async-done | bytes 655376 | tf_op jit(solution)/shard_map/while/body/eval_jaxpr/psum | solution.py:17
  191.8 112.5 %all-reduce.2.cloned.1.call-done = bf16[512,640]{1,0:T(8,128)(2,1)} async-done(((bf16[512,640]{1,0:T(8,128)(2,1)}), bf16[512,640]{1,0:T(8,128)(2,1)}) %all-reduce.2.cloned.1.call-update) | async-done | bytes 655376 | tf_op jit(solution)/shard_map/while/body/eval_jaxpr/psum | solution.py:17
  312.1 112.5 %all-reduce.2.cloned.1.call-done = bf16[512,640]{1,0:T(8,128)(2,1)} async-done(((bf16[512,640]{1,0:T(8,128)(2,1)}), bf16[512,640]{1,0:T(8,128)(2,1)}) %all-reduce.2.cloned.1.call-update) | async-done | bytes 655376 | tf_op jit(solution)/shard_map/while/body/eval_jaxpr/psum | solution.py:17
  432.4 112.5 %all-reduce.2.cloned.1.call-done = bf16[512,640]{1,0:T(8,128)(2,1)} async-done(((bf16[512,640]{1,0:T(8,128)(2,1)}), bf16[512,640]{1,0:T(8,128)(2,1)}) %all-reduce.2.cloned.1.call-update) | async-done | bytes 655376 | tf_op jit(solution)/shard_map/while/body/eval_jaxpr/psum | solution.py:17
  552.7 112.5 %all-reduce.2.cloned.1.call-done = bf16[512,640]{1,0:T(8,128)(2,1)} async-done(((bf16[512,640]{1,0:T(8,128)(2,1)}), bf16[512,640]{1,0:T(8,128)(2,1)}) %all-reduce.2.cloned.1.call-update) | async-done | bytes 655376 | tf_op jit(solution)/shard_map/while/body/eval_jaxpr/psum | solution.py:17
  673.1 112.5 %all-reduce.2.cloned.1.call-done = bf16[512,640]{1,0:T(8,128)(2,1)} async-done(((bf16[512,640]{1,0:T(8,128)(2,1)}), bf16[512,640]{1,0:T(8,128)(2,1)}) %all-reduce.2.cloned.1.call-update) | async-done | bytes 655376 | tf_op jit(solution)/shard_map/while/body/eval_jaxpr/psum | solution.py:17
  793.4 112.5 %all-reduce.2.cloned.1.call-done = bf16[512,640]{1,0:T(8,128)(2,1)} async-done(((bf16[512,640]{1,0:T(8,128)(2,1)}), bf16[512,640]{1,0:T(8,128)(2,1)}) %all-reduce.2.cloned.1.call-update) | async-done | bytes 655376 | tf_op jit(solution)/shard_map/while/body/eval_jaxpr/psum | solution.py:17
  913.7 112.5 %all-reduce.2.cloned.1.call-done = bf16[512,640]{1,0:T(8,128)(2,1)} async-done(((bf16[512,640]{1,0:T(8,128)(2,1)}), bf16[512,640]{1,0:T(8,128)(2,1)}) %all-reduce.2.cloned.1.call-update) | async-done | bytes 655376 | tf_op jit(solution)/shard_map/while/body/eval_jaxpr/psum | solution.py:17
  1034.0 112.5 %all-reduce.2.cloned.1.call-done = bf16[512,640]{1,0:T(8,128)(2,1)} async-done(((bf16[512,640]{1,0:T(8,128)(2,1)}), bf16[512,640]{1,0:T(8,128)(2,1)}) %all-reduce.2.cloned.1.call-update) | async-done | bytes 655376 | tf_op jit(solution)/shard_map/while/body/eval_jaxpr/psum | solution.py:17
  1154.4 112.5 %all-reduce.2.cloned.1.call-done = bf16[512,640]{1,0:T(8,128)(2,1)} async-done(((bf16[512,640]{1,0:T(8,128)(2,1)}), bf16[512,640]{1,0:T(8,128)(2,1)}) %all-reduce.2.cloned.1.call-update) | async-done | bytes 655376 | tf_op jit(solution)/shard_map/while/body/eval_jaxpr/psum | solution.py:17
  1274.7 112.5 %all-reduce.2.cloned.1.call-done = bf16[512,640]{1,0:T(8,128)(2,1)} async-done(((bf16[512,640]{1,0:T(8,128)(2,1)}), bf16[512,640]{1,0:T(8,128)(2,1)}) %all-reduce.2.cloned.1.call-update) | async-done | bytes 655376 | tf_op jit(solution)/shard_map/while/body/eval_jaxpr/psum | solution.py:17
  1395.0 112.5 %all-reduce.2.cloned.1.call-done = bf16[512,640]{1,0:T(8,128)(2,1)} async-done(((bf16[512,640]{1,0:T(8,128)(2,1)}), bf16[512,640]{1,0:T(8,128)(2,1)}) %all-reduce.2.cloned.1.call-update) | async-done | bytes 655376 | tf_op jit(solution)/shard_map/while/body/eval_jaxpr/psum | solution.py:17
  1515.3 112.5 %all-reduce.2.cloned.1.call-done = bf16[512,640]{1,0:T(8,128)(2,1)} async-done(((bf16[512,640]{1,0:T(8,128)(2,1)}), bf16[512,640]{1,0:T(8,128)(2,1)}) %all-reduce.2.cloned.1.call-update) | async-done | bytes 655376 | tf_op jit(solution)/shard_map/while/body/eval_jaxpr/psum | solution.py:17
  1635.6 112.5 %all-reduce.2.cloned.1.call-done = bf16[512,640]{1,0:T(8,128)(2,1)} async-done(((bf16[512,640]{1,0:T(8,128)(2,1)}), bf16[512,640]{1,0:T(8,128)(2,1)}) %all-reduce.2.cloned.1.call-update) | async-done | bytes 655376 | tf_op jit(solution)/shard_map/while/body/eval_jaxpr/psum | solution.py:17
  1756.0 112.5 %all-reduce.2.cloned.1.call-done = bf16[512,640]{1,0:T(8,128)(2,1)} async-done(((bf16[512,640]{1,0:T(8,128)(2,1)}), bf16[512,640]{1,0:T(8,128)(2,1)}) %all-reduce.2.cloned.1.call-update) | async-done | bytes 655376 | tf_op jit(solution)/shard_map/while/body/eval_jaxpr/psum | solution.py:17
  1876.3 112.5 %all-reduce.2.cloned.1.call-done = bf16[512,640]{1,0:T(8,128)(2,1)} async-done(((bf16[512,640]{1,0:T(8,128)(2,1)}), bf16[512,640]{1,0:T(8,128)(2,1)}) %all-reduce.2.cloned.1.call-update) | async-done | bytes 655376 | tf_op jit(solution)/shard_map/while/body/eval_jaxpr/psum | solution.py:17
  1993.1 45.6 %all-gather.7.cloned.1.call-done = bf16[4,2,40,5120]{3,2,1,0:T(8,128)(2,1)} async-done(((bf16[4,2,40,640]{3,2,1,0:T(8,128)(2,1)}), bf16[4,2,40,5120]{3,2,1,0:T(8,128)(2,1)}) %all-gather.7.cloned.1.call-update) | async-done | bytes 3276816 | tf_op jit(solution)/shard_map/all_gather | solution.py:85
  2038.7 3.8 fusion.32
  2048.3 6.6 convolution_add_fusion
  2056.8 36.9 %all-gather.9.cloned.1.call-done = bf16[4,64,40,128]{3,2,1,0:T(8,128)(2,1)} async-done(((bf16[4,2,40,128]{3,2,1,0:T(8,128)(2,1)}), bf16[4,64,40,128]{3,2,1,0:T(8,128)(2,1)}) %all-gather.9.cloned.1.call-update) | async-done | bytes 2621456 | tf_op jit(solution)/shard_map/all_gather | solution.py:149
  2093.7 51.3 %all-gather.11.cloned.1.call-done = bf16[4,64,40,128]{3,2,1,0:T(8,128)(2,1)} async-done(((bf16[4,2,40,128]{3,2,1,0:T(8,128)(2,1)}), bf16[4,64,40,128]{3,2,1,0:T(8,128)(2,1)}) %all-gather.11.cloned.1.call-update) | async-done | bytes 2621456 | tf_op jit(solution)/shard_map/all_gather | solution.py:150
  2144.9 37.8 %while.33 = (s32[]{:T(128)}, f32[4,1,5,80]{3,2,0,1:T(8,128)S(1)}, f32[4,1,5,80]{3,2,0,1:T(8,128)S(1)}, f32[4,1,5,80,128]{4,3,2,0,1:T(8,128)S(1)}, s32[4,640]{1,0...) while((s32[]{:T(128)}, f32[4,1,5,80]{3,2,0,1:T(8,128)S(1)}, ...), condition=%wide.region_6.7_spmd.clone, body=%wide.region_3.6_spmd.clone.sunk | while | flops 538275264 | bytes 32348064 | solution.py:164
  2145.2 3.9 fusion.62
  2149.1 3.9 fusion.65
  2154.7 3.9 fusion.62
  2158.6 3.9 fusion.65
  2164.1 3.9 fusion.62
  2168.0 3.9 fusion.65
  2173.6 3.9 fusion.62
  2177.5 3.9 fusion.65
  (332 shorter events, 108.4 us)
Async XLA Ops:
  6.5 4.0 copy-start
  6.5 57.1 %all-gather.5.cloned.1.call-start = ((), (), s32[]{:S(2)}) async-start(), calls=%async_computation | async-start | bytes 2703360 | tf_op jit(solution)/shard_map/all_gather | solution.py:74
  66.4 1925.6 %copy-start.6 = (s32[4,512]{1,0:T(4,128)S(1)}, s32[4,512]{1,0:T(4,128)}, u32[]{:S(2)}) copy-start(s32[4,512]{1,0:T(4,128)} %param.18) | copy-start | bytes 24580
  66.4 1926.5 %copy-start.8 = (bf16[128]{0:T(256)(128)(2,1)S(1)}, bf16[128]{0:T(256)(128)(2,1)}, u32[]{:S(2)}) copy-start(bf16[128]{0:T(256)(128)(2,1)} %param.23) | copy-start | bytes 772
  66.4 117.5 %all-reduce.2.cloned.1.call-start = ((), (), s32[]{:S(2)}) async-start(), calls=%async_computation.4 | async-start | bytes 1310720 | tf_op jit(solution)/shard_map/while/body/eval_jaxpr/psum | solution.py:17
  186.2 118.1 %all-reduce.2.cloned.1.call-start = ((), (), s32[]{:S(2)}) async-start(), calls=%async_computation.4 | async-start | bytes 1310720 | tf_op jit(solution)/shard_map/while/body/eval_jaxpr/psum | solution.py:17
  306.5 118.1 %all-reduce.2.cloned.1.call-start = ((), (), s32[]{:S(2)}) async-start(), calls=%async_computation.4 | async-start | bytes 1310720 | tf_op jit(solution)/shard_map/while/body/eval_jaxpr/psum | solution.py:17
  426.8 118.1 %all-reduce.2.cloned.1.call-start = ((), (), s32[]{:S(2)}) async-start(), calls=%async_computation.4 | async-start | bytes 1310720 | tf_op jit(solution)/shard_map/while/body/eval_jaxpr/psum | solution.py:17
  547.1 118.1 %all-reduce.2.cloned.1.call-start = ((), (), s32[]{:S(2)}) async-start(), calls=%async_computation.4 | async-start | bytes 1310720 | tf_op jit(solution)/shard_map/while/body/eval_jaxpr/psum | solution.py:17
  667.4 118.1 %all-reduce.2.cloned.1.call-start = ((), (), s32[]{:S(2)}) async-start(), calls=%async_computation.4 | async-start | bytes 1310720 | tf_op jit(solution)/shard_map/while/body/eval_jaxpr/psum | solution.py:17
  787.8 118.1 %all-reduce.2.cloned.1.call-start = ((), (), s32[]{:S(2)}) async-start(), calls=%async_computation.4 | async-start | bytes 1310720 | tf_op jit(solution)/shard_map/while/body/eval_jaxpr/psum | solution.py:17
  908.1 118.1 %all-reduce.2.cloned.1.call-start = ((), (), s32[]{:S(2)}) async-start(), calls=%async_computation.4 | async-start | bytes 1310720 | tf_op jit(solution)/shard_map/while/body/eval_jaxpr/psum | solution.py:17
  1028.4 118.1 %all-reduce.2.cloned.1.call-start = ((), (), s32[]{:S(2)}) async-start(), calls=%async_computation.4 | async-start | bytes 1310720 | tf_op jit(solution)/shard_map/while/body/eval_jaxpr/psum | solution.py:17
  1148.7 118.1 %all-reduce.2.cloned.1.call-start = ((), (), s32[]{:S(2)}) async-start(), calls=%async_computation.4 | async-start | bytes 1310720 | tf_op jit(solution)/shard_map/while/body/eval_jaxpr/psum | solution.py:17
  1269.1 118.1 %all-reduce.2.cloned.1.call-start = ((), (), s32[]{:S(2)}) async-start(), calls=%async_computation.4 | async-start | bytes 1310720 | tf_op jit(solution)/shard_map/while/body/eval_jaxpr/psum | solution.py:17
  1389.4 118.1 %all-reduce.2.cloned.1.call-start = ((), (), s32[]{:S(2)}) async-start(), calls=%async_computation.4 | async-start | bytes 1310720 | tf_op jit(solution)/shard_map/while/body/eval_jaxpr/psum | solution.py:17
  1509.7 118.1 %all-reduce.2.cloned.1.call-start = ((), (), s32[]{:S(2)}) async-start(), calls=%async_computation.4 | async-start | bytes 1310720 | tf_op jit(solution)/shard_map/while/body/eval_jaxpr/psum | solution.py:17
  1630.0 118.1 %all-reduce.2.cloned.1.call-start = ((), (), s32[]{:S(2)}) async-start(), calls=%async_computation.4 | async-start | bytes 1310720 | tf_op jit(solution)/shard_map/while/body/eval_jaxpr/psum | solution.py:17
  1750.3 118.1 %all-reduce.2.cloned.1.call-start = ((), (), s32[]{:S(2)}) async-start(), calls=%async_computation.4 | async-start | bytes 1310720 | tf_op jit(solution)/shard_map/while/body/eval_jaxpr/psum | solution.py:17
  1870.7 118.1 %all-reduce.2.cloned.1.call-start = ((), (), s32[]{:S(2)}) async-start(), calls=%async_computation.4 | async-start | bytes 1310720 | tf_op jit(solution)/shard_map/while/body/eval_jaxpr/psum | solution.py:17
  1991.0 47.7 %all-gather.7.cloned.1.call-start = ((), (), s32[]{:S(2)}) async-start(), calls=%async_computation.1 | async-start | bytes 3686400 | tf_op jit(solution)/shard_map/all_gather | solution.py:85
  1992.0 101.7 %all-gather.9.cloned.1.call-start = ((), (), s32[]{:S(2)}) async-start(), calls=%async_computation.2 | async-start | bytes 2703360 | tf_op jit(solution)/shard_map/all_gather | solution.py:149
  2038.7 6.9 copy-start.7
  2038.7 7.0 copy-start.1
  2044.6 100.3 %all-gather.11.cloned.1.call-start = ((), (), s32[]{:S(2)}) async-start(), calls=%async_computation.3 | async-start | bytes 2703360 | tf_op jit(solution)/shard_map/all_gather | solution.py:150
  2055.1 0.9 copy-start.4
  2055.2 1.0 copy-start.5
  2055.6 89.3 %copy-start.3 = (f32[4,1,5,80,128]{4,3,2,0,1:T(8,128)S(1)}, f32[4,1,5,80,128]{4,3,2,0,1:T(8,128)}, u32[]{:S(2)}) copy-start(f32[4,1,5,80,128]{4,3,2,0,1:T(8,128)} %custom-call.3) | copy-start | bytes 2457604
  2149.1 3.9 copy-start.2
  2158.6 3.9 copy-start.2
  2168.0 3.9 copy-start.2
  2177.5 3.9 copy-start.2
Sparse Core Ops, SparseCore 0:
  9.9 53.7 all-gather.4
  71.8 112.0 all-reduce.1
  191.6 112.6 all-reduce.1
  311.9 112.6 all-reduce.1
  432.2 112.6 all-reduce.1
  552.5 112.6 all-reduce.1
  672.8 112.6 all-reduce.1
  793.2 112.6 all-reduce.1
  913.5 112.6 all-reduce.1
  1033.8 112.6 all-reduce.1
  1154.1 112.6 all-reduce.1
  1274.5 112.6 all-reduce.1
  1394.8 112.6 all-reduce.1
  1515.1 112.6 all-reduce.1
  1635.4 112.6 all-reduce.1
  1755.7 112.6 all-reduce.1
  1876.1 112.6 all-reduce.1
  1993.3 45.3 all-gather.6
  2044.7 48.8 all-gather.8
  2096.1 48.7 all-gather.10
where the time goes:
time: 2190 us
  waiting for transfers between devices  1990 us (91%)
  local copies, waits for them, and re-layouts  53.7 us (2%)
  other arithmetic  53 us (2%)
  loops' own time  43 us (2%)
  matrix products  41.3 us (2%)
    psum x16, waiting for transfers between devices, broadcast(): return lax.psum(block, axis)  1800 us
    all_gather x1, waiting for transfers between devices, per_device(): piece = lax.all_gather(text_tokens, 'ctx', axis=1, tiled=True)  52.3 us
    all_gather x1, waiting for transfers between devices, per_device(): value_piece = lax.all_gather(value_rows, 'ctx', axis=1, tiled=True)  51.3 us
    all_gather x1, waiting for transfers between devices, per_device(): piece = lax.all_gather(token_rows, 'mp', axis=3, tiled=True)  45.6 us
  transfers between devices with their start and end apart: 20, of which 20 were waited for; matrix products, arithmetic and copies ran while one was open for 1% of the time, Pallas kernels for 0%

commit v1 on v0

v1 whole, which is shorter than its diff:
```python
import functools
import math

import jax
import jax.numpy as jnp
from jax import lax
from jax.experimental import pallas as pl
from jax.experimental.pallas import tpu as pltpu
from jax.sharding import PartitionSpec as P

HEAD = 128
NEG_FILL = -1e30
ROPE_BASE = 1000000.0
GROUPS = 4
MEMBERS = 8
PLANES = 8


def shifted(n, by):
    return [(i, (i + by) % n) for i in range(n)]


def ctx_pairs(dy=0, dx=0, dc=0):
    pairs = []
    for i in range(32):
        y, x, c = i // 8, (i // 2) % 4, i % 2
        pairs.append((i, ((y + dy) % 4) * 8 + ((x + dx) % 4) * 2 + (c + dc) % 2))
    return pairs


def rope_tables(positions):
    half = HEAD // 2
    frequency = ROPE_BASE ** (-(jnp.arange(half, dtype=jnp.float32) * 2.0) / HEAD)
    angles = positions.astype(jnp.float32)[:, None] * frequency
    angles = jnp.concatenate([angles, angles], axis=-1)
    return jnp.cos(angles), jnp.sin(angles)


def rotate(rows, cosine, sine):
    half = HEAD // 2
    turned = jnp.concatenate([-rows[..., half:], rows[..., :half]], axis=-1)
    return rows * cosine[:, None, :] + turned * sine[:, None, :]


def attend_kernel(heads, step, first, last, member_ref, q_ref, k_ref, v_ref, o_ref):
    member = member_ref[0]
    keys_step = MEMBERS * step
    scale = 1.0 / math.sqrt(HEAD)
    shape = (heads, step, MEMBERS, step)
    q_idx = lax.broadcasted_iota(jnp.int32, (step, keys_step), 0)
    lane = lax.broadcasted_iota(jnp.int32, (step, keys_step), 1)
    k_idx = lane % step
    k_mem = lane // step
    allowed = (k_idx < q_idx) | ((k_idx == q_idx) & (k_mem <= member))
    allowed = jnp.concatenate([allowed] * heads, axis=0)
    for part in range(first, last):
        rows = pl.ds((part - first) * step, step)
        q = jnp.concatenate(
            [q_ref[rows, h * HEAD : (h + 1) * HEAD] for h in range(heads)], axis=0
        )
        scores = []
        for kp in range(part + 1):
            keys = k_ref[:, kp * step : (kp + 1) * step, :].reshape(keys_step, HEAD)
            s = lax.dot_general(
                q, keys, (((1,), (1,)), ((), ())), preferred_element_type=jnp.float32
            ) * scale
            if kp == part:
                s = jnp.where(allowed, s, NEG_FILL)
            scores.append(s)
        top = functools.reduce(
            jnp.maximum, [jnp.max(s, axis=-1, keepdims=True) for s in scores]
        )
        total = jnp.zeros((heads * step, 1), jnp.float32)
        acc = jnp.zeros((heads * step, HEAD), jnp.float32)
        for kp, s in enumerate(scores):
            w = jnp.exp(s - top)
            total = total + jnp.sum(w, axis=-1, keepdims=True)
            vals = v_ref[:, kp * step : (kp + 1) * step, :].reshape(keys_step, HEAD)
            acc = acc + jnp.dot(
                w.astype(jnp.bfloat16), vals, preferred_element_type=jnp.float32
            )
        out = (acc / total).astype(jnp.bfloat16)
        for h in range(heads):
            o_ref[rows, h * HEAD : (h + 1) * HEAD] = out[h * step : (h + 1) * step, :]


def attend(member, q, k, v, heads, step, first, last):
    vmem = pl.BlockSpec(memory_space=pltpu.VMEM)
    return pl.pallas_call(
        functools.partial(attend_kernel, heads, step, first, last),
        out_shape=jax.ShapeDtypeStruct(q.shape, jnp.bfloat16),
        in_specs=[pl.BlockSpec(memory_space=pltpu.SMEM), vmem, vmem, vmem],
        out_specs=vmem,
        compiler_params=pltpu.CompilerParams(vmem_limit_bytes=48 * 1024 * 1024),
        cost_estimate=pl.CostEstimate(
            flops=1300000000, bytes_accessed=4000000, transcendentals=2500000
        ),
    )(member, q, k, v)


def per_device(
    clip_store,
    text_tokens,
    candidates,
    clip_slot,
    text_positions,
    block_order,
    w_query,
    b_query,
    key_value_weight,
    value_offset_bias,
):
    me = lax.axis_index("ctx")
    plane = lax.axis_index("mp")
    group = me // MEMBERS
    member = me % MEMBERS
    clips_here, clip_len, feat = clip_store.shape
    seqs, cands = candidates.shape
    text_len = text_positions.shape[1]
    devices = GROUPS * MEMBERS
    per = clip_len // devices
    text_here = text_tokens.shape[1]

    slots = jnp.take(clip_slot, candidates.reshape(-1))
    holders = slots // clips_here
    which = jnp.sum(jnp.where(holders == me, slots % clips_here, 0))
    held = lax.dynamic_index_in_dim(clip_store, which, 0, keepdims=False)
    held = held.reshape(GROUPS, per, MEMBERS, feat).transpose(0, 2, 1, 3)
    held = held.reshape(devices, per, feat)
    texts = text_tokens.reshape(seqs, text_here // MEMBERS, MEMBERS, feat)
    texts = texts.transpose(0, 2, 1, 3).reshape(devices, text_here // MEMBERS, feat)
    sent = jnp.concatenate([held, texts], axis=1)
    sent = lax.all_to_all(sent, "ctx", 0, 0, tiled=True)
    got = jnp.take(sent[:, :per], holders, axis=0).reshape(seqs, cands, per, feat)
    text_rows = sent[:, per:].reshape(-1, feat)

    pieces = []
    for dy in range(GROUPS):
        seq_to = (group + dy) % GROUPS
        out = lax.dynamic_index_in_dim(got, seq_to, 0, keepdims=False)
        pieces.append(out if dy == 0 else lax.ppermute(out, "ctx", ctx_pairs(dy=dy)))
    stacked = jnp.stack(pieces, axis=0)
    order = (group - jnp.arange(GROUPS)) % GROUPS
    stacked = jnp.take(stacked, order, axis=0)
    rows = jnp.transpose(stacked, (1, 0, 2, 3)).reshape(-1, feat)
    rows = jnp.concatenate([rows, text_rows], axis=0)
    count = rows.shape[0]

    width = w_query.shape[1]
    kv_flat = key_value_weight.reshape(key_value_weight.shape[0], -1)

    def product(part, owner):
        wq = lax.dynamic_slice_in_dim(w_query, owner * feat, feat, 0)
        wk = lax.dynamic_slice_in_dim(kv_flat, owner * feat, feat, 0)
        return (
            jnp.dot(part, wq, preferred_element_type=jnp.float32),
            jnp.dot(part, wk, preferred_element_type=jnp.float32),
        )

    def add(a, b):
        return (a[0] + b[0], a[1] + b[1])

    sums = product(rows, plane)
    fwd, bwd = rows, rows
    for hop in range(1, PLANES // 2):
        fwd = lax.ppermute(fwd, "mp", shifted(PLANES, 1))
        bwd = lax.ppermute(bwd, "mp", shifted(PLANES, -1))
        sums = add(sums, product(fwd, (plane - hop) % PLANES))
        sums = add(sums, product(bwd, (plane + hop) % PLANES))
    cut = count // 2
    far = jnp.concatenate(
        [
            lax.ppermute(fwd[:cut], "mp", shifted(PLANES, 1)),
            lax.ppermute(bwd[cut:], "mp", shifted(PLANES, -1)),
        ],
        axis=0,
    )
    q_sum, kv_sum = add(sums, product(far, (plane + PLANES // 2) % PLANES))

    visual = cands * clip_len
    pos = MEMBERS * jnp.arange(count, dtype=jnp.int32) + member
    my_text = lax.dynamic_index_in_dim(text_positions, group, 0, keepdims=False)
    text_at = lax.dynamic_index_in_dim(
        my_text.reshape(text_len // MEMBERS, MEMBERS), member, 1, keepdims=False
    )
    rope_pos = jnp.concatenate([pos[: visual // MEMBERS], text_at], axis=0)
    cosine, sine = rope_tables(rope_pos)
    heads = width // HEAD
    q_raw = (q_sum + b_query.astype(jnp.float32)).reshape(count, heads, HEAD)
    queries = rotate(q_raw, cosine, sine).astype(jnp.bfloat16).reshape(count, width)
    k_raw = kv_sum[:, :HEAD].reshape(count, 1, HEAD)
    keys = rotate(k_raw, cosine, sine).astype(jnp.bfloat16).reshape(count, HEAD)
    values = (kv_sum[:, HEAD:] + value_offset_bias.astype(jnp.float32)).astype(jnp.bfloat16)

    own = jnp.stack([keys, values], axis=0)
    by_x = [own] + [lax.ppermute(own, "ctx", ctx_pairs(dx=dx)) for dx in range(1, 4)]
    by_x = jnp.stack(by_x, axis=0)
    my_x, my_core = member // 2, member % 2
    by_x = jnp.take(by_x, (my_x - jnp.arange(4)) % 4, axis=0)
    other = lax.ppermute(by_x, "ctx", ctx_pairs(dc=1))
    both = jnp.where(my_core == 0, jnp.stack([by_x, other], 1), jnp.stack([other, by_x], 1))
    both = both.reshape(MEMBERS, 2, count, HEAD)
    all_keys, all_values = both[:, 0], both[:, 1]

    out = attend(
        member.astype(jnp.int32).reshape(1), queries, all_keys, all_values,
        heads, clip_len // MEMBERS, 0, count * MEMBERS // clip_len,
    )

    blocks = block_order.shape[0]
    block_len = (visual + text_len) // blocks
    sub = block_len // MEMBERS
    send = jnp.take(out.reshape(blocks, sub, width), block_order, axis=0)
    send = send.reshape(devices, 2 * sub, width)
    recv = lax.all_to_all(send, "ctx", 0, 0, tiled=True)
    recv = recv.reshape(GROUPS, MEMBERS, 2, sub, width)
    return recv.transpose(0, 2, 3, 1, 4).reshape(seqs, 2, block_len, width)


def solution(mesh):
    placed = (
        P("ctx", None, "mp"),
        P(None, "ctx", "mp"),
        P(),
        P(),
        P(),
        P(),
        P(None, "mp"),
        P("mp"),
        P(None, None, "mp"),
        P("mp"),
    )
    return jax.shard_map(
        per_device,
        mesh=mesh,
        in_specs=placed,
        out_specs=P(None, "ctx", None, "mp"),
        check_vma=False,
    )
```

time: 2190 us -> 147 us (0.07)
  waiting for transfers between devices: 1990 us -> 26.3 us
  loops' own time: 43 us -> 0 us
  starting transfers between devices: 0.99 us -> 39.5 us
  other arithmetic: 53 us -> 14.8 us
  local copies, waits for them, and re-layouts: 53.7 us -> 19.6 us
  matrix products: 41.3 us -> 19.1 us
    psum x16 -> x0, waiting for transfers between devices: 1800 us -> none  [broadcast(): return lax.psum(block, axis)]
    all_gather x4 -> x0, waiting for transfers between devices: 186 us -> none  [the longest x1 52.3 us: per_device(): piece = lax.all_gather(text_tokens, 'ctx', axis=1, tiled=True)]
    another operation x2 -> x0, loops' own time: 43 us -> none  [the longest x1 42.7 us: per_device(): token_rows = lax.fori_loop(0, seq_count * cand_count, fetch_one, token_rows)]
    select_n x68 -> x11, other arithmetic: 38.2 us -> 3.05 us  [the longest x1 1.52 us: per_device(): jnp.where(my_core == 0, jnp.stack([by_x, other], 1), jnp.stack([other, by...]
    gather x23 -> x7, local copies, waits for them, and re-layouts: 36.3 us -> 4.11 us  [the longest x2 1.4 us: per_device(): slots = jnp.take(clip_slot, candidates.reshape(-1))]
    ppermute x0 -> x15, starting transfers between devices: none -> 30.9 us  [the longest x3 10.8 us: per_device(): bwd = lax.ppermute(bwd, 'mp', shifted(PLANES, -1))]
    dot_general x10 -> x16, matrix products: 41.3 us -> 19.1 us  [the longest x8 15.8 us: product(): jnp.dot(part, wq, preferred_element_type=jnp.float32)]
  transfers between devices with their start and end apart: 20 -> 16, of which waited for: 20 -> 6; matrix products, arithmetic and copies ran while one was open for 1% -> 25% of each run, Pallas kernels for 0% -> 0%
where the time goes in v1:
time: 147 us; the launch traced here: 146 us
  starting transfers between devices  39.5 us (27%)
  waiting for transfers between devices  26.3 us (18%)
  local copies, waits for them, and re-layouts  19.6 us (13%)
  matrix products  19.1 us (13%)
  blocking collectives  19.1 us (13%)
  other arithmetic  14.8 us (10%)
  Pallas kernels  4.74 us (3%)
  between operations  2.7 us (2%)
    all_to_all x1, blocking collectives, per_device(): recv = lax.all_to_all(send, 'ctx', 0, 0, tiled=True)  19.1 us
    dot_general x8, matrix products, product(): jnp.dot(part, wq, preferred_element_type=jnp.float32)  15.8 us
    all_to_all x1, waiting for transfers between devices, per_device(): sent = lax.all_to_all(sent, 'ctx', 0, 0, tiled=True)  14.9 us
    ppermute x3, starting transfers between devices, per_device(): bwd = lax.ppermute(bwd, 'mp', shifted(PLANES, -1))  10.8 us
    all_to_all x1, starting transfers between devices, per_device(): sent = lax.all_to_all(sent, 'ctx', 0, 0, tiled=True)  8.59 us
    ppermute x3, starting transfers between devices, per_device(): lax.ppermute(own, 'ctx', ctx_pairs(dx=dx))  7 us
    mul x3, local copies, waits for them, and re-layouts, rotate(): return rows * cosine[:, None, :] + turned * sine[:, None, :]  5.91 us
    ppermute x1, starting transfers between devices, per_device(): other = lax.ppermute(by_x, 'ctx', ctx_pairs(dc=1))  5.06 us
  transfers between devices with their start and end apart: 16, of which 6 were waited for; matrix products, arithmetic and copies ran while one was open for 25% of the time, Pallas kernels for 0%

profile of v1, /device:TPU:1, one launch (start us, length us, event | category | flops | bytes accessed | tf_op | source)
XLA Modules:
  0.0 145.7 jit_solution(18002772259237704826)
XLA Ops:
  3.0 1.3 fusion.56
  7.6 8.6 %all-to-all-start = ((bf16[32,18,640]{2,1,0:T(8,128)(2,1)}), bf16[32,18,640]{2,1,0:T(8,128)(2,1)S(1)}, u32[]{:S(2)}, u32[]{:S(2)}) async-start(bf16[32,18,640]{2,1,0:T(8,128)(2,1)} %pad_maximum_fusion), calls=%async_computation | async-start | bytes 1966080 | tf_op jit(solution)/shard_map/all_to_all | solution.py:133
  17.8 14.9 %all-to-all-done = bf16[32,18,640]{2,1,0:T(8,128)(2,1)S(1)} async-done(((bf16[32,18,640]{2,1,0:T(8,128)(2,1)}), bf16[32,18,640]{2,1,0:T(8,128)(2,1)S(1)}, u32[]{:S(2)}, u32[]{:S(2)}) %all-to-all-start) | async-done | bytes 737312 | tf_op jit(solution)/shard_map/all_to_all | solution.py:133
  33.6 1.7 %collective-permute-start.1 = (bf16[4,16,640]{2,1,0:T(8,128)(2,1)S(1)}, bf16[4,16,640]{2,1,0:T(8,128)(2,1)S(1)}, u32[]{:S(2)}, u32[]{:S(2)}) collective-permute-start(bf16[4,16,640]{2,1,0:T(8,128)(2,1)S(1)} %get-tuple-element.15), channel_id=1, source_target_pairs={{0,128},{8,136},{16,144},{24,152},{32,160},{40,168},{48,176},{56,1... | collective-permute-start | bytes 245768 | tf_op jit(solution)/shard_map/ppermute | solution.py:141
  35.3 1.4 collective-permute-start.2
  36.8 3.6 %collective-permute-done = bf16[4,16,640]{2,1,0:T(8,128)(2,1)S(1)} collective-permute-done((bf16[4,16,640]{2,1,0:T(8,128)(2,1)S(1)}, bf16[4,16,640]{2,1,0:T(8,128)(2,1)S(1)}, u32[]{:S(2)}, u32[]{:S(2)}) %collective-permute-start) | collective-permute-done | bytes 81952 | tf_op jit(solution)/shard_map/ppermute | solution.py:141
  41.3 1.7 %collective-permute-start.3 = (bf16[320,640]{1,0:T(8,128)(2,1)S(1)}, bf16[320,640]{1,0:T(8,128)(2,1)S(1)}, u32[]{:S(2)}, u32[]{:S(2)}) collective-permute-start(bf16[320,640]{1,0:T(8,128)(2,1)S(1)} %pad_maximum_fusion.2), channel_id=1, source_target_pairs={{0,1},{1,2},{2,3},{3,4},{4,5},{5,6},{6,7},{7,0},{8,9},{9,10},{10,1... | collective-permute-start | bytes 1228808 | tf_op jit(solution)/shard_map/ppermute | solution.py:166
  43.0 4.0 %collective-permute-start.4 = (bf16[320,640]{1,0:T(8,128)(2,1)S(1)}, bf16[320,640]{1,0:T(8,128)(2,1)S(1)}, u32[]{:S(2)}, u32[]{:S(2)}) collective-permute-start(bf16[320,640]{1,0:T(8,128)(2,1)S(1)} %pad_maximum_fusion.2), channel_id=1, source_target_pairs={{0,7},{1,0},{2,1},{3,2},{4,3},{5,4},{6,5},{7,6},{8,15},{9,8},{10,9... | collective-permute-start | bytes 1228808 | tf_op jit(solution)/shard_map/ppermute | solution.py:167
  47.1 3.6 %copy.47 = bf16[640,8,2,128]{3,1,2,0:T(8,128)(2,1)} copy(bf16[640,8,2,128]{3,2,1,0:T(2,128)(2,1)} %bitcast.104) | data formatting | bytes 5242880
  52.3 1.7 %fusion.17 = f32[320,640]{1,0:T(8,128)S(1)} fusion(bf16[5120,640]{1,0:T(8,128)(2,1)} %param.16, s32[]{:T(128)S(6)} %select_n.345, bf16[64,640]{1,0:T(8,128)(2,1)S(1)} %reshape.397, bf16[256,640]{1,0:T(8,128)(2,1)S(1)} %bitcast.103), kind=kOutput, calls=%fused_computation.35 | convolution fusion | flops 262963200 | bytes 2048004 | tf_op jit(solution)/shard_map/dot_general | solution.py:156
  54.3 3.4 %collective-permute-start.6 = (bf16[320,640]{1,0:T(8,128)(2,1)S(1)}, bf16[320,640]{1,0:T(8,128)(2,1)S(1)}, u32[]{:S(2)}, u32[]{:S(2)}) collective-permute-start(bf16[320,640]{1,0:T(8,128)(2,1)S(1)} %collective-permute-done.4), channel_id=1, source_target_pairs={{0,7},{1,0},{2,1},{3,2},{4,3},{5,4},{6,5},{7,6},{8,15},{9,8},{10,9... | collective-permute-start | bytes 1228808 | tf_op jit(solution)/shard_map/ppermute | solution.py:167
  57.7 1.7 %convolution_add_fusion.3 = f32[320,640]{1,0:T(8,128)S(1)} fusion(f32[320,640]{1,0:T(8,128)S(1)} %fusion.17, bf16[320,640]{1,0:T(8,128)(2,1)S(1)} %collective-permute-done.3, bf16[5120,640]{1,0:T(8,128)(2,1)} %param.16, s32[]{:T(128)S(6)} %select_n.347), kind=kOutput, calls=%fused_computation.14 | convolution fusion | flops 262348800 | bytes 2867204 | tf_op jit(solution)/shard_map/dot_general | solution.py:156
  59.4 1.7 %convolution_add_fusion.2 = f32[320,640]{1,0:T(8,128)S(1)} fusion(f32[320,640]{1,0:T(8,128)S(1)} %convolution_add_fusion.3, bf16[320,640]{1,0:T(8,128)(2,1)S(1)} %collective-permute-done.4, bf16[5120,640]{1,0:T(8,128)(2,1)} %param.16, s32[]{:T(128)S(6)} %select_n.349), kind=kOutput, calls=%fused_computation.13 | convolution fusion | flops 262348800 | bytes 2867204 | tf_op jit(solution)/shard_map/dot_general | solution.py:156
  61.7 2.3 %collective-permute-done.6 = bf16[320,640]{1,0:T(8,128)(2,1)S(1)} collective-permute-done((bf16[320,640]{1,0:T(8,128)(2,1)S(1)}, bf16[320,640]{1,0:T(8,128)(2,1)S(1)}, u32[]{:S(2)}, u32[]{:S(2)}) %collective-permute-start.6) | collective-permute-done | bytes 409632 | tf_op jit(solution)/shard_map/ppermute | solution.py:167
  64.0 3.4 %collective-permute-start.8 = (bf16[320,640]{1,0:T(8,128)(2,1)S(1)}, bf16[320,640]{1,0:T(8,128)(2,1)S(1)}, u32[]{:S(2)}, u32[]{:S(2)}) collective-permute-start(bf16[320,640]{1,0:T(8,128)(2,1)S(1)} %collective-permute-done.6), channel_id=1, source_target_pairs={{0,7},{1,0},{2,1},{3,2},{4,3},{5,4},{6,5},{7,6},{8,15},{9,8},{10,9... | collective-permute-start | bytes 1228808 | tf_op jit(solution)/shard_map/ppermute | solution.py:167
  68.3 1.7 %fusion.12 = f32[320,640]{1,0:T(8,128)S(1)} fusion(bf16[320,640]{1,0:T(8,128)(2,1)S(1)} %collective-permute-done.6, bf16[5120,640]{1,0:T(8,128)(2,1)} %param.16, s32[]{:T(128)S(6)} %select_n.353), kind=kOutput, calls=%fused_computation.30 | convolution fusion | flops 262144000 | bytes 2048004 | tf_op jit(solution)/shard_map/dot_general | solution.py:156
  70.0 2.6 %fusion.3 = f32[320,640]{1,0:T(8,128)} fusion(f32[320,640]{1,0:T(8,128)S(1)} %fusion.12, f32[320,640]{1,0:T(8,128)S(1)} %convolution_add_fusion.2, bf16[320,640]{1,0:T(8,128)(2,1)S(1)} %collective-permute-done.5, bf16[5120,640]{1,0:T(8,128)(2,1)} %param.16, s32[]{:T(128)S(6)} %select_n.351), kind=kOutput, calls=%fused_computation.12 | convolution fusion | flops 262553600 | bytes 3686404 | tf_op jit(solution)/shard_map/dot_general | solution.py:156
  72.6 3.9 %collective-permute-done.7 = bf16[320,640]{1,0:T(8,128)(2,1)S(1)} collective-permute-done((bf16[320,640]{1,0:T(8,128)(2,1)S(1)}, bf16[320,640]{1,0:T(8,128)(2,1)S(1)}, u32[]{:S(2)}, u32[]{:S(2)}) %collective-permute-start.7) | collective-permute-done | bytes 409632 | tf_op jit(solution)/shard_map/ppermute | solution.py:166
  76.6 2.7 %collective-permute-start.10 = (bf16[160,640]{1,0:T(8,128)(2,1)S(1)}, bf16[160,640]{1,0:T(8,128)(2,1)S(1)}, u32[]{:S(2)}, u32[]{:S(2)}) collective-permute-start(bf16[160,640]{1,0:T(8,128)(2,1)S(1)} %slice.65), channel_id=1, source_target_pairs={{0,7},{1,0},{2,1},{3,2},{4,3},{5,4},{6,5},{7,6},{8,15},{9,8},{10,9... | collective-permute-start | bytes 614408 | tf_op jit(solution)/shard_map/ppermute | solution.py:174
  79.3 1.7 %fusion.9 = f32[320,640]{1,0:T(8,128)S(1)} fusion(bf16[320,640]{1,0:T(8,128)(2,1)S(1)} %collective-permute-done.8, bf16[5120,640]{1,0:T(8,128)(2,1)} %param.16, s32[]{:T(128)S(6)} %select_n.357), kind=kOutput, calls=%fused_computation.27 | convolution fusion | flops 262144000 | bytes 2048004 | tf_op jit(solution)/shard_map/dot_general | solution.py:156
  83.4 1.4 fusion.37
  86.2 6.3 %collective-permute-start.12 = (bf16[2,320,128]{2,1,0:T(8,128)(2,1)}, bf16[2,320,128]{2,1,0:T(8,128)(2,1)}, u32[]{:S(2)}, u32[]{:S(2)}) collective-permute-start(bf16[2,320,128]{2,1,0:T(8,128)(2,1)} %get-tuple-element.18), channel_id=1, source_target_pairs={{0,32},{8,40},{16,48},{24,56},{32,0},{40,8},{48,16},{56,24},{64,96... | collective-permute-start | bytes 491528 | tf_op jit(solution)/shard_map/ppermute | solution.py:196
  92.5 2.6 %fusion.7 = f32[320,640]{1,0:T(8,128)} fusion(bf16[320,640]{1,0:T(8,128)(2,1)S(1)} %constant_dynamic-update-slice_fusion, bf16[5120,640]{1,0:T(8,128)(2,1)} %param.16, s32[]{:T(128)S(6)} %select_n.359), kind=kOutput, calls=%fused_computation.25 | convolution fusion | flops 262144000 | bytes 2048004 | tf_op jit(solution)/shard_map/dot_general | solution.py:156
  96.0 2.2 %fusion.2 = f32[320,640]{1,0:T(8,128)S(1)} fusion(f32[320,640]{1,0:T(8,128)} %fusion.7, f32[320,640]{1,0:T(8,128)S(1)} %fusion.9, f32[320,640]{1,0:T(8,128)} %fusion.3, bf16[320,640]{1,0:T(8,128)(2,1)S(1)} %collective-permute-done.7, bf16[5120,640]{1,0:T(8,128)(2,1)} %param.16, s32[]{:T(128)S(6)} %select_n.355, f32[640]{0:T(1024)S(1)} %convert_element_type.24), kind=kOutput, calls=%fused_computation.10 | convolution fusion | flops 262963200 | bytes 4508164 | tf_op jit(solution)/shard_map/dot_general | solution.py:156
  103.1 5.1 %collective-permute-start.14 = (bf16[4,2,320,128]{3,2,1,0:T(8,128)(2,1)}, bf16[4,2,320,128]{3,2,1,0:T(8,128)(2,1)}, u32[]{:S(2)}, u32[]{:S(2)}) collective-permute-start(bf16[4,2,320,128]{3,2,1,0:T(8,128)(2,1)} %broadcast_select_fusion), channel_id=1, source_target_pairs={{0,8},{8,0},{16,24},{24,16},{32,40},{40,32},{48,56},{56,48},{64,72... | collective-permute-start | bytes 1966088 | tf_op jit(solution)/shard_map/ppermute | solution.py:200
  108.2 2.3 %maximum_multiply_fusion = f32[320,5,128]{0,2,1:T(8,128)} fusion(f32[320,5,64]{0,2,1:T(8,128)} %get-tuple-element.10, f32[320,5,64]{0,2,1:T(8,128)} %get-tuple-element.9, f32[320,128]{0,1:T(8,128)} %copy.36), kind=kLoop, calls=%fused_computation.23 | loop fusion | flops 409600 | bytes 1802240 | tf_op jit(solution)/shard_map/mul | solution.py:42
  111.6 2.4 %copy.34 = f32[320,640]{1,0:T(8,128)} copy(f32[320,640]{0,1:T(8,128)} %bitcast.100) | data formatting | bytes 1638400 | tf_op jit(solution)/shard_map/mul | solution.py:42
  114.1 2.4 %copy.37 = f32[320,640]{1,0:T(8,128)} copy(f32[320,640]{0,1:T(8,128)} %bitcast.98) | data formatting | bytes 1638400 | tf_op jit(solution)/shard_map/mul | solution.py:42
  116.5 1.5 %add_convert_fusion.q_ref = bf16[320,640]{1,0:T(8,128)(2,1)S(1)} fusion(f32[320,640]{1,0:T(8,128)} %copy.37, f32[320,640]{1,0:T(8,128)S(1)} %fusion.2, f32[320,640]{1,0:T(8,128)} %copy.34), kind=kLoop, calls=%fused_computation.24 | loop fusion | flops 614400 | bytes 2867200 | tf_op jit(solution)/shard_map/convert_element_type | solution.py:190
  118.2 1.5 %maximum_select_fusion = bf16[4,2,2,320,128]{4,3,2,0,1:T(8,128)(2,1)S(1)} fusion(bf16[4,1,2,320,128]{4,3,2,0,1:T(8,128)(2,1)} %bitcast.34, bf16[4,1,2,320,128]{4,3,2,0,1:T(8,128)(2,1)S(1)} %bitcast_select_fusion, pred[]{:T(512)S(6)} %eq.31), kind=kLoop, calls=%fused_computation.6 | loop fusion | flops 1966080 | bytes 2621441 | tf_op jit(solution)/shard_map/jit(_where)/select_n | solution.py:201
  119.9 4.7 %shard_map.100 = bf16[320,640]{1,0:T(8,128)(2,1)S(1)} custom-call(s32[1]{0:T(128)} %bitcast.member_ref, bf16[320,640]{1,0:T(8,128)(2,1)S(1)} %add_convert_fusion.q_ref, bf16[8,320,128]{2,1,0:T(8,128)(2,1)S(1)} %get-tuple-element.8.k_ref, bf16[8,320,128]{2,1,0:T(8,128)(2,1)S(1)} %get-tuple-element.7.v_ref), custom_call_target="tpu_custom_call" | custom-call | flops 1300000000 | bytes 4000000 | tf_op jit(solution)/shard_map/pallas_call | solution.py:89
  125.8 19.1 %all_to_all.10 = bf16[32,10,640]{2,1,0:T(8,128)(2,1)S(1)} all-to-all(bf16[32,10,640]{2,1,0:T(8,128)(2,1)S(1)} %broadcast_select_fusion.1), channel_id=1, replica_groups=mesh['ctx'=32,'mp'=8] {'ctx'}, dimensions={0} | all-to-all | bytes 819200 | tf_op jit(solution)/shard_map/all_to_all | solution.py:215
  (113 shorter events, 23.8 us)
Async XLA Ops:
  0.0 6.3 %copy-start = (bf16[2,512,640]{2,1,0:T(8,128)(2,1)S(1)}, bf16[2,512,640]{2,1,0:T(8,128)(2,1)}, u32[]{:S(2)}) copy-start(bf16[2,512,640]{2,1,0:T(8,128)(2,1)} %param.10) | copy-start | bytes 3932164
  0.0 6.4 %copy-start.4 = (bf16[4,16,640]{2,1,0:T(8,128)(2,1)S(1)}, bf16[4,16,640]{2,1,0:T(8,128)(2,1)}, u32[]{:S(2)}) copy-start(bf16[4,16,640]{2,1,0:T(8,128)(2,1)} %param.11) | copy-start | bytes 245764
  6.4 11.3 %copy-start.6 = (s32[64]{0:T(128)S(1)}, s32[64]{0:T(128)}, u32[]{:S(2)}) copy-start(s32[64]{0:T(128)} %param.15) | copy-start | bytes 772
  7.6 25.1 %all-to-all-start = ((bf16[32,18,640]{2,1,0:T(8,128)(2,1)}), bf16[32,18,640]{2,1,0:T(8,128)(2,1)S(1)}, u32[]{:S(2)}, u32[]{:S(2)}) async-start(bf16[32,18,640]{2,1,0:T(8,128)(2,1)} %pad_maximum_fusion), calls=%async_computation | async-start | bytes 1966080 | tf_op jit(solution)/shard_map/all_to_all | solution.py:133
  33.5 6.9 %collective-permute-start = (bf16[4,16,640]{2,1,0:T(8,128)(2,1)S(1)}, bf16[4,16,640]{2,1,0:T(8,128)(2,1)S(1)}, u32[]{:S(2)}, u32[]{:S(2)}) collective-permute-start(bf16[4,16,640]{2,1,0:T(8,128)(2,1)S(1)} %get-tuple-element.16), channel_id=1, source_target_pairs={{0,64},{8,72},{16,80},{24,88},{32,96},{40,104},{48,112},{56,120},{... | collective-permute-start | bytes 245768 | tf_op jit(solution)/shard_map/ppermute | solution.py:141
  33.6 6.8 %collective-permute-start.1 = (bf16[4,16,640]{2,1,0:T(8,128)(2,1)S(1)}, bf16[4,16,640]{2,1,0:T(8,128)(2,1)S(1)}, u32[]{:S(2)}, u32[]{:S(2)}) collective-permute-start(bf16[4,16,640]{2,1,0:T(8,128)(2,1)S(1)} %get-tuple-element.15), channel_id=1, source_target_pairs={{0,128},{8,136},{16,144},{24,152},{32,160},{40,168},{48,176},{56,1... | collective-permute-start | bytes 245768 | tf_op jit(solution)/shard_map/ppermute | solution.py:141
  35.3 5.2 %collective-permute-start.2 = (bf16[4,16,640]{2,1,0:T(8,128)(2,1)S(1)}, bf16[4,16,640]{2,1,0:T(8,128)(2,1)S(1)}, u32[]{:S(2)}, u32[]{:S(2)}) collective-permute-start(bf16[4,16,640]{2,1,0:T(8,128)(2,1)S(1)} %get-tuple-element.14), channel_id=1, source_target_pairs={{0,192},{8,200},{16,208},{24,216},{32,224},{40,232},{48,240},{56,2... | collective-permute-start | bytes 245768 | tf_op jit(solution)/shard_map/ppermute | solution.py:141
  41.3 16.4 %collective-permute-start.3 = (bf16[320,640]{1,0:T(8,128)(2,1)S(1)}, bf16[320,640]{1,0:T(8,128)(2,1)S(1)}, u32[]{:S(2)}, u32[]{:S(2)}) collective-permute-start(bf16[320,640]{1,0:T(8,128)(2,1)S(1)} %pad_maximum_fusion.2), channel_id=1, source_target_pairs={{0,1},{1,2},{2,3},{3,4},{4,5},{5,6},{6,7},{7,0},{8,9},{9,10},{10,1... | collective-permute-start | bytes 1228808 | tf_op jit(solution)/shard_map/ppermute | solution.py:166
  43.0 11.3 %collective-permute-start.4 = (bf16[320,640]{1,0:T(8,128)(2,1)S(1)}, bf16[320,640]{1,0:T(8,128)(2,1)S(1)}, u32[]{:S(2)}, u32[]{:S(2)}) collective-permute-start(bf16[320,640]{1,0:T(8,128)(2,1)S(1)} %pad_maximum_fusion.2), channel_id=1, source_target_pairs={{0,7},{1,0},{2,1},{3,2},{4,3},{5,4},{6,5},{7,6},{8,15},{9,8},{10,9... | collective-permute-start | bytes 1228808 | tf_op jit(solution)/shard_map/ppermute | solution.py:167
  47.0 3.6 %copy-start.7 = (bf16[128]{0:T(256)(128)(2,1)S(1)}, bf16[128]{0:T(256)(128)(2,1)}, u32[]{:S(2)}) copy-start(bf16[128]{0:T(256)(128)(2,1)} %param.19) | copy-start | bytes 772
  47.0 3.6 %copy-start.5 = (bf16[640]{0:T(1024)(128)(2,1)S(1)}, bf16[640]{0:T(1024)(128)(2,1)}, u32[]{:S(2)}) copy-start(bf16[640]{0:T(1024)(128)(2,1)} %param.17) | copy-start | bytes 3844
  54.0 7.0 %copy-start.1 = (bf16[640,8,2,128]{3,1,2,0:T(8,128)(2,1)S(1)}, bf16[640,8,2,128]{3,1,2,0:T(8,128)(2,1)}, u32[]{:S(2)}) copy-start(bf16[640,8,2,128]{3,1,2,0:T(8,128)(2,1)} %copy.47) | copy-start | bytes 7864324
  54.3 9.7 %collective-permute-start.6 = (bf16[320,640]{1,0:T(8,128)(2,1)S(1)}, bf16[320,640]{1,0:T(8,128)(2,1)S(1)}, u32[]{:S(2)}, u32[]{:S(2)}) collective-permute-start(bf16[320,640]{1,0:T(8,128)(2,1)S(1)} %collective-permute-done.4), channel_id=1, source_target_pairs={{0,7},{1,0},{2,1},{3,2},{4,3},{5,4},{6,5},{7,6},{8,15},{9,8},{10,9... | collective-permute-start | bytes 1228808 | tf_op jit(solution)/shard_map/ppermute | solution.py:167
  57.7 10.0 %collective-permute-start.5 = (bf16[320,640]{1,0:T(8,128)(2,1)S(1)}, bf16[320,640]{1,0:T(8,128)(2,1)S(1)}, u32[]{:S(2)}, u32[]{:S(2)}) collective-permute-start(bf16[320,640]{1,0:T(8,128)(2,1)S(1)} %collective-permute-done.3), channel_id=1, source_target_pairs={{0,1},{1,2},{2,3},{3,4},{4,5},{5,6},{6,7},{7,0},{8,9},{9,10},{10,1... | collective-permute-start | bytes 1228808 | tf_op jit(solution)/shard_map/ppermute | solution.py:166
  64.0 12.6 %collective-permute-start.8 = (bf16[320,640]{1,0:T(8,128)(2,1)S(1)}, bf16[320,640]{1,0:T(8,128)(2,1)S(1)}, u32[]{:S(2)}, u32[]{:S(2)}) collective-permute-start(bf16[320,640]{1,0:T(8,128)(2,1)S(1)} %collective-permute-done.6), channel_id=1, source_target_pairs={{0,7},{1,0},{2,1},{3,2},{4,3},{5,4},{6,5},{7,6},{8,15},{9,8},{10,9... | collective-permute-start | bytes 1228808 | tf_op jit(solution)/shard_map/ppermute | solution.py:167
  67.7 8.8 %collective-permute-start.7 = (bf16[320,640]{1,0:T(8,128)(2,1)S(1)}, bf16[320,640]{1,0:T(8,128)(2,1)S(1)}, u32[]{:S(2)}, u32[]{:S(2)}) collective-permute-start(bf16[320,640]{1,0:T(8,128)(2,1)S(1)} %collective-permute-done.5), channel_id=1, source_target_pairs={{0,1},{1,2},{2,3},{3,4},{4,5},{5,6},{6,7},{7,0},{8,9},{9,10},{10,1... | collective-permute-start | bytes 1228808 | tf_op jit(solution)/shard_map/ppermute | solution.py:166
  76.5 6.1 %collective-permute-start.9 = (bf16[160,640]{1,0:T(8,128)(2,1)S(1)}, bf16[160,640]{1,0:T(8,128)(2,1)S(1)}, u32[]{:S(2)}, u32[]{:S(2)}) collective-permute-start(bf16[160,640]{1,0:T(8,128)(2,1)S(1)} %slice.64), channel_id=1, source_target_pairs={{0,1},{1,2},{2,3},{3,4},{4,5},{5,6},{6,7},{7,0},{8,9},{9,10},{10,1... | collective-permute-start | bytes 614408 | tf_op jit(solution)/shard_map/ppermute | solution.py:173
  76.6 6.0 %collective-permute-start.10 = (bf16[160,640]{1,0:T(8,128)(2,1)S(1)}, bf16[160,640]{1,0:T(8,128)(2,1)S(1)}, u32[]{:S(2)}, u32[]{:S(2)}) collective-permute-start(bf16[160,640]{1,0:T(8,128)(2,1)S(1)} %slice.65), channel_id=1, source_target_pairs={{0,7},{1,0},{2,1},{3,2},{4,3},{5,4},{6,5},{7,6},{8,15},{9,8},{10,9... | collective-permute-start | bytes 614408 | tf_op jit(solution)/shard_map/ppermute | solution.py:174
  85.5 14.1 %collective-permute-start.11 = (bf16[2,320,128]{2,1,0:T(8,128)(2,1)}, bf16[2,320,128]{2,1,0:T(8,128)(2,1)S(1)}, u32[]{:S(2)}, u32[]{:S(2)}) collective-permute-start(bf16[2,320,128]{2,1,0:T(8,128)(2,1)} %get-tuple-element.18), channel_id=1, source_target_pairs={{0,16},{8,24},{16,32},{24,40},{32,48},{40,56},{48,0},{56,8},{64,80... | collective-permute-start | bytes 491528 | tf_op jit(solution)/shard_map/ppermute | solution.py:196
  86.2 13.4 %collective-permute-start.12 = (bf16[2,320,128]{2,1,0:T(8,128)(2,1)}, bf16[2,320,128]{2,1,0:T(8,128)(2,1)}, u32[]{:S(2)}, u32[]{:S(2)}) collective-permute-start(bf16[2,320,128]{2,1,0:T(8,128)(2,1)} %get-tuple-element.18), channel_id=1, source_target_pairs={{0,32},{8,40},{16,48},{24,56},{32,0},{40,8},{48,16},{56,24},{64,96... | collective-permute-start | bytes 491528 | tf_op jit(solution)/shard_map/ppermute | solution.py:196
  92.5 7.1 %collective-permute-start.13 = (bf16[2,320,128]{2,1,0:T(8,128)(2,1)}, bf16[2,320,128]{2,1,0:T(8,128)(2,1)}, u32[]{:S(2)}, u32[]{:S(2)}) collective-permute-start(bf16[2,320,128]{2,1,0:T(8,128)(2,1)} %get-tuple-element.18), channel_id=1, source_target_pairs={{0,48},{8,56},{16,0},{24,8},{32,16},{40,24},{48,32},{56,40},{64,11... | collective-permute-start | bytes 491528 | tf_op jit(solution)/shard_map/ppermute | solution.py:196
  99.6 0.7 copy-start.3
  102.2 8.3 %copy-start.2 = (f32[320,128]{1,0:T(8,128)S(1)}, f32[320,128]{1,0:T(8,128)}, u32[]{:S(2)}) copy-start(f32[320,128]{1,0:T(8,128)} %get-tuple-element.20) | copy-start | bytes 491524
  103.1 15.0 %collective-permute-start.14 = (bf16[4,2,320,128]{3,2,1,0:T(8,128)(2,1)}, bf16[4,2,320,128]{3,2,1,0:T(8,128)(2,1)}, u32[]{:S(2)}, u32[]{:S(2)}) collective-permute-start(bf16[4,2,320,128]{3,2,1,0:T(8,128)(2,1)} %broadcast_select_fusion), channel_id=1, source_target_pairs={{0,8},{8,0},{16,24},{24,16},{32,40},{40,32},{48,56},{56,48},{64,72... | collective-permute-start | bytes 1966088 | tf_op jit(solution)/shard_map/ppermute | solution.py:200

commit v2 on v1

v2 whole, which is shorter than its diff:
```python
import functools
import math

import jax
import jax.numpy as jnp
from jax import lax
from jax.experimental import pallas as pl
from jax.experimental.pallas import tpu as pltpu
from jax.sharding import PartitionSpec as P

HEAD = 128
NEG_FILL = -1e30
ROPE_BASE = 1000000.0
GROUPS = 4
MEMBERS = 8
DEVICES = GROUPS * MEMBERS
PLANES = 8
MULTIPLY_AT = (1, 2, 3)
STEP = 64
PART = 16
TEXT = 2
SMALL_VMEM = 16 * 1024 * 1024
MID_VMEM = 24 * 1024 * 1024
VMEM_SPEC = pl.BlockSpec(memory_space=pltpu.VMEM)
SMEM_SPEC = pl.BlockSpec(memory_space=pltpu.SMEM)
HBM_SPEC = pl.BlockSpec(memory_space=pltpu.HBM)


def in_hbm(*arrays):
    return [pltpu.with_memory_space_constraint(array, pltpu.HBM) for array in arrays]


def shifted(n, by):
    return [(i, (i + by) % n) for i in range(n)]


def ctx_pairs(move):
    pairs = []
    for i in range(DEVICES):
        y, x, c = move(i // MEMBERS, (i // 2) % 4, i % 2)
        pairs.append((i, (y % 4) * MEMBERS + (x % 4) * 2 + c))
    return pairs


def across(first):
    return ctx_pairs(lambda y, x, c: (y, x ^ (1 if (c == 0) == first else 3), c))


def far_pairs():
    return [
        (i * PLANES + z, i * PLANES + (z + (1 if i % 2 == 0 else -1)) % PLANES)
        for i in range(DEVICES)
        for z in range(PLANES)
    ]


def rope_tables(positions):
    half = HEAD // 2
    frequency = ROPE_BASE ** (-(jnp.arange(half, dtype=jnp.float32) * 2.0) / HEAD)
    angles = positions.astype(jnp.float32)[:, None] * frequency
    cosine, sine = jnp.cos(angles), jnp.sin(angles)
    return jnp.concatenate([cosine, cosine], -1), jnp.concatenate([-sine, sine], -1)


def rows_of(refs):
    return refs[0][...] if len(refs) == 1 else jnp.concatenate([r[...] for r in refs], axis=0)


def products_kernel(groups, halves, fresh, owners_ref, wq_hbm, wk_hbm, *refs):
    wq_ref, wk_ref, sems = refs[-3:]
    q_out, k_out = refs[-5:-3]
    feat = wq_ref.shape[1]
    copies = []
    for i in range(groups):
        at = pl.ds(pl.multiple_of(owners_ref[i] * feat, feat), feat)
        for n, (src, dst) in enumerate(((wq_hbm, wq_ref), (wk_hbm, wk_ref))):
            copy = pltpu.make_async_copy(src.at[at, :], dst.at[i], sems.at[n, i])
            copy.start()
            copies.append(copy)
    q = None if fresh else refs[-7][...]
    k = None if fresh else refs[-6][...]
    for i in range(groups):
        copies[2 * i].wait()
        copies[2 * i + 1].wait()
        rows = rows_of(refs[i * halves : (i + 1) * halves])
        more_q = jnp.dot(rows, wq_ref[i], preferred_element_type=jnp.float32)
        more_k = jnp.dot(rows, wk_ref[i], preferred_element_type=jnp.float32)
        q = more_q if q is None else q + more_q
        k = more_k if k is None else k + more_k
    q_out[...] = q
    k_out[...] = k


def add_products(sums, parts, owners, w_query, kv_flat):
    halves, groups = len(parts[0]), len(parts)
    feat = parts[0][0].shape[1]
    count = sum(part.shape[0] for part in parts[0])
    q_cols, k_cols = w_query.shape[1], kv_flat.shape[1]
    args = sum(parts, []) + list(sums or ())
    return pl.pallas_call(
        functools.partial(products_kernel, groups, halves, sums is None),
        in_specs=[SMEM_SPEC, HBM_SPEC, HBM_SPEC] + [VMEM_SPEC] * len(args),
        out_specs=[VMEM_SPEC] * 2,
        out_shape=[
            jax.ShapeDtypeStruct((count, q_cols), jnp.float32),
            jax.ShapeDtypeStruct((count, k_cols), jnp.float32),
        ],
        scratch_shapes=[
            pltpu.VMEM((groups, feat, q_cols), jnp.bfloat16),
            pltpu.VMEM((groups, feat, k_cols), jnp.bfloat16),
            pltpu.SemaphoreType.DMA((2, groups)),
        ],
        compiler_params=pltpu.CompilerParams(vmem_limit_bytes=SMALL_VMEM),
        cost_estimate=pl.CostEstimate(
            flops=4 * groups * count * feat * (q_cols + k_cols),
            bytes_accessed=groups * feat * (q_cols + k_cols) * 2,
            transcendentals=0,
        ),
    )(jnp.stack(owners).astype(jnp.int32), *in_hbm(w_query, kv_flat), *args)


def finish_kernel(halves, owner_ref, wq_hbm, wk_hbm, *refs):
    q_sum, k_sum, cos_ref, sin_ref, qb_ref, vb_ref, q_out, kv_out, wq_ref, wk_ref, sems = refs[halves:]
    feat = wq_ref.shape[0]
    at = pl.ds(pl.multiple_of(owner_ref[0] * feat, feat), feat)
    copy_k = pltpu.make_async_copy(wk_hbm.at[at, :], wk_ref, sems.at[0])
    copy_q = pltpu.make_async_copy(wq_hbm.at[at, :], wq_ref, sems.at[1])
    copy_k.start()
    copy_q.start()
    rows = rows_of(refs[:halves])
    copy_k.wait()
    k = k_sum[...] + jnp.dot(rows, wk_ref[...], preferred_element_type=jnp.float32)
    copy_q.wait()
    q = q_sum[...] + jnp.dot(rows, wq_ref[...], preferred_element_type=jnp.float32)
    q = q + qb_ref[...].astype(jnp.float32)
    cosine, sine = cos_ref[...], sin_ref[...]

    def rotated(x):
        return (x * cosine + pltpu.roll(x, HEAD // 2, 1) * sine).astype(jnp.bfloat16)

    kv_out[:, :HEAD] = rotated(k[:, :HEAD])
    kv_out[:, HEAD:] = (k[:, HEAD:] + vb_ref[...].astype(jnp.float32)).astype(jnp.bfloat16)
    for h in range(q.shape[1] // HEAD):
        at = slice(h * HEAD, (h + 1) * HEAD)
        q_out[:, at] = rotated(q[:, at])


def finish(sums, far, owner, w_query, kv_flat, cosine, sine, q_bias, v_bias):
    count, feat = sums[0].shape[0], far[0].shape[1]
    q_cols, k_cols = w_query.shape[1], kv_flat.shape[1]
    args = [*far, *sums, cosine, sine, q_bias.reshape(1, -1), v_bias.reshape(1, -1)]
    return pl.pallas_call(
        functools.partial(finish_kernel, len(far)),
        in_specs=[SMEM_SPEC, HBM_SPEC, HBM_SPEC] + [VMEM_SPEC] * len(args),
        out_specs=[VMEM_SPEC] * 2,
        out_shape=[jax.ShapeDtypeStruct(s.shape, jnp.bfloat16) for s in sums],
        scratch_shapes=[
            pltpu.VMEM((feat, q_cols), jnp.bfloat16),
            pltpu.VMEM((feat, k_cols), jnp.bfloat16),
            pltpu.SemaphoreType.DMA((2,)),
        ],
        compiler_params=pltpu.CompilerParams(vmem_limit_bytes=SMALL_VMEM),
        cost_estimate=pl.CostEstimate(
            flops=2 * count * feat * (q_cols + k_cols), bytes_accessed=2000000, transcendentals=0
        ),
    )(owner.reshape(1).astype(jnp.int32), *in_hbm(w_query, kv_flat), *args)


def one_hot(hit):
    return jnp.where(hit, 1.0, 0.0).astype(jnp.bfloat16)


def iotas(shape):
    return lax.broadcasted_iota(jnp.int32, shape, 0), lax.broadcasted_iota(jnp.int32, shape, 1)


def pack_kernel(clips_here, cand_ref, slot_ref, me_ref, clip_hbm, text_ref, o_ref, held_ref, sem):
    me = me_ref[0]
    which = jnp.int32(0)
    for s in range(cand_ref.shape[0]):
        for k in range(cand_ref.shape[1]):
            slot = slot_ref[cand_ref[s, k]]
            which = jnp.where(slot // clips_here == me, slot % clips_here, which)
    copy = pltpu.make_async_copy(clip_hbm.at[which], held_ref, sem)
    copy.start()
    feat = held_ref.shape[1]
    folds = feat // HEAD
    rows = PART * MEMBERS
    to, at = iotas((rows, PART))
    m, r = to // PART, to % PART
    for y in range(GROUPS):
        text = text_ref[y]
        beside = jnp.zeros((rows, HEAD), jnp.float32)
        for fold in range(folds):
            hit = (r % folds == fold) & (r < TEXT * folds) & (at == m + MEMBERS * (r // folds))
            beside = beside + jnp.dot(
                one_hot(hit), text[:, fold * HEAD : (fold + 1) * HEAD],
                preferred_element_type=jnp.float32,
            )
        o_ref[pl.ds(y * MEMBERS, MEMBERS), :, feat:] = beside.astype(jnp.bfloat16).reshape(
            MEMBERS, PART, HEAD
        )
    to, at = iotas((rows, rows))
    pick = one_hot(at == MEMBERS * (to % PART) + to // PART)
    copy.wait()
    for y in range(GROUPS):
        out = jnp.dot(pick, held_ref[rows * y : rows * (y + 1)], preferred_element_type=jnp.float32)
        o_ref[pl.ds(y * MEMBERS, MEMBERS), :, :feat] = out.astype(jnp.bfloat16).reshape(
            MEMBERS, PART, feat
        )


def pack(candidates, clip_slot, me, clip_store, text_tokens):
    clips_here, clip_len, feat = clip_store.shape
    return pl.pallas_call(
        functools.partial(pack_kernel, clips_here),
        out_shape=jax.ShapeDtypeStruct((DEVICES, PART, feat + HEAD), jnp.bfloat16),
        in_specs=[SMEM_SPEC] * 3 + [HBM_SPEC, VMEM_SPEC],
        out_specs=VMEM_SPEC,
        scratch_shapes=[pltpu.VMEM((clip_len, feat), jnp.bfloat16), pltpu.SemaphoreType.DMA],
        compiler_params=pltpu.CompilerParams(vmem_limit_bytes=SMALL_VMEM),
    )(*in_hbm(candidates, clip_slot), me.reshape(1).astype(jnp.int32), *in_hbm(clip_store, text_tokens))


def unpack_kernel(clips_here, cand_ref, slot_ref, group_ref, sent_ref, own_ref, *out_refs):
    group = group_ref[0]
    feat = own_ref.shape[1]
    folds = feat // HEAD
    beside = sent_ref[:, :, feat:].reshape(DEVICES * PART, HEAD)
    to, at = iotas((TEXT * DEVICES, DEVICES * PART))
    for fold in range(folds):
        hit = at == (to // TEXT) * PART + (to % TEXT) * folds + fold
        own_ref[:STEP, fold * HEAD : (fold + 1) * HEAD] = jnp.dot(
            one_hot(hit), beside, preferred_element_type=jnp.float32
        ).astype(jnp.bfloat16)
    cands = cand_ref.shape[1]
    for dy in range(GROUPS):
        seq = (group + dy) % GROUPS
        for k in range(cands):
            source = slot_ref[cand_ref[seq, k]] // clips_here
            rows = sent_ref[source, :, :feat]
            if dy == 0:
                own_ref[STEP + PART * k : STEP + PART * (k + 1)] = rows
            else:
                out_refs[dy - 1][PART * k : PART * (k + 1)] = rows


def unpack(candidates, clip_slot, group, sent, clips_here):
    feat = sent.shape[2] - HEAD
    shapes = [(2 * STEP, feat)] + [(STEP, feat)] * (GROUPS - 1)
    return pl.pallas_call(
        functools.partial(unpack_kernel, clips_here),
        out_shape=[jax.ShapeDtypeStruct(s, jnp.bfloat16) for s in shapes],
        in_specs=[SMEM_SPEC] * 3 + [VMEM_SPEC],
        out_specs=[VMEM_SPEC] * GROUPS,
        compiler_params=pltpu.CompilerParams(vmem_limit_bytes=SMALL_VMEM),
    )(*in_hbm(candidates, clip_slot), group.reshape(1).astype(jnp.int32), sent)


def attend_kernel(heads, clips, info_ref, q_ref, *refs):
    o_ref, key_refs = refs[-1], refs[:-1]
    group, member = info_ref[0], info_ref[1]
    my_x, my_core = member // 2, member % 2
    scale = math.log2(math.e) / math.sqrt(HEAD)

    def spans(part):
        if part == clips:
            return [(0, STEP)]
        return [(STEP + dy * STEP + PART * part, PART) for dy in range(GROUPS)]

    def idx_of(row, part):
        if part == clips:
            return row
        return ((group + GROUPS - row // PART) % GROUPS) * PART + row % PART

    keys_step = MEMBERS * STEP
    lane = lax.broadcasted_iota(jnp.int32, (STEP, keys_step), 1)
    row = lax.broadcasted_iota(jnp.int32, (STEP, keys_step), 0)
    slot = lane // STEP
    core = (my_core + slot // 4) % 2
    by_near, by_far = jnp.where(core == 0, 1, 3), jnp.where(core == 0, 3, 1)
    x = my_x ^ jnp.where(slot % 2 == 1, by_near, 0) ^ jnp.where((slot // 2) % 2 == 1, by_far, 0)
    k_mem = 2 * x + core

    def gather(part, at):
        return jnp.concatenate(
            [
                ref[piece, pl.ds(first, n), at : at + HEAD]
                for ref in key_refs
                for piece in range(2)
                for first, n in spans(part)
            ],
            axis=0,
        )

    for part in range(clips + 1):
        k_pos = MEMBERS * idx_of(lane % STEP, part) + k_mem
        q_pos = MEMBERS * idx_of(row, part) + member
        allowed = jnp.concatenate([k_pos <= q_pos] * heads, axis=0)
        q = jnp.concatenate(
            [
                q_ref[pl.ds(first, n), h * HEAD : (h + 1) * HEAD]
                for h in range(heads)
                for first, n in spans(part)
            ],
            axis=0,
        )
        scores = []
        for kp in range(part + 1):
            s = lax.dot_general(
                q, gather(kp, 0), (((1,), (1,)), ((), ())), preferred_element_type=jnp.float32
            ) * scale
            if kp == part:
                s = jnp.where(allowed, s, NEG_FILL)
            scores.append(s)
        top = functools.reduce(
            jnp.maximum, [jnp.max(s, axis=-1, keepdims=True) for s in scores]
        )
        total = jnp.zeros((heads * STEP, 1), jnp.float32)
        acc = jnp.zeros((heads * STEP, HEAD), jnp.float32)
        for kp, s in enumerate(scores):
            w = jnp.exp2(s - top)
            total = total + jnp.sum(w, axis=-1, keepdims=True)
            acc = acc + jnp.dot(
                w.astype(jnp.bfloat16), gather(kp, HEAD), preferred_element_type=jnp.float32
            )
        out = (acc / total).astype(jnp.bfloat16)
        for h in range(heads):
            at = slice(h * HEAD, (h + 1) * HEAD)
            if part == clips:
                o_ref[pl.ds(part * STEP, STEP), at] = out[h * STEP : (h + 1) * STEP]
                continue
            for dy in range(GROUPS):
                y = (group + GROUPS - dy) % GROUPS
                to = pl.ds(pl.multiple_of(part * STEP + y * PART, PART), PART)
                first = h * STEP + dy * PART
                o_ref[to, at] = out[first : first + PART]


def attend(info, q, pieces, heads, clips):
    return pl.pallas_call(
        functools.partial(attend_kernel, heads, clips),
        out_shape=jax.ShapeDtypeStruct(q.shape, jnp.bfloat16),
        in_specs=[SMEM_SPEC] + [VMEM_SPEC] * (1 + len(pieces)),
        out_specs=VMEM_SPEC,
        compiler_params=pltpu.CompilerParams(vmem_limit_bytes=MID_VMEM),
        cost_estimate=pl.CostEstimate(
            flops=1300000000, bytes_accessed=4000000, transcendentals=2500000
        ),
    )(info, q, *pieces)


def per_device(
    clip_store,
    text_tokens,
    candidates,
    clip_slot,
    text_positions,
    block_order,
    w_query,
    b_query,
    key_value_weight,
    value_offset_bias,
):
    me = lax.axis_index("ctx")
    plane = lax.axis_index("mp")
    group, member = me // MEMBERS, me % MEMBERS
    core = member % 2
    clips_here, clip_len, feat = clip_store.shape
    seqs, cands = candidates.shape
    text_len = text_positions.shape[1]
    width = w_query.shape[1]
    heads = width // HEAD

    sent = pack(candidates, clip_slot, me, clip_store, text_tokens)
    sent = lax.all_to_all(sent, "ctx", 0, 0, tiled=True)

    kv_flat = key_value_weight.reshape(key_value_weight.shape[0], -1)
    text_at = lax.dynamic_index_in_dim(
        lax.dynamic_index_in_dim(text_positions, group, 0, keepdims=False).reshape(-1, MEMBERS),
        member, 1, keepdims=False,
    )
    clip_idx = STEP * jnp.arange(cands)[:, None] + jnp.arange(PART)[None, :]

    def clip_pos(dy):
        y = (group - dy) % GROUPS
        return (MEMBERS * (clip_idx + PART * y) + member).astype(jnp.int32).reshape(-1)

    cosine, sine = rope_tables(jnp.concatenate([text_at] + [clip_pos(dy) for dy in range(GROUPS)]))
    sent, kv_flat, cosine, sine = lax.optimization_barrier((sent, kv_flat, cosine, sine))

    first, *others = unpack(candidates, clip_slot, group, sent, clips_here)
    arrived = [
        lax.ppermute(out, "ctx", ctx_pairs(lambda y, x, c, dy=dy: (y + dy, x, c)))
        for dy, out in enumerate(others, 1)
    ]
    own = [first, jnp.concatenate(arrived, 0)]

    fwd, bwd = list(own), list(own)
    sums, parts, owners = None, [own], [plane]
    for hop in range(1, PLANES // 2):
        for h in range(len(own)):
            fwd[h] = lax.ppermute(fwd[h], "mp", shifted(PLANES, 1))
            bwd[h] = lax.ppermute(bwd[h], "mp", shifted(PLANES, -1))
        if hop in MULTIPLY_AT:
            sums = add_products(sums, parts, owners, w_query, kv_flat)
            fwd[-1], bwd[-1], sums = lax.optimization_barrier((fwd[-1], bwd[-1], sums))
            parts, owners = [], []
        parts += [list(fwd), list(bwd)]
        owners += [(plane - hop) % PLANES, (plane + hop) % PLANES]
    far = [
        lax.ppermute(jnp.where(core == 0, fwd[h], bwd[h]), ("ctx", "mp"), far_pairs())
        for h in range(len(own))
    ]
    sums = add_products(sums, parts, owners, w_query, kv_flat)
    far[-1], sums = lax.optimization_barrier((far[-1], sums))
    q, kv = finish(
        sums, far, (plane + PLANES // 2) % PLANES, w_query, kv_flat,
        cosine, sine, b_query, value_offset_bias,
    )

    near = jnp.stack([kv, lax.ppermute(kv, "ctx", across(True))])
    off = lax.ppermute(near, "ctx", across(False))
    swap = ctx_pairs(lambda y, x, c: (y, x, 1 - c))
    pieces = [near, off, lax.ppermute(near, "ctx", swap), lax.ppermute(off, "ctx", swap)]

    info = jnp.stack([group, member]).astype(jnp.int32)
    out = attend(info, q, pieces, heads, cands)

    blocks = block_order.shape[0]
    block_len = (cands * clip_len + text_len) // blocks
    sub = block_len // MEMBERS
    send = jnp.take(out.reshape(blocks, sub, width), block_order, axis=0)
    send = send.reshape(DEVICES, 2 * sub, width)
    recv = lax.all_to_all(send, "ctx", 0, 0, tiled=True)
    recv = recv.reshape(GROUPS, MEMBERS, 2, sub, width)
    return recv.transpose(0, 2, 3, 1, 4).reshape(seqs, 2, block_len, width)


def solution(mesh):
    placed = (
        P("ctx", None, "mp"),
        P(None, "ctx", "mp"),
        P(),
        P(),
        P(),
        P(),
        P(None, "mp"),
        P("mp"),
        P(None, None, "mp"),
        P("mp"),
    )
    return jax.shard_map(
        per_device,
        mesh=mesh,
        in_specs=placed,
        out_specs=P(None, "ctx", None, "mp"),
        check_vma=False,
    )
```

time: 147 us -> 123 us (0.84)
  matrix products: 19.1 us -> 0 us
  Pallas kernels: 4.74 us -> 23.8 us
  local copies, waits for them, and re-layouts: 19.6 us -> 4.8 us
  starting transfers between devices: 39.5 us -> 53.8 us
  other arithmetic: 14.8 us -> 1.48 us
  waiting for transfers between devices: 26.3 us -> 18 us
  between operations: 2.7 us -> 0.41 us
    dot_general x16 -> x0, matrix products: 19.1 us -> none  [the longest x8 15.8 us: product(): jnp.dot(part, wq, preferred_element_type=jnp.float32)]
    pallas_call x1 -> x8, Pallas kernels: 4.74 us -> 23.8 us  [the longest x4 12 us: add_products(): pl.pallas_call(functools.partial(products_kernel, groups, halves, sums is...]
    ppermute x15 -> x21, starting transfers between devices: 30.9 us -> 45.2 us  [the longest x6 17.4 us: per_device(): bwd[h] = lax.ppermute(bwd[h], 'mp', shifted(PLANES, -1))]
    mul x3 -> x0, local copies, waits for them, and re-layouts: 5.91 us -> none  [rotate(): return rows * cosine[:, None, :] + turned * sine[:, None, :]]
    all_to_all x1, waiting for transfers between devices: 14.9 us -> 10.6 us  [per_device(): sent = lax.all_to_all(sent, 'ctx', 0, 0, tiled=True)]
    ppermute x15 -> x21, waiting for transfers between devices: 11.3 us -> 7.43 us  [the longest x3 3 us: per_device(): lax.ppermute(out, 'ctx', ctx_pairs(lambda y, x, c, dy=dy: (y + dy, x, c)))]
    gather x5 -> x0, local copies, waits for them, and re-layouts: 3.29 us -> none  [the longest x2 1.4 us: per_device(): slots = jnp.take(clip_slot, candidates.reshape(-1))]
    another operation x4 -> x5, other arithmetic: 3.4 us -> 0.33 us  [the longest x3 0.22 us: add_products(): jnp.stack(owners).astype(jnp.int32)]
  transfers between devices with their start and end apart: 16 -> 22, of which waited for: 6 -> 6; matrix products, arithmetic and copies ran while one was open for 25% -> 3% of each run, Pallas kernels for 0% -> 10%
where the time goes in v2:
time: 123 us; the launch traced here: 122 us
  starting transfers between devices  53.8 us (44%)
  Pallas kernels  23.8 us (19%)
  blocking collectives  20 us (16%)
  waiting for transfers between devices  18 us (15%)
  local copies, waits for them, and re-layouts  4.8 us (4%)
  other arithmetic  1.48 us (1%)
    all_to_all x1, blocking collectives, per_device(): recv = lax.all_to_all(send, 'ctx', 0, 0, tiled=True)  20 us
    ppermute x6, starting transfers between devices, per_device(): bwd[h] = lax.ppermute(bwd[h], 'mp', shifted(PLANES, -1))  17.4 us
    pallas_call x4, Pallas kernels, add_products(): pl.pallas_call(functools.partial(products_kernel, groups, halves, sums is...  12 us
    ppermute x1, starting transfers between devices, per_device(): lax.ppermute(near, 'ctx', swap)  10.8 us
    all_to_all x1, waiting for transfers between devices, per_device(): sent = lax.all_to_all(sent, 'ctx', 0, 0, tiled=True)  10.6 us
    all_to_all x1, starting transfers between devices, per_device(): sent = lax.all_to_all(sent, 'ctx', 0, 0, tiled=True)  8.6 us
    pallas_call x1, Pallas kernels, attend(): pl.pallas_call(functools.partial(attend_kernel, heads, clips), out_shape=...  5.29 us
    ppermute x1, starting transfers between devices, per_device(): lax.ppermute(off, 'ctx', swap)  4.59 us
  transfers between devices with their start and end apart: 22, of which 6 were waited for; matrix products, arithmetic and copies ran while one was open for 3% of the time, Pallas kernels for 10%

profile of v2, /device:TPU:1, one launch (start us, length us, event | category | flops | bytes accessed | tf_op | source)
XLA Modules:
  0.0 122.4 jit_solution(3087816056642400274)
XLA Ops:
  0.0 3.5 %shard_map.100 = bf16[32,16,768]{2,1,0:T(8,128)(2,1)} custom-call(s32[4,4]{1,0:T(4,128)} %cand_ref.3, s32[64]{0:T(128)} %slot_ref.3, s32[1]{0:T(128)} %bitcast.3.me_ref, bf16[2,512,640]{2,1,0:T(8,128)(2,1)} %clip_hbm.1, bf16[4,16,640]{2,1,0:T(8,128)(2,1)} %text_ref.1), custom_call_target="tpu_custom_call" | custom-call | tf_op jit(solution)/shard_map/pallas_call | solution.py:215
  3.5 8.6 %all-to-all-start = ((bf16[32,16,768]{2,1,0:T(8,128)(2,1)}), bf16[32,16,768]{2,1,0:T(8,128)(2,1)S(1)}, u32[]{:S(2)}, u32[]{:S(2)}) async-start(bf16[32,16,768]{2,1,0:T(8,128)(2,1)} %shard_map.100), calls=%async_computation | async-start | bytes 1572864 | tf_op jit(solution)/shard_map/all_to_all | solution.py:376
  13.0 1.9 %copy.21 = bf16[640,8,2,128]{3,1,2,0:T(8,128)(2,1)} copy(bf16[640,8,2,128]{3,2,1,0:T(2,128)(2,1)S(1)} %bitcast.33) | data formatting | bytes 5242880
  15.7 10.6 %all-to-all-done.sent_ref = bf16[32,16,768]{2,1,0:T(8,128)(2,1)S(1)} async-done(((bf16[32,16,768]{2,1,0:T(8,128)(2,1)}), bf16[32,16,768]{2,1,0:T(8,128)(2,1)S(1)}, u32[]{:S(2)}, u32[]{:S(2)}) %all-to-all-start) | async-done | bytes 786464 | tf_op jit(solution)/shard_map/all_to_all | solution.py:376
  26.3 1.0 shard_map.101
  27.4 1.7 %collective-permute-start = (bf16[128,640]{1,0:T(8,128)(2,1)S(1)}, bf16[128,640]{1,0:T(8,128)(2,1)S(1)}, u32[]{:S(2)}, u32[]{:S(2)}) collective-permute-start(bf16[128,640]{1,0:T(8,128)(2,1)S(1)} %get-tuple-element.40.refs_0_), channel_id=1, source_target_pairs={{0,1},{1,2},{2,3},{3,4},{4,5},{5,6},{6,7},{7,0},{8,9},{9,10},{10,1... | collective-permute-start | bytes 491528 | tf_op jit(solution)/shard_map/ppermute | solution.py:403
  29.1 4.0 %collective-permute-start.3 = (bf16[128,640]{1,0:T(8,128)(2,1)S(1)}, bf16[128,640]{1,0:T(8,128)(2,1)S(1)}, u32[]{:S(2)}, u32[]{:S(2)}) collective-permute-start(bf16[128,640]{1,0:T(8,128)(2,1)S(1)} %get-tuple-element.40.refs_0_), channel_id=1, source_target_pairs={{0,7},{1,0},{2,1},{3,2},{4,3},{5,4},{6,5},{7,6},{8,15},{9,8},{10,9... | collective-permute-start | bytes 491528 | tf_op jit(solution)/shard_map/ppermute | solution.py:404
  33.2 1.5 %collective-permute-start.8 = (bf16[64,640]{1,0:T(8,128)(2,1)S(1)}, bf16[64,640]{1,0:T(8,128)(2,1)S(1)}, u32[]{:S(2)}, u32[]{:S(2)}) collective-permute-start(bf16[64,640]{1,0:T(8,128)(2,1)S(1)} %get-tuple-element.42), channel_id=1, source_target_pairs={{0,128},{8,136},{16,144},{24,152},{32,160},{40,168},{48,176},{56,1... | collective-permute-start | bytes 245768 | tf_op jit(solution)/shard_map/ppermute | solution.py:394
  34.7 1.6 %collective-permute-start.9 = (bf16[64,640]{1,0:T(8,128)(2,1)S(1)}, bf16[64,640]{1,0:T(8,128)(2,1)S(1)}, u32[]{:S(2)}, u32[]{:S(2)}) collective-permute-start(bf16[64,640]{1,0:T(8,128)(2,1)S(1)} %get-tuple-element.43), channel_id=1, source_target_pairs={{0,192},{8,200},{16,208},{24,216},{32,224},{40,232},{48,240},{56,2... | collective-permute-start | bytes 245768 | tf_op jit(solution)/shard_map/ppermute | solution.py:394
  36.3 1.6 %collective-permute-done.8 = bf16[64,640]{1,0:T(8,128)(2,1)S(1)} collective-permute-done((bf16[64,640]{1,0:T(8,128)(2,1)S(1)}, bf16[64,640]{1,0:T(8,128)(2,1)S(1)}, u32[]{:S(2)}, u32[]{:S(2)}) %collective-permute-start.8) | collective-permute-done | bytes 81952 | tf_op jit(solution)/shard_map/ppermute | solution.py:394
  38.0 1.4 %collective-permute-done.9 = bf16[64,640]{1,0:T(8,128)(2,1)S(1)} collective-permute-done((bf16[64,640]{1,0:T(8,128)(2,1)S(1)}, bf16[64,640]{1,0:T(8,128)(2,1)S(1)}, u32[]{:S(2)}, u32[]{:S(2)}) %collective-permute-start.9) | collective-permute-done | bytes 81952 | tf_op jit(solution)/shard_map/ppermute | solution.py:394
  39.4 2.7 %collective-permute-start.11 = (bf16[192,640]{1,0:T(8,128)(2,1)S(1)}, bf16[192,640]{1,0:T(8,128)(2,1)S(1)}, u32[]{:S(2)}, u32[]{:S(2)}) collective-permute-start(bf16[192,640]{1,0:T(8,128)(2,1)S(1)} %constant_dynamic-update-slice_fusion.refs_1_), channel_id=1, source_target_pairs={{0,7},{1,0},{2,1},{3,2},{4,3},{5,4},{6,5},{7,6},{8,15},{9,8},{10,9... | collective-permute-start | bytes 737288 | tf_op jit(solution)/shard_map/ppermute | solution.py:404
  42.1 2.7 %collective-permute-start.4 = (bf16[128,640]{1,0:T(8,128)(2,1)S(1)}, bf16[128,640]{1,0:T(8,128)(2,1)}, u32[]{:S(2)}, u32[]{:S(2)}) collective-permute-start(bf16[128,640]{1,0:T(8,128)(2,1)S(1)} %collective-permute-done.3.refs_2_), channel_id=1, source_target_pairs={{0,7},{1,0},{2,1},{3,2},{4,3},{5,4},{6,5},{7,6},{8,15},{9,8},{10,9... | collective-permute-start | bytes 491528 | tf_op jit(solution)/shard_map/ppermute | solution.py:404
  44.9 1.9 %shard_map.102 = (f32[320,640]{1,0:T(8,128)S(1)}, f32[320,256]{1,0:T(8,128)S(1)}) custom-call(s32[1]{0:T(128)} %bitcast.4.owners_ref, bf16[5120,640]{1,0:T(8,128)(2,1)} %wq_hbm.9, bf16[5120,256]{1,0:T(8,128)(2,1)} %bitcast.28, bf16[128,640]{1,0:T(8,128)(2,1)S(1)} %get-tuple-element.40.refs_0_, bf16[192,640]{1,0:T(8,128)(2,1)S(1)} %constant_dynamic-update-slice_fusion.refs_1_), custom_call_target="tpu_custom_call" | custom-call | flops 734003200 | bytes 1146880 | tf_op jit(solution)/shard_map/pallas_call | solution.py:100
  46.9 2.7 %collective-permute-start.13 = (bf16[192,640]{1,0:T(8,128)(2,1)S(1)}, bf16[192,640]{1,0:T(8,128)(2,1)S(1)}, u32[]{:S(2)}, u32[]{:S(2)}) collective-permute-start(bf16[192,640]{1,0:T(8,128)(2,1)S(1)} %collective-permute-done.11.refs_3_), channel_id=1, source_target_pairs={{0,7},{1,0},{2,1},{3,2},{4,3},{5,4},{6,5},{7,6},{8,15},{9,8},{10,9... | collective-permute-start | bytes 737288 | tf_op jit(solution)/shard_map/ppermute | solution.py:404
  49.6 2.7 %collective-permute-start.5 = (bf16[128,640]{1,0:T(8,128)(2,1)}, bf16[128,640]{1,0:T(8,128)(2,1)S(1)}, u32[]{:S(2)}, u32[]{:S(2)}) collective-permute-start(bf16[128,640]{1,0:T(8,128)(2,1)} %collective-permute-done.4.refs_2_), channel_id=1, source_target_pairs={{0,7},{1,0},{2,1},{3,2},{4,3},{5,4},{6,5},{7,6},{8,15},{9,8},{10,9... | collective-permute-start | bytes 491528 | tf_op jit(solution)/shard_map/ppermute | solution.py:404
  52.3 3.2 %shard_map.103 = (f32[320,640]{1,0:T(8,128)S(1)}, f32[320,256]{1,0:T(8,128)S(1)}) custom-call(s32[2]{0:T(128)S(1)} %pad_add_fusion.1.owners_ref, bf16[5120,640]{1,0:T(8,128)(2,1)} %wq_hbm.9, bf16[5120,256]{1,0:T(8,128)(2,1)} %bitcast.29, bf16[128,640]{1,0:T(8,128)(2,1)S(1)} %collective-permute-done.refs_0_, ...), custom_call_target="tpu_custom_call" | custom-call | flops 1468006400 | bytes 2293760 | tf_op jit(solution)/shard_map/pallas_call | solution.py:100
  55.7 2.7 %collective-permute-start.15 = (bf16[192,640]{1,0:T(8,128)(2,1)S(1)}, bf16[192,640]{1,0:T(8,128)(2,1)S(1)}, u32[]{:S(2)}, u32[]{:S(2)}) collective-permute-start(bf16[192,640]{1,0:T(8,128)(2,1)S(1)} %collective-permute-done.13.refs_3_), channel_id=1, source_target_pairs={{0,7},{1,0},{2,1},{3,2},{4,3},{5,4},{6,5},{7,6},{8,15},{9,8},{10,9... | collective-permute-start | bytes 737288 | tf_op jit(solution)/shard_map/ppermute | solution.py:404
  58.4 2.0 %collective-permute-start.6 = (bf16[128,640]{1,0:T(8,128)(2,1)S(1)}, bf16[128,640]{1,0:T(8,128)(2,1)S(1)}, u32[]{:S(2)}, u32[]{:S(2)}) collective-permute-start(bf16[128,640]{1,0:T(8,128)(2,1)S(1)} %broadcast_select_fusion.2), channel_id=1, source_target_pairs={{0,1},{1,2},{2,3},{3,4},{4,5},{5,6},{6,7},{7,0},{8,15},{9,8},{10,9... | collective-permute-start | bytes 491528 | tf_op jit(solution)/shard_map/ppermute | solution.py:412
  60.4 3.6 %shard_map.104 = (f32[320,640]{1,0:T(8,128)S(1)}, f32[320,256]{1,0:T(8,128)S(1)}) custom-call(s32[2]{0:T(128)S(1)} %pad_add_fusion.2.owners_ref, bf16[5120,640]{1,0:T(8,128)(2,1)} %wq_hbm.9, bf16[5120,256]{1,0:T(8,128)(2,1)} %bitcast.30, bf16[128,640]{1,0:T(8,128)(2,1)S(1)} %collective-permute-done.1.refs_0_, ...), custom_call_target="tpu_custom_call" | custom-call | flops 1468006400 | bytes 2293760 | tf_op jit(solution)/shard_map/pallas_call | solution.py:100
  64.1 2.0 %collective-permute-start.16 = (bf16[192,640]{1,0:T(8,128)(2,1)S(1)}, bf16[192,640]{1,0:T(8,128)(2,1)S(1)}, u32[]{:S(2)}, u32[]{:S(2)}) collective-permute-start(bf16[192,640]{1,0:T(8,128)(2,1)S(1)} %broadcast_select_fusion.1), channel_id=1, source_target_pairs={{0,1},{1,2},{2,3},{3,4},{4,5},{5,6},{6,7},{7,0},{8,15},{9,8},{10,9... | collective-permute-start | bytes 737288 | tf_op jit(solution)/shard_map/ppermute | solution.py:412
  66.2 3.2 %shard_map.105 = (f32[320,640]{1,0:T(8,128)S(1)}, f32[320,256]{1,0:T(8,128)S(1)}) custom-call(s32[2]{0:T(128)S(1)} %pad_add_fusion.3.owners_ref, bf16[5120,640]{1,0:T(8,128)(2,1)} %wq_hbm.9, bf16[5120,256]{1,0:T(8,128)(2,1)} %bitcast.31, bf16[128,640]{1,0:T(8,128)(2,1)S(1)} %collective-permute-done.2.refs_0_, ...), custom_call_target="tpu_custom_call" | custom-call | flops 1468006400 | bytes 2293760 | tf_op jit(solution)/shard_map/pallas_call | solution.py:100
  69.9 2.1 %shard_map.106 = (bf16[320,640]{1,0:T(8,128)(2,1)S(1)}, bf16[320,256]{1,0:T(8,128)(2,1)S(1)}) custom-call(s32[1]{0:T(128)} %bitcast.2.owner_ref, bf16[5120,640]{1,0:T(8,128)(2,1)} %wq_hbm.9, bf16[5120,256]{1,0:T(8,128)(2,1)} %bitcast.32, bf16[128,640]{1,0:T(8,128)(2,1)S(1)} %collective-permute-done.6.refs_0_, ...), custom_call_target="tpu_custom_call" | custom-call | flops 367001600 | bytes 2000000 | tf_op jit(solution)/shard_map/pallas_call | solution.py:152
  72.0 3.2 %collective-permute-start.17 = (bf16[320,256]{1,0:T(8,128)(2,1)S(1)}, bf16[320,256]{1,0:T(8,128)(2,1)S(1)}, u32[]{:S(2)}, u32[]{:S(2)}) collective-permute-start(bf16[320,256]{1,0:T(8,128)(2,1)S(1)} %get-tuple-element.70), channel_id=1, source_target_pairs={{0,16},{8,56},{16,0},{24,40},{32,48},{40,24},{48,32},{56,8},{64,80... | collective-permute-start | bytes 491528 | tf_op jit(solution)/shard_map/ppermute | solution.py:422
  75.2 2.7 %collective-permute-done.17 = bf16[320,256]{1,0:T(8,128)(2,1)S(1)} collective-permute-done((bf16[320,256]{1,0:T(8,128)(2,1)S(1)}, bf16[320,256]{1,0:T(8,128)(2,1)S(1)}, u32[]{:S(2)}, u32[]{:S(2)}) %collective-permute-start.17) | collective-permute-done | bytes 163872 | tf_op jit(solution)/shard_map/ppermute | solution.py:422
  78.5 10.8 %collective-permute-start.19 = (bf16[2,320,256]{2,1,0:T(8,128)(2,1)S(1)}, bf16[2,320,256]{2,1,0:T(8,128)(2,1)S(1)}, u32[]{:S(2)}, u32[]{:S(2)}) collective-permute-start(bf16[2,320,256]{2,1,0:T(8,128)(2,1)S(1)} %pad_maximum_fusion.refs_0_), channel_id=1, source_target_pairs={{0,8},{8,0},{16,24},{24,16},{32,40},{40,32},{48,56},{56,48},{64,72... | collective-permute-start | bytes 983048 | tf_op jit(solution)/shard_map/ppermute | solution.py:425
  89.2 4.6 %collective-permute-start.20 = (bf16[2,320,256]{2,1,0:T(8,128)(2,1)S(1)}, bf16[2,320,256]{2,1,0:T(8,128)(2,1)S(1)}, u32[]{:S(2)}, u32[]{:S(2)}) collective-permute-start(bf16[2,320,256]{2,1,0:T(8,128)(2,1)S(1)} %collective-permute-done.18.refs_1_), channel_id=1, source_target_pairs={{0,8},{8,0},{16,24},{24,16},{32,40},{40,32},{48,56},{56,48},{64,72... | collective-permute-start | bytes 983048 | tf_op jit(solution)/shard_map/ppermute | solution.py:425
  93.8 1.2 %collective-permute-done.20.refs_3_ = bf16[2,320,256]{2,1,0:T(8,128)(2,1)S(1)} collective-permute-done((bf16[2,320,256]{2,1,0:T(8,128)(2,1)S(1)}, bf16[2,320,256]{2,1,0:T(8,128)(2,1)S(1)}, u32[]{:S(2)}, u32[]{:S(2)}) %collective-permute-start.20) | collective-permute-done | bytes 327712 | tf_op jit(solution)/shard_map/ppermute | solution.py:425
  95.1 5.3 %shard_map.107 = bf16[320,640]{1,0:T(8,128)(2,1)S(1)} custom-call(s32[2]{0:T(128)S(1)} %pad_add_fusion.info_ref, bf16[320,640]{1,0:T(8,128)(2,1)S(1)} %get-tuple-element.69.q_ref, bf16[2,320,256]{2,1,0:T(8,128)(2,1)S(1)} %pad_maximum_fusion.refs_0_, bf16[2,320,256]{2,1,0:T(8,128)(2,1)S(1)} %collective-permute-done.18.refs_1_, ...), custom_call_target="tpu_custom_call" | custom-call | flops 1300000000 | bytes 4000000 | tf_op jit(solution)/shard_map/pallas_call | solution.py:341
  100.5 0.7 gather_fusion
  101.5 20.0 %all_to_all.10 = bf16[32,10,640]{2,1,0:T(8,128)(2,1)S(1)} all-to-all(bf16[32,10,640]{2,1,0:T(8,128)(2,1)S(1)} %broadcast_select_fusion), channel_id=1, replica_groups=mesh['ctx'=32,'mp'=8] {'ctx'}, dimensions={0} | all-to-all | bytes 819200 | tf_op jit(solution)/shard_map/all_to_all | solution.py:435
  121.6 0.8 copy.22
  (71 shorter events, 3.9 us)
Async XLA Ops:
  0.0 12.6 %copy-start = (s32[4,512]{1,0:T(4,128)S(1)}, s32[4,512]{1,0:T(4,128)}, u32[]{:S(2)}) copy-start(s32[4,512]{1,0:T(4,128)} %param.14) | copy-start | bytes 24580
  0.0 13.0 %copy-start.2 = (bf16[5120,2,128]{2,1,0:T(2,128)(2,1)S(1)}, bf16[5120,2,128]{2,1,0:T(2,128)(2,1)}, u32[]{:S(2)}) copy-start(bf16[5120,2,128]{2,1,0:T(2,128)(2,1)} %param.18) | copy-start | bytes 7864324
  3.5 22.8 %all-to-all-start = ((bf16[32,16,768]{2,1,0:T(8,128)(2,1)}), bf16[32,16,768]{2,1,0:T(8,128)(2,1)S(1)}, u32[]{:S(2)}, u32[]{:S(2)}) async-start(bf16[32,16,768]{2,1,0:T(8,128)(2,1)} %shard_map.100), calls=%async_computation | async-start | bytes 1572864 | tf_op jit(solution)/shard_map/all_to_all | solution.py:376
  27.3 9.0 %collective-permute-start.7 = (bf16[64,640]{1,0:T(8,128)(2,1)S(1)}, bf16[64,640]{1,0:T(8,128)(2,1)S(1)}, u32[]{:S(2)}, u32[]{:S(2)}) collective-permute-start(bf16[64,640]{1,0:T(8,128)(2,1)S(1)} %get-tuple-element.41), channel_id=1, source_target_pairs={{0,64},{8,72},{16,80},{24,88},{32,96},{40,104},{48,112},{56,120},{... | collective-permute-start | bytes 245768 | tf_op jit(solution)/shard_map/ppermute | solution.py:394
  27.4 14.7 %collective-permute-start = (bf16[128,640]{1,0:T(8,128)(2,1)S(1)}, bf16[128,640]{1,0:T(8,128)(2,1)S(1)}, u32[]{:S(2)}, u32[]{:S(2)}) collective-permute-start(bf16[128,640]{1,0:T(8,128)(2,1)S(1)} %get-tuple-element.40.refs_0_), channel_id=1, source_target_pairs={{0,1},{1,2},{2,3},{3,4},{4,5},{5,6},{6,7},{7,0},{8,9},{9,10},{10,1... | collective-permute-start | bytes 491528 | tf_op jit(solution)/shard_map/ppermute | solution.py:403
  29.1 13.0 %collective-permute-start.3 = (bf16[128,640]{1,0:T(8,128)(2,1)S(1)}, bf16[128,640]{1,0:T(8,128)(2,1)S(1)}, u32[]{:S(2)}, u32[]{:S(2)}) collective-permute-start(bf16[128,640]{1,0:T(8,128)(2,1)S(1)} %get-tuple-element.40.refs_0_), channel_id=1, source_target_pairs={{0,7},{1,0},{2,1},{3,2},{4,3},{5,4},{6,5},{7,6},{8,15},{9,8},{10,9... | collective-permute-start | bytes 491528 | tf_op jit(solution)/shard_map/ppermute | solution.py:404
  33.2 4.8 %collective-permute-start.8 = (bf16[64,640]{1,0:T(8,128)(2,1)S(1)}, bf16[64,640]{1,0:T(8,128)(2,1)S(1)}, u32[]{:S(2)}, u32[]{:S(2)}) collective-permute-start(bf16[64,640]{1,0:T(8,128)(2,1)S(1)} %get-tuple-element.42), channel_id=1, source_target_pairs={{0,128},{8,136},{16,144},{24,152},{32,160},{40,168},{48,176},{56,1... | collective-permute-start | bytes 245768 | tf_op jit(solution)/shard_map/ppermute | solution.py:394
  34.7 4.6 %collective-permute-start.9 = (bf16[64,640]{1,0:T(8,128)(2,1)S(1)}, bf16[64,640]{1,0:T(8,128)(2,1)S(1)}, u32[]{:S(2)}, u32[]{:S(2)}) collective-permute-start(bf16[64,640]{1,0:T(8,128)(2,1)S(1)} %get-tuple-element.43), channel_id=1, source_target_pairs={{0,192},{8,200},{16,208},{24,216},{32,224},{40,232},{48,240},{56,2... | collective-permute-start | bytes 245768 | tf_op jit(solution)/shard_map/ppermute | solution.py:394
  39.3 7.4 %collective-permute-start.10 = (bf16[192,640]{1,0:T(8,128)(2,1)S(1)}, bf16[192,640]{1,0:T(8,128)(2,1)S(1)}, u32[]{:S(2)}, u32[]{:S(2)}) collective-permute-start(bf16[192,640]{1,0:T(8,128)(2,1)S(1)} %constant_dynamic-update-slice_fusion.refs_1_), channel_id=1, source_target_pairs={{0,1},{1,2},{2,3},{3,4},{4,5},{5,6},{6,7},{7,0},{8,9},{9,10},{10,1... | collective-permute-start | bytes 737288 | tf_op jit(solution)/shard_map/ppermute | solution.py:403
  39.4 7.3 %collective-permute-start.11 = (bf16[192,640]{1,0:T(8,128)(2,1)S(1)}, bf16[192,640]{1,0:T(8,128)(2,1)S(1)}, u32[]{:S(2)}, u32[]{:S(2)}) collective-permute-start(bf16[192,640]{1,0:T(8,128)(2,1)S(1)} %constant_dynamic-update-slice_fusion.refs_1_), channel_id=1, source_target_pairs={{0,7},{1,0},{2,1},{3,2},{4,3},{5,4},{6,5},{7,6},{8,15},{9,8},{10,9... | collective-permute-start | bytes 737288 | tf_op jit(solution)/shard_map/ppermute | solution.py:404
  42.1 7.4 %collective-permute-start.1 = (bf16[128,640]{1,0:T(8,128)(2,1)S(1)}, bf16[128,640]{1,0:T(8,128)(2,1)S(1)}, u32[]{:S(2)}, u32[]{:S(2)}) collective-permute-start(bf16[128,640]{1,0:T(8,128)(2,1)S(1)} %collective-permute-done.refs_0_), channel_id=1, source_target_pairs={{0,1},{1,2},{2,3},{3,4},{4,5},{5,6},{6,7},{7,0},{8,9},{9,10},{10,1... | collective-permute-start | bytes 491528 | tf_op jit(solution)/shard_map/ppermute | solution.py:403
  42.1 7.4 %collective-permute-start.4 = (bf16[128,640]{1,0:T(8,128)(2,1)S(1)}, bf16[128,640]{1,0:T(8,128)(2,1)}, u32[]{:S(2)}, u32[]{:S(2)}) collective-permute-start(bf16[128,640]{1,0:T(8,128)(2,1)S(1)} %collective-permute-done.3.refs_2_), channel_id=1, source_target_pairs={{0,7},{1,0},{2,1},{3,2},{4,3},{5,4},{6,5},{7,6},{8,15},{9,8},{10,9... | collective-permute-start | bytes 491528 | tf_op jit(solution)/shard_map/ppermute | solution.py:404
  46.8 8.8 %collective-permute-start.12 = (bf16[192,640]{1,0:T(8,128)(2,1)S(1)}, bf16[192,640]{1,0:T(8,128)(2,1)S(1)}, u32[]{:S(2)}, u32[]{:S(2)}) collective-permute-start(bf16[192,640]{1,0:T(8,128)(2,1)S(1)} %collective-permute-done.10.refs_1_), channel_id=1, source_target_pairs={{0,1},{1,2},{2,3},{3,4},{4,5},{5,6},{6,7},{7,0},{8,9},{9,10},{10,1... | collective-permute-start | bytes 737288 | tf_op jit(solution)/shard_map/ppermute | solution.py:403
  46.9 8.7 %collective-permute-start.13 = (bf16[192,640]{1,0:T(8,128)(2,1)S(1)}, bf16[192,640]{1,0:T(8,128)(2,1)S(1)}, u32[]{:S(2)}, u32[]{:S(2)}) collective-permute-start(bf16[192,640]{1,0:T(8,128)(2,1)S(1)} %collective-permute-done.11.refs_3_), channel_id=1, source_target_pairs={{0,7},{1,0},{2,1},{3,2},{4,3},{5,4},{6,5},{7,6},{8,15},{9,8},{10,9... | collective-permute-start | bytes 737288 | tf_op jit(solution)/shard_map/ppermute | solution.py:404
  49.5 8.8 %collective-permute-start.2 = (bf16[128,640]{1,0:T(8,128)(2,1)S(1)}, bf16[128,640]{1,0:T(8,128)(2,1)S(1)}, u32[]{:S(2)}, u32[]{:S(2)}) collective-permute-start(bf16[128,640]{1,0:T(8,128)(2,1)S(1)} %collective-permute-done.1.refs_0_), channel_id=1, source_target_pairs={{0,1},{1,2},{2,3},{3,4},{4,5},{5,6},{6,7},{7,0},{8,9},{9,10},{10,1... | collective-permute-start | bytes 491528 | tf_op jit(solution)/shard_map/ppermute | solution.py:403
  49.6 8.8 %collective-permute-start.5 = (bf16[128,640]{1,0:T(8,128)(2,1)}, bf16[128,640]{1,0:T(8,128)(2,1)S(1)}, u32[]{:S(2)}, u32[]{:S(2)}) collective-permute-start(bf16[128,640]{1,0:T(8,128)(2,1)} %collective-permute-done.4.refs_2_), channel_id=1, source_target_pairs={{0,7},{1,0},{2,1},{3,2},{4,3},{5,4},{6,5},{7,6},{8,15},{9,8},{10,9... | collective-permute-start | bytes 491528 | tf_op jit(solution)/shard_map/ppermute | solution.py:404
  55.6 8.5 %collective-permute-start.14 = (bf16[192,640]{1,0:T(8,128)(2,1)S(1)}, bf16[192,640]{1,0:T(8,128)(2,1)S(1)}, u32[]{:S(2)}, u32[]{:S(2)}) collective-permute-start(bf16[192,640]{1,0:T(8,128)(2,1)S(1)} %collective-permute-done.12.refs_1_), channel_id=1, source_target_pairs={{0,1},{1,2},{2,3},{3,4},{4,5},{5,6},{6,7},{7,0},{8,9},{9,10},{10,1... | collective-permute-start | bytes 737288 | tf_op jit(solution)/shard_map/ppermute | solution.py:403
  55.7 8.4 %collective-permute-start.15 = (bf16[192,640]{1,0:T(8,128)(2,1)S(1)}, bf16[192,640]{1,0:T(8,128)(2,1)S(1)}, u32[]{:S(2)}, u32[]{:S(2)}) collective-permute-start(bf16[192,640]{1,0:T(8,128)(2,1)S(1)} %collective-permute-done.13.refs_3_), channel_id=1, source_target_pairs={{0,7},{1,0},{2,1},{3,2},{4,3},{5,4},{6,5},{7,6},{8,15},{9,8},{10,9... | collective-permute-start | bytes 737288 | tf_op jit(solution)/shard_map/ppermute | solution.py:404
  58.4 7.8 %copy-start.3 = (bf16[640]{0:T(1024)(128)(2,1)S(1)}, bf16[640]{0:T(1024)(128)(2,1)}, u32[]{:S(2)}) copy-start(bf16[640]{0:T(1024)(128)(2,1)} %param.17) | copy-start | bytes 3844
  58.4 11.5 %collective-permute-start.6 = (bf16[128,640]{1,0:T(8,128)(2,1)S(1)}, bf16[128,640]{1,0:T(8,128)(2,1)S(1)}, u32[]{:S(2)}, u32[]{:S(2)}) collective-permute-start(bf16[128,640]{1,0:T(8,128)(2,1)S(1)} %broadcast_select_fusion.2), channel_id=1, source_target_pairs={{0,1},{1,2},{2,3},{3,4},{4,5},{5,6},{6,7},{7,0},{8,15},{9,8},{10,9... | collective-permute-start | bytes 491528 | tf_op jit(solution)/shard_map/ppermute | solution.py:412
  64.1 5.8 %collective-permute-start.16 = (bf16[192,640]{1,0:T(8,128)(2,1)S(1)}, bf16[192,640]{1,0:T(8,128)(2,1)S(1)}, u32[]{:S(2)}, u32[]{:S(2)}) collective-permute-start(bf16[192,640]{1,0:T(8,128)(2,1)S(1)} %broadcast_select_fusion.1), channel_id=1, source_target_pairs={{0,1},{1,2},{2,3},{3,4},{4,5},{5,6},{6,7},{7,0},{8,15},{9,8},{10,9... | collective-permute-start | bytes 737288 | tf_op jit(solution)/shard_map/ppermute | solution.py:412
  66.2 3.7 %copy-start.1 = (bf16[128]{0:T(256)(128)(2,1)S(1)}, bf16[128]{0:T(256)(128)(2,1)}, u32[]{:S(2)}) copy-start(bf16[128]{0:T(256)(128)(2,1)} %param.19) | copy-start | bytes 772
  69.9 8.1 %copy-start.4 = (s32[64]{0:T(128)S(1)}, s32[64]{0:T(128)}, u32[]{:S(2)}) copy-start(s32[64]{0:T(128)} %param.15) | copy-start | bytes 772
  72.0 5.9 %collective-permute-start.17 = (bf16[320,256]{1,0:T(8,128)(2,1)S(1)}, bf16[320,256]{1,0:T(8,128)(2,1)S(1)}, u32[]{:S(2)}, u32[]{:S(2)}) collective-permute-start(bf16[320,256]{1,0:T(8,128)(2,1)S(1)} %get-tuple-element.70), channel_id=1, source_target_pairs={{0,16},{8,56},{16,0},{24,40},{32,48},{40,24},{48,32},{56,8},{64,80... | collective-permute-start | bytes 491528 | tf_op jit(solution)/shard_map/ppermute | solution.py:422
  77.9 11.3 %collective-permute-start.18 = (bf16[2,320,256]{2,1,0:T(8,128)(2,1)S(1)}, bf16[2,320,256]{2,1,0:T(8,128)(2,1)S(1)}, u32[]{:S(2)}, u32[]{:S(2)}) collective-permute-start(bf16[2,320,256]{2,1,0:T(8,128)(2,1)S(1)} %pad_maximum_fusion.refs_0_), channel_id=1, source_target_pairs={{0,48},{8,24},{16,32},{24,8},{32,16},{40,56},{48,0},{56,40},{64,11... | collective-permute-start | bytes 983048 | tf_op jit(solution)/shard_map/ppermute | solution.py:423
  78.5 15.4 %collective-permute-start.19 = (bf16[2,320,256]{2,1,0:T(8,128)(2,1)S(1)}, bf16[2,320,256]{2,1,0:T(8,128)(2,1)S(1)}, u32[]{:S(2)}, u32[]{:S(2)}) collective-permute-start(bf16[2,320,256]{2,1,0:T(8,128)(2,1)S(1)} %pad_maximum_fusion.refs_0_), channel_id=1, source_target_pairs={{0,8},{8,0},{16,24},{24,16},{32,40},{40,32},{48,56},{56,48},{64,72... | collective-permute-start | bytes 983048 | tf_op jit(solution)/shard_map/ppermute | solution.py:425
  89.2 5.8 %collective-permute-start.20 = (bf16[2,320,256]{2,1,0:T(8,128)(2,1)S(1)}, bf16[2,320,256]{2,1,0:T(8,128)(2,1)S(1)}, u32[]{:S(2)}, u32[]{:S(2)}) collective-permute-start(bf16[2,320,256]{2,1,0:T(8,128)(2,1)S(1)} %collective-permute-done.18.refs_1_), channel_id=1, source_target_pairs={{0,8},{8,0},{16,24},{24,16},{32,40},{40,32},{48,56},{56,48},{64,72... | collective-permute-start | bytes 983048 | tf_op jit(solution)/shard_map/ppermute | solution.py:425

commit v3 on v2

--- a/solution.py
+++ b/solution.py
@@ -119,51 +119,44 @@
     )(jnp.stack(owners).astype(jnp.int32), *in_hbm(w_query, kv_flat), *args)
 
 
-def finish_kernel(halves, owner_ref, wq_hbm, wk_hbm, *refs):
-    q_sum, k_sum, cos_ref, sin_ref, qb_ref, vb_ref, q_out, kv_out, wq_ref, wk_ref, sems = refs[halves:]
-    feat = wq_ref.shape[0]
+def rotated(x, cosine, sine):
+    return (x * cosine + pltpu.roll(x, HEAD // 2, 1) * sine).astype(jnp.bfloat16)
+
+
+def finish_kernel(halves, keys, owner_ref, w_hbm, *refs):
+    sum_ref, cos_ref, sin_ref, bias_ref, o_ref, w_ref, sem = refs[halves:]
+    feat = w_ref.shape[0]
     at = pl.ds(pl.multiple_of(owner_ref[0] * feat, feat), feat)
-    copy_k = pltpu.make_async_copy(wk_hbm.at[at, :], wk_ref, sems.at[0])
-    copy_q = pltpu.make_async_copy(wq_hbm.at[at, :], wq_ref, sems.at[1])
-    copy_k.start()
-    copy_q.start()
+    copy = pltpu.make_async_copy(w_hbm.at[at, :], w_ref, sem)
+    copy.start()
     rows = rows_of(refs[:halves])
-    copy_k.wait()
-    k = k_sum[...] + jnp.dot(rows, wk_ref[...], preferred_element_type=jnp.float32)
-    copy_q.wait()
-    q = q_sum[...] + jnp.dot(rows, wq_ref[...], preferred_element_type=jnp.float32)
-    q = q + qb_ref[...].astype(jnp.float32)
-    cosine, sine = cos_ref[...], sin_ref[...]
-
-    def rotated(x):
-        return (x * cosine + pltpu.roll(x, HEAD // 2, 1) * sine).astype(jnp.bfloat16)
-
-    kv_out[:, :HEAD] = rotated(k[:, :HEAD])
-    kv_out[:, HEAD:] = (k[:, HEAD:] + vb_ref[...].astype(jnp.float32)).astype(jnp.bfloat16)
-    for h in range(q.shape[1] // HEAD):
+    copy.wait()
+    out = sum_ref[...] + jnp.dot(rows, w_ref[...], preferred_element_type=jnp.float32)
+    bias = bias_ref[...].astype(jnp.float32)
+    if keys:
+        o_ref[:, :HEAD] = rotated(out[:, :HEAD], cos_ref[...], sin_ref[...])
+        o_ref[:, HEAD:] = (out[:, HEAD:] + bias).astype(jnp.bfloat16)
+        return
+    out = out + bias
+    for h in range(out.shape[1] // HEAD):
         at = slice(h * HEAD, (h + 1) * HEAD)
-        q_out[:, at] = rotated(q[:, at])
-
-
-def finish(sums, far, owner, w_query, kv_flat, cosine, sine, q_bias, v_bias):
-    count, feat = sums[0].shape[0], far[0].shape[1]
-    q_cols, k_cols = w_query.shape[1], kv_flat.shape[1]
-    args = [*far, *sums, cosine, sine, q_bias.reshape(1, -1), v_bias.reshape(1, -1)]
+        o_ref[:, at] = rotated(out[:, at], cos_ref[...], sin_ref[...])
+
+
+def finish(keys, total, far, owner, weight, cosine, sine, bias):
+    (count, cols), feat = total.shape, far[0].shape[1]
+    args = [*far, total, cosine, sine, bias.reshape(1, -1)]
     return pl.pallas_call(
-        functools.partial(finish_kernel, len(far)),
-        in_specs=[SMEM_SPEC, HBM_SPEC, HBM_SPEC] + [VMEM_SPEC] * len(args),
-        out_specs=[VMEM_SPEC] * 2,
-        out_shape=[jax.ShapeDtypeStruct(s.shape, jnp.bfloat16) for s in sums],
-        scratch_shapes=[
-            pltpu.VMEM((feat, q_cols), jnp.bfloat16),
-            pltpu.VMEM((feat, k_cols), jnp.bfloat16),
-            pltpu.SemaphoreType.DMA((2,)),
-        ],
+        functools.partial(finish_kernel, len(far), keys),
+        in_specs=[SMEM_SPEC, HBM_SPEC] + [VMEM_SPEC] * len(args),
+        out_specs=VMEM_SPEC,
+        out_shape=jax.ShapeDtypeStruct((count, cols), jnp.bfloat16),
+        scratch_shapes=[pltpu.VMEM((feat, cols), jnp.bfloat16), pltpu.SemaphoreType.DMA],
         compiler_params=pltpu.CompilerParams(vmem_limit_bytes=SMALL_VMEM),
         cost_estimate=pl.CostEstimate(
-            flops=2 * count * feat * (q_cols + k_cols), bytes_accessed=2000000, transcendentals=0
+            flops=4 * count * feat * cols, bytes_accessed=2000000, transcendentals=0
         ),
-    )(owner.reshape(1).astype(jnp.int32), *in_hbm(w_query, kv_flat), *args)
+    )(owner.reshape(1).astype(jnp.int32), *in_hbm(weight), *args)
 
 
 def one_hot(hit):
@@ -293,6 +286,9 @@
             axis=0,
         )
 
+    def tiles(array):
+        return [array[:, n : n + HEAD] for n in range(0, keys_step, HEAD)]
+
     for part in range(clips + 1):
         k_pos = MEMBERS * idx_of(lane % STEP, part) + k_mem
         q_pos = MEMBERS * idx_of(row, part) + member
@@ -313,17 +309,18 @@
             if kp == part:
                 s = jnp.where(allowed, s, NEG_FILL)
             scores.append(s)
-        top = functools.reduce(
-            jnp.maximum, [jnp.max(s, axis=-1, keepdims=True) for s in scores]
-        )
-        total = jnp.zeros((heads * STEP, 1), jnp.float32)
-        acc = jnp.zeros((heads * STEP, HEAD), jnp.float32)
+        top = functools.reduce(jnp.maximum, [tile for s in scores for tile in tiles(s)])
+        top = jnp.max(top, axis=-1, keepdims=True)
+        total, acc = None, None
         for kp, s in enumerate(scores):
             w = jnp.exp2(s - top)
-            total = total + jnp.sum(w, axis=-1, keepdims=True)
-            acc = acc + jnp.dot(
+            more = functools.reduce(jnp.add, tiles(w))
+            total = more if total is None else total + more
+            more = jnp.dot(
                 w.astype(jnp.bfloat16), gather(kp, HEAD), preferred_element_type=jnp.float32
             )
+            acc = more if acc is None else acc + more
+        total = jnp.sum(total, axis=-1, keepdims=True)
         out = (acc / total).astype(jnp.bfloat16)
         for h in range(heads):
             at = slice(h * HEAD, (h + 1) * HEAD)
@@ -394,6 +391,7 @@
         lax.ppermute(out, "ctx", ctx_pairs(lambda y, x, c, dy=dy: (y + dy, x, c)))
         for dy, out in enumerate(others, 1)
     ]
+    first, arrived[0] = lax.optimization_barrier((first, arrived[0]))
     own = [first, jnp.concatenate(arrived, 0)]
 
     fwd, bwd = list(own), list(own)
@@ -414,12 +412,13 @@
     ]
     sums = add_products(sums, parts, owners, w_query, kv_flat)
     far[-1], sums = lax.optimization_barrier((far[-1], sums))
-    q, kv = finish(
-        sums, far, (plane + PLANES // 2) % PLANES, w_query, kv_flat,
-        cosine, sine, b_query, value_offset_bias,
-    )
-
-    near = jnp.stack([kv, lax.ppermute(kv, "ctx", across(True))])
+    opposite = (plane + PLANES // 2) % PLANES
+    kv = finish(True, sums[1], far, opposite, kv_flat, cosine, sine, value_offset_bias)
+    q = finish(False, sums[0], far, opposite, w_query, cosine, sine, b_query)
+
+    beside = lax.ppermute(kv, "ctx", across(True))
+    beside, q = lax.optimization_barrier((beside, q))
+    near = jnp.stack([kv, beside])
     off = lax.ppermute(near, "ctx", across(False))
     swap = ctx_pairs(lambda y, x, c: (y, x, 1 - c))
     pieces = [near, off, lax.ppermute(near, "ctx", swap), lax.ppermute(off, "ctx", swap)]

time: 123 us -> 120 us (0.976)
  blocking collectives: 20 us -> 16.4 us
  starting transfers between devices: 53.8 us -> 50.4 us
  waiting for transfers between devices: 18 us -> 20.2 us
  Pallas kernels: 23.8 us -> 25.2 us
    all_to_all x1, blocking collectives: 20 us -> 16.4 us  [per_device(): recv = lax.all_to_all(send, 'ctx', 0, 0, tiled=True)]
    ppermute x6, waiting for transfers between devices: 0.02 us -> 2.28 us  [per_device(): fwd[h] = lax.ppermute(fwd[h], 'mp', shifted(PLANES, 1))]
    ppermute x2, starting transfers between devices: 4.01 us -> 1.9 us  [per_device(): lax.ppermute(jnp.where(core == 0, fwd[h], bwd[h]), ('ctx', 'mp'), far_pai...]
    ppermute x1, starting transfers between devices: 10.8 us -> 8.98 us  [per_device(): lax.ppermute(near, 'ctx', swap)]
    ppermute x1, waiting for transfers between devices: 2.71 us -> 1.22 us  [per_device(): beside = lax.ppermute(kv, 'ctx', across(True))]
    ppermute x1, starting transfers between devices: 4.59 us -> 5.9 us  [per_device(): lax.ppermute(off, 'ctx', swap)]
    pallas_call x1 -> x2, Pallas kernels: 2.06 us -> 3.14 us  [finish(): pl.pallas_call(functools.partial(finish_kernel, len(far), keys), in_specs...]
  transfers between devices with their start and end apart: 22 -> 22, of which waited for: 6 -> 8; matrix products, arithmetic and copies ran while one was open for 3% -> 4% of each run, Pallas kernels for 10% -> 12%
where the time goes in v3:
time: 120 us
  starting transfers between devices  50.4 us (42%)
  Pallas kernels  25.2 us (21%)
  waiting for transfers between devices  20.2 us (17%)
  blocking collectives  16.4 us (14%)
  local copies, waits for them, and re-layouts  4.81 us (4%)
  other arithmetic  2.15 us (2%)
    ppermute x6, starting transfers between devices, per_device(): bwd[h] = lax.ppermute(bwd[h], 'mp', shifted(PLANES, -1))  17.3 us
    all_to_all x1, blocking collectives, per_device(): recv = lax.all_to_all(send, 'ctx', 0, 0, tiled=True)  16.4 us
    pallas_call x4, Pallas kernels, add_products(): pl.pallas_call(functools.partial(products_kernel, groups, halves, sums is...  12.1 us
    all_to_all x1, waiting for transfers between devices, per_device(): sent = lax.all_to_all(sent, 'ctx', 0, 0, tiled=True)  10.6 us
    ppermute x1, starting transfers between devices, per_device(): lax.ppermute(near, 'ctx', swap)  8.98 us
    all_to_all x1, starting transfers between devices, per_device(): sent = lax.all_to_all(sent, 'ctx', 0, 0, tiled=True)  8.6 us
    ppermute x1, starting transfers between devices, per_device(): lax.ppermute(off, 'ctx', swap)  5.9 us
    pallas_call x1, Pallas kernels, attend(): pl.pallas_call(functools.partial(attend_kernel, heads, clips), out_shape=...  5.53 us
  transfers between devices with their start and end apart: 22, of which 8 were waited for; matrix products, arithmetic and copies ran while one was open for 4% of the time, Pallas kernels for 12%

profile of v3, /device:TPU:1, one launch (start us, length us, event | category | flops | bytes accessed | tf_op | source)
XLA Modules:
  0.0 119.6 jit_solution(14314136441437786677)
XLA Ops:
  0.0 3.5 %shard_map.100 = bf16[32,16,768]{2,1,0:T(8,128)(2,1)} custom-call(s32[4,4]{1,0:T(4,128)} %cand_ref.3, s32[64]{0:T(128)} %slot_ref.3, s32[1]{0:T(128)} %bitcast.3.me_ref, bf16[2,512,640]{2,1,0:T(8,128)(2,1)} %clip_hbm.1, bf16[4,16,640]{2,1,0:T(8,128)(2,1)} %text_ref.1), custom_call_target="tpu_custom_call" | custom-call | tf_op jit(solution)/shard_map/pallas_call | solution.py:208
  3.5 8.6 %all-to-all-start = ((bf16[32,16,768]{2,1,0:T(8,128)(2,1)}), bf16[32,16,768]{2,1,0:T(8,128)(2,1)S(1)}, u32[]{:S(2)}, u32[]{:S(2)}) async-start(bf16[32,16,768]{2,1,0:T(8,128)(2,1)} %shard_map.100), calls=%async_computation | async-start | bytes 1572864 | tf_op jit(solution)/shard_map/all_to_all | solution.py:373
  13.0 1.9 %copy.21 = bf16[640,8,2,128]{3,1,2,0:T(8,128)(2,1)} copy(bf16[640,8,2,128]{3,2,1,0:T(2,128)(2,1)S(1)} %bitcast.33) | data formatting | bytes 5242880
  15.7 10.6 %all-to-all-done.sent_ref = bf16[32,16,768]{2,1,0:T(8,128)(2,1)S(1)} async-done(((bf16[32,16,768]{2,1,0:T(8,128)(2,1)}), bf16[32,16,768]{2,1,0:T(8,128)(2,1)S(1)}, u32[]{:S(2)}, u32[]{:S(2)}) %all-to-all-start) | async-done | bytes 786464 | tf_op jit(solution)/shard_map/all_to_all | solution.py:373
  26.3 1.0 shard_map.101
  27.4 1.7 %collective-permute-start.8 = (bf16[64,640]{1,0:T(8,128)(2,1)S(1)}, bf16[64,640]{1,0:T(8,128)(2,1)S(1)}, u32[]{:S(2)}, u32[]{:S(2)}) collective-permute-start(bf16[64,640]{1,0:T(8,128)(2,1)S(1)} %get-tuple-element.46), channel_id=1, source_target_pairs={{0,128},{8,136},{16,144},{24,152},{32,160},{40,168},{48,176},{56,1... | collective-permute-start | bytes 245768 | tf_op jit(solution)/shard_map/ppermute | solution.py:391
  29.1 1.6 %collective-permute-start.9 = (bf16[64,640]{1,0:T(8,128)(2,1)S(1)}, bf16[64,640]{1,0:T(8,128)(2,1)S(1)}, u32[]{:S(2)}, u32[]{:S(2)}) collective-permute-start(bf16[64,640]{1,0:T(8,128)(2,1)S(1)} %get-tuple-element.47), channel_id=1, source_target_pairs={{0,192},{8,200},{16,208},{24,216},{32,224},{40,232},{48,240},{56,2... | collective-permute-start | bytes 245768 | tf_op jit(solution)/shard_map/ppermute | solution.py:391
  30.7 3.4 %collective-permute-done = bf16[64,640]{1,0:T(8,128)(2,1)S(1)} collective-permute-done((bf16[64,640]{1,0:T(8,128)(2,1)S(1)}, bf16[64,640]{1,0:T(8,128)(2,1)S(1)}, u32[]{:S(2)}, u32[]{:S(2)}) %collective-permute-start) | collective-permute-done | bytes 81952 | tf_op jit(solution)/shard_map/ppermute | solution.py:391
  34.2 1.6 %collective-permute-start.1 = (bf16[128,640]{1,0:T(8,128)(2,1)S(1)}, bf16[128,640]{1,0:T(8,128)(2,1)S(1)}, u32[]{:S(2)}, u32[]{:S(2)}) collective-permute-start(bf16[128,640]{1,0:T(8,128)(2,1)S(1)} %get-tuple-element.44.refs_0_), channel_id=1, source_target_pairs={{0,1},{1,2},{2,3},{3,4},{4,5},{5,6},{6,7},{7,0},{8,9},{9,10},{10,1... | collective-permute-start | bytes 491528 | tf_op jit(solution)/shard_map/ppermute | solution.py:401
  35.8 3.9 %collective-permute-start.4 = (bf16[128,640]{1,0:T(8,128)(2,1)S(1)}, bf16[128,640]{1,0:T(8,128)(2,1)S(1)}, u32[]{:S(2)}, u32[]{:S(2)}) collective-permute-start(bf16[128,640]{1,0:T(8,128)(2,1)S(1)} %get-tuple-element.44.refs_0_), channel_id=1, source_target_pairs={{0,7},{1,0},{2,1},{3,2},{4,3},{5,4},{6,5},{7,6},{8,15},{9,8},{10,9... | collective-permute-start | bytes 491528 | tf_op jit(solution)/shard_map/ppermute | solution.py:402
  39.9 2.7 %collective-permute-start.11 = (bf16[192,640]{1,0:T(8,128)(2,1)S(1)}, bf16[192,640]{1,0:T(8,128)(2,1)S(1)}, u32[]{:S(2)}, u32[]{:S(2)}) collective-permute-start(bf16[192,640]{1,0:T(8,128)(2,1)S(1)} %constant_dynamic-update-slice_fusion.refs_1_), channel_id=1, source_target_pairs={{0,7},{1,0},{2,1},{3,2},{4,3},{5,4},{6,5},{7,6},{8,15},{9,8},{10,9... | collective-permute-start | bytes 737288 | tf_op jit(solution)/shard_map/ppermute | solution.py:402
  43.2 2.7 %collective-permute-start.5 = (bf16[128,640]{1,0:T(8,128)(2,1)S(1)}, bf16[128,640]{1,0:T(8,128)(2,1)}, u32[]{:S(2)}, u32[]{:S(2)}) collective-permute-start(bf16[128,640]{1,0:T(8,128)(2,1)S(1)} %collective-permute-done.4.refs_2_), channel_id=1, source_target_pairs={{0,7},{1,0},{2,1},{3,2},{4,3},{5,4},{6,5},{7,6},{8,15},{9,8},{10,9... | collective-permute-start | bytes 491528 | tf_op jit(solution)/shard_map/ppermute | solution.py:402
  46.0 1.9 %shard_map.102 = (f32[320,640]{1,0:T(8,128)S(1)}, f32[320,256]{1,0:T(8,128)S(1)}) custom-call(s32[1]{0:T(128)} %bitcast.4.owners_ref, bf16[5120,640]{1,0:T(8,128)(2,1)} %w_hbm.1, bf16[5120,256]{1,0:T(8,128)(2,1)} %bitcast.28, bf16[128,640]{1,0:T(8,128)(2,1)S(1)} %get-tuple-element.44.refs_0_, bf16[192,640]{1,0:T(8,128)(2,1)S(1)} %constant_dynamic-update-slice_fusion.refs_1_), custom_call_target="tpu_custom_call" | custom-call | flops 734003200 | bytes 1146880 | tf_op jit(solution)/shard_map/pallas_call | solution.py:100
  48.6 2.7 %collective-permute-start.13 = (bf16[192,640]{1,0:T(8,128)(2,1)S(1)}, bf16[192,640]{1,0:T(8,128)(2,1)S(1)}, u32[]{:S(2)}, u32[]{:S(2)}) collective-permute-start(bf16[192,640]{1,0:T(8,128)(2,1)S(1)} %collective-permute-done.11.refs_3_), channel_id=1, source_target_pairs={{0,7},{1,0},{2,1},{3,2},{4,3},{5,4},{6,5},{7,6},{8,15},{9,8},{10,9... | collective-permute-start | bytes 737288 | tf_op jit(solution)/shard_map/ppermute | solution.py:402
  51.3 0.9 collective-permute-done.2.refs_0_
  52.2 2.7 %collective-permute-start.6 = (bf16[128,640]{1,0:T(8,128)(2,1)}, bf16[128,640]{1,0:T(8,128)(2,1)S(1)}, u32[]{:S(2)}, u32[]{:S(2)}) collective-permute-start(bf16[128,640]{1,0:T(8,128)(2,1)} %collective-permute-done.5.refs_2_), channel_id=1, source_target_pairs={{0,7},{1,0},{2,1},{3,2},{4,3},{5,4},{6,5},{7,6},{8,15},{9,8},{10,9... | collective-permute-start | bytes 491528 | tf_op jit(solution)/shard_map/ppermute | solution.py:402
  54.9 3.2 %shard_map.103 = (f32[320,640]{1,0:T(8,128)S(1)}, f32[320,256]{1,0:T(8,128)S(1)}) custom-call(s32[2]{0:T(128)S(1)} %pad_add_fusion.1.owners_ref, bf16[5120,640]{1,0:T(8,128)(2,1)} %w_hbm.1, bf16[5120,256]{1,0:T(8,128)(2,1)} %bitcast.29, bf16[128,640]{1,0:T(8,128)(2,1)S(1)} %collective-permute-done.1.refs_0_, ...), custom_call_target="tpu_custom_call" | custom-call | flops 1468006400 | bytes 2293760 | tf_op jit(solution)/shard_map/pallas_call | solution.py:100
  58.3 2.7 %collective-permute-start.15 = (bf16[192,640]{1,0:T(8,128)(2,1)S(1)}, bf16[192,640]{1,0:T(8,128)(2,1)S(1)}, u32[]{:S(2)}, u32[]{:S(2)}) collective-permute-start(bf16[192,640]{1,0:T(8,128)(2,1)S(1)} %collective-permute-done.13.refs_3_), channel_id=1, source_target_pairs={{0,7},{1,0},{2,1},{3,2},{4,3},{5,4},{6,5},{7,6},{8,15},{9,8},{10,9... | collective-permute-start | bytes 737288 | tf_op jit(solution)/shard_map/ppermute | solution.py:402
  61.7 1.5 %collective-permute-start.7 = (bf16[128,640]{1,0:T(8,128)(2,1)}, bf16[128,640]{1,0:T(8,128)(2,1)S(1)}, u32[]{:S(2)}, u32[]{:S(2)}) collective-permute-start(bf16[128,640]{1,0:T(8,128)(2,1)} %broadcast_select_fusion.2), channel_id=1, source_target_pairs={{0,1},{1,2},{2,3},{3,4},{4,5},{5,6},{6,7},{7,0},{8,15},{9,8},{10,9... | collective-permute-start | bytes 491528 | tf_op jit(solution)/shard_map/ppermute | solution.py:410
  63.2 3.7 %shard_map.104 = (f32[320,640]{1,0:T(8,128)S(1)}, f32[320,256]{1,0:T(8,128)S(1)}) custom-call(s32[2]{0:T(128)S(1)} %pad_add_fusion.2.owners_ref, bf16[5120,640]{1,0:T(8,128)(2,1)} %w_hbm.1, bf16[5120,256]{1,0:T(8,128)(2,1)} %bitcast.30, bf16[128,640]{1,0:T(8,128)(2,1)} %collective-permute-done.2.refs_0_, ...), custom_call_target="tpu_custom_call" | custom-call | flops 1468006400 | bytes 2293760 | tf_op jit(solution)/shard_map/pallas_call | solution.py:100
  67.4 3.2 %shard_map.105 = (f32[320,640]{1,0:T(8,128)S(1)}, f32[320,256]{1,0:T(8,128)S(1)}) custom-call(s32[2]{0:T(128)S(1)} %pad_add_fusion.3.owners_ref, bf16[5120,640]{1,0:T(8,128)(2,1)} %w_hbm.1, bf16[5120,256]{1,0:T(8,128)(2,1)} %bitcast.31, bf16[128,640]{1,0:T(8,128)(2,1)S(1)} %collective-permute-done.3.refs_0_, ...), custom_call_target="tpu_custom_call" | custom-call | flops 1468006400 | bytes 2293760 | tf_op jit(solution)/shard_map/pallas_call | solution.py:100
  70.7 1.4 %collective-permute-done.16.refs_1_ = bf16[192,640]{1,0:T(8,128)(2,1)S(1)} collective-permute-done((bf16[192,640]{1,0:T(8,128)(2,1)S(1)}, bf16[192,640]{1,0:T(8,128)(2,1)S(1)}, u32[]{:S(2)}, u32[]{:S(2)}) %collective-permute-start.16) | collective-permute-done | bytes 245792 | tf_op jit(solution)/shard_map/ppermute | solution.py:410
  72.1 1.4 %shard_map.106 = bf16[320,256]{1,0:T(8,128)(2,1)S(1)} custom-call(s32[1]{0:T(128)} %bitcast.2.owner_ref, bf16[5120,256]{1,0:T(8,128)(2,1)} %bitcast.32, bf16[128,640]{1,0:T(8,128)(2,1)S(1)} %collective-permute-done.7.refs_0_, bf16[192,640]{1,0:T(8,128)(2,1)S(1)} %collective-permute-done.16.refs_1_, f32[320,256]{1,0:T(8,128)S(1)} %get-tuple-element.69.refs_2_, ...), custom_call_target="tpu_custom_call" | custom-call | flops 209715200 | bytes 2000000 | tf_op jit(solution)/shard_map/pallas_call | solution.py:149
  73.5 2.4 %collective-permute-start.17 = (bf16[320,256]{1,0:T(8,128)(2,1)S(1)}, bf16[320,256]{1,0:T(8,128)(2,1)S(1)}, u32[]{:S(2)}, u32[]{:S(2)}) collective-permute-start(bf16[320,256]{1,0:T(8,128)(2,1)S(1)} %shard_map.106), channel_id=1, source_target_pairs={{0,16},{8,56},{16,0},{24,40},{32,48},{40,24},{48,32},{56,8},{64,80... | collective-permute-start | bytes 491528 | tf_op jit(solution)/shard_map/ppermute | solution.py:419
  75.9 1.8 %shard_map.107.q_ref = bf16[320,640]{1,0:T(8,128)(2,1)S(1)} custom-call(s32[1]{0:T(128)} %bitcast.2.owner_ref, bf16[5120,640]{1,0:T(8,128)(2,1)} %w_hbm.1, bf16[128,640]{1,0:T(8,128)(2,1)S(1)} %collective-permute-done.7.refs_0_, bf16[192,640]{1,0:T(8,128)(2,1)S(1)} %collective-permute-done.16.refs_1_, f32[320,640]{1,0:T(8,128)S(1)} %get-tuple-element.72.refs_2_, ...), custom_call_target="tpu_custom_call" | custom-call | flops 524288000 | bytes 2000000 | tf_op jit(solution)/shard_map/pallas_call | solution.py:149
  77.7 1.2 %collective-permute-done.17 = bf16[320,256]{1,0:T(8,128)(2,1)S(1)} collective-permute-done((bf16[320,256]{1,0:T(8,128)(2,1)S(1)}, bf16[320,256]{1,0:T(8,128)(2,1)S(1)}, u32[]{:S(2)}, u32[]{:S(2)}) %collective-permute-start.17) | collective-permute-done | bytes 163872 | tf_op jit(solution)/shard_map/ppermute | solution.py:419
  79.5 9.0 %collective-permute-start.19 = (bf16[2,320,256]{2,1,0:T(8,128)(2,1)S(1)}, bf16[2,320,256]{2,1,0:T(8,128)(2,1)S(1)}, u32[]{:S(2)}, u32[]{:S(2)}) collective-permute-start(bf16[2,320,256]{2,1,0:T(8,128)(2,1)S(1)} %pad_maximum_fusion.refs_0_), channel_id=1, source_target_pairs={{0,8},{8,0},{16,24},{24,16},{32,40},{40,32},{48,56},{56,48},{64,72... | collective-permute-start | bytes 983048 | tf_op jit(solution)/shard_map/ppermute | solution.py:424
  88.5 5.9 %collective-permute-start.20 = (bf16[2,320,256]{2,1,0:T(8,128)(2,1)S(1)}, bf16[2,320,256]{2,1,0:T(8,128)(2,1)S(1)}, u32[]{:S(2)}, u32[]{:S(2)}) collective-permute-start(bf16[2,320,256]{2,1,0:T(8,128)(2,1)S(1)} %collective-permute-done.18.refs_1_), channel_id=1, source_target_pairs={{0,8},{8,0},{16,24},{24,16},{32,40},{40,32},{48,56},{56,48},{64,72... | collective-permute-start | bytes 983048 | tf_op jit(solution)/shard_map/ppermute | solution.py:424
  94.4 1.2 %collective-permute-done.20.refs_3_ = bf16[2,320,256]{2,1,0:T(8,128)(2,1)S(1)} collective-permute-done((bf16[2,320,256]{2,1,0:T(8,128)(2,1)S(1)}, bf16[2,320,256]{2,1,0:T(8,128)(2,1)S(1)}, u32[]{:S(2)}, u32[]{:S(2)}) %collective-permute-start.20) | collective-permute-done | bytes 327712 | tf_op jit(solution)/shard_map/ppermute | solution.py:424
  95.7 5.5 %shard_map.108 = bf16[320,640]{1,0:T(8,128)(2,1)S(1)} custom-call(s32[2]{0:T(128)S(1)} %pad_add_fusion.info_ref, bf16[320,640]{1,0:T(8,128)(2,1)S(1)} %shard_map.107.q_ref, bf16[2,320,256]{2,1,0:T(8,128)(2,1)S(1)} %pad_maximum_fusion.refs_0_, bf16[2,320,256]{2,1,0:T(8,128)(2,1)S(1)} %collective-permute-done.18.refs_1_, ...), custom_call_target="tpu_custom_call" | custom-call | flops 1300000000 | bytes 4000000 | tf_op jit(solution)/shard_map/pallas_call | solution.py:338
  102.4 16.4 %all_to_all.10 = bf16[32,10,640]{2,1,0:T(8,128)(2,1)S(1)} all-to-all(bf16[32,10,640]{2,1,0:T(8,128)(2,1)S(1)} %broadcast_select_fusion), channel_id=1, replica_groups=mesh['ctx'=32,'mp'=8] {'ctx'}, dimensions={0} | all-to-all | bytes 819200 | tf_op jit(solution)/shard_map/all_to_all | solution.py:434
  118.9 0.8 copy.22
  (72 shorter events, 6.4 us)
Async XLA Ops:
  0.0 12.6 %copy-start = (s32[4,512]{1,0:T(4,128)S(1)}, s32[4,512]{1,0:T(4,128)}, u32[]{:S(2)}) copy-start(s32[4,512]{1,0:T(4,128)} %param.14) | copy-start | bytes 24580
  0.0 13.0 %copy-start.2 = (bf16[5120,2,128]{2,1,0:T(2,128)(2,1)S(1)}, bf16[5120,2,128]{2,1,0:T(2,128)(2,1)}, u32[]{:S(2)}) copy-start(bf16[5120,2,128]{2,1,0:T(2,128)(2,1)} %param.18) | copy-start | bytes 7864324
  3.5 22.8 %all-to-all-start = ((bf16[32,16,768]{2,1,0:T(8,128)(2,1)}), bf16[32,16,768]{2,1,0:T(8,128)(2,1)S(1)}, u32[]{:S(2)}, u32[]{:S(2)}) async-start(bf16[32,16,768]{2,1,0:T(8,128)(2,1)} %shard_map.100), calls=%async_computation | async-start | bytes 1572864 | tf_op jit(solution)/shard_map/all_to_all | solution.py:373
  27.3 6.8 %collective-permute-start = (bf16[64,640]{1,0:T(8,128)(2,1)S(1)}, bf16[64,640]{1,0:T(8,128)(2,1)S(1)}, u32[]{:S(2)}, u32[]{:S(2)}) collective-permute-start(bf16[64,640]{1,0:T(8,128)(2,1)S(1)} %get-tuple-element.43), channel_id=1, source_target_pairs={{0,64},{8,72},{16,80},{24,88},{32,96},{40,104},{48,112},{56,120},{... | collective-permute-start | bytes 245768 | tf_op jit(solution)/shard_map/ppermute | solution.py:391
  27.4 12.4 %collective-permute-start.8 = (bf16[64,640]{1,0:T(8,128)(2,1)S(1)}, bf16[64,640]{1,0:T(8,128)(2,1)S(1)}, u32[]{:S(2)}, u32[]{:S(2)}) collective-permute-start(bf16[64,640]{1,0:T(8,128)(2,1)S(1)} %get-tuple-element.46), channel_id=1, source_target_pairs={{0,128},{8,136},{16,144},{24,152},{32,160},{40,168},{48,176},{56,1... | collective-permute-start | bytes 245768 | tf_op jit(solution)/shard_map/ppermute | solution.py:391
  29.1 10.7 %collective-permute-start.9 = (bf16[64,640]{1,0:T(8,128)(2,1)S(1)}, bf16[64,640]{1,0:T(8,128)(2,1)S(1)}, u32[]{:S(2)}, u32[]{:S(2)}) collective-permute-start(bf16[64,640]{1,0:T(8,128)(2,1)S(1)} %get-tuple-element.47), channel_id=1, source_target_pairs={{0,192},{8,200},{16,208},{24,216},{32,224},{40,232},{48,240},{56,2... | collective-permute-start | bytes 245768 | tf_op jit(solution)/shard_map/ppermute | solution.py:391
  34.2 9.1 %collective-permute-start.1 = (bf16[128,640]{1,0:T(8,128)(2,1)S(1)}, bf16[128,640]{1,0:T(8,128)(2,1)S(1)}, u32[]{:S(2)}, u32[]{:S(2)}) collective-permute-start(bf16[128,640]{1,0:T(8,128)(2,1)S(1)} %get-tuple-element.44.refs_0_), channel_id=1, source_target_pairs={{0,1},{1,2},{2,3},{3,4},{4,5},{5,6},{6,7},{7,0},{8,9},{9,10},{10,1... | collective-permute-start | bytes 491528 | tf_op jit(solution)/shard_map/ppermute | solution.py:401
  35.8 7.4 %collective-permute-start.4 = (bf16[128,640]{1,0:T(8,128)(2,1)S(1)}, bf16[128,640]{1,0:T(8,128)(2,1)S(1)}, u32[]{:S(2)}, u32[]{:S(2)}) collective-permute-start(bf16[128,640]{1,0:T(8,128)(2,1)S(1)} %get-tuple-element.44.refs_0_), channel_id=1, source_target_pairs={{0,7},{1,0},{2,1},{3,2},{4,3},{5,4},{6,5},{7,6},{8,15},{9,8},{10,9... | collective-permute-start | bytes 491528 | tf_op jit(solution)/shard_map/ppermute | solution.py:402
  39.8 8.8 %collective-permute-start.10 = (bf16[192,640]{1,0:T(8,128)(2,1)S(1)}, bf16[192,640]{1,0:T(8,128)(2,1)S(1)}, u32[]{:S(2)}, u32[]{:S(2)}) collective-permute-start(bf16[192,640]{1,0:T(8,128)(2,1)S(1)} %constant_dynamic-update-slice_fusion.refs_1_), channel_id=1, source_target_pairs={{0,1},{1,2},{2,3},{3,4},{4,5},{5,6},{6,7},{7,0},{8,9},{9,10},{10,1... | collective-permute-start | bytes 737288 | tf_op jit(solution)/shard_map/ppermute | solution.py:401
  39.9 8.7 %collective-permute-start.11 = (bf16[192,640]{1,0:T(8,128)(2,1)S(1)}, bf16[192,640]{1,0:T(8,128)(2,1)S(1)}, u32[]{:S(2)}, u32[]{:S(2)}) collective-permute-start(bf16[192,640]{1,0:T(8,128)(2,1)S(1)} %constant_dynamic-update-slice_fusion.refs_1_), channel_id=1, source_target_pairs={{0,7},{1,0},{2,1},{3,2},{4,3},{5,4},{6,5},{7,6},{8,15},{9,8},{10,9... | collective-permute-start | bytes 737288 | tf_op jit(solution)/shard_map/ppermute | solution.py:402
  43.2 9.0 %collective-permute-start.2 = (bf16[128,640]{1,0:T(8,128)(2,1)S(1)}, bf16[128,640]{1,0:T(8,128)(2,1)}, u32[]{:S(2)}, u32[]{:S(2)}) collective-permute-start(bf16[128,640]{1,0:T(8,128)(2,1)S(1)} %collective-permute-done.1.refs_0_), channel_id=1, source_target_pairs={{0,1},{1,2},{2,3},{3,4},{4,5},{5,6},{6,7},{7,0},{8,9},{9,10},{10,1... | collective-permute-start | bytes 491528 | tf_op jit(solution)/shard_map/ppermute | solution.py:401
  43.2 9.0 %collective-permute-start.5 = (bf16[128,640]{1,0:T(8,128)(2,1)S(1)}, bf16[128,640]{1,0:T(8,128)(2,1)}, u32[]{:S(2)}, u32[]{:S(2)}) collective-permute-start(bf16[128,640]{1,0:T(8,128)(2,1)S(1)} %collective-permute-done.4.refs_2_), channel_id=1, source_target_pairs={{0,7},{1,0},{2,1},{3,2},{4,3},{5,4},{6,5},{7,6},{8,15},{9,8},{10,9... | collective-permute-start | bytes 491528 | tf_op jit(solution)/shard_map/ppermute | solution.py:402
  48.6 9.6 %collective-permute-start.12 = (bf16[192,640]{1,0:T(8,128)(2,1)S(1)}, bf16[192,640]{1,0:T(8,128)(2,1)S(1)}, u32[]{:S(2)}, u32[]{:S(2)}) collective-permute-start(bf16[192,640]{1,0:T(8,128)(2,1)S(1)} %collective-permute-done.10.refs_1_), channel_id=1, source_target_pairs={{0,1},{1,2},{2,3},{3,4},{4,5},{5,6},{6,7},{7,0},{8,9},{9,10},{10,1... | collective-permute-start | bytes 737288 | tf_op jit(solution)/shard_map/ppermute | solution.py:401
  48.6 9.6 %collective-permute-start.13 = (bf16[192,640]{1,0:T(8,128)(2,1)S(1)}, bf16[192,640]{1,0:T(8,128)(2,1)S(1)}, u32[]{:S(2)}, u32[]{:S(2)}) collective-permute-start(bf16[192,640]{1,0:T(8,128)(2,1)S(1)} %collective-permute-done.11.refs_3_), channel_id=1, source_target_pairs={{0,7},{1,0},{2,1},{3,2},{4,3},{5,4},{6,5},{7,6},{8,15},{9,8},{10,9... | collective-permute-start | bytes 737288 | tf_op jit(solution)/shard_map/ppermute | solution.py:402
  52.2 8.8 %collective-permute-start.3 = (bf16[128,640]{1,0:T(8,128)(2,1)}, bf16[128,640]{1,0:T(8,128)(2,1)S(1)}, u32[]{:S(2)}, u32[]{:S(2)}) collective-permute-start(bf16[128,640]{1,0:T(8,128)(2,1)} %collective-permute-done.2.refs_0_), channel_id=1, source_target_pairs={{0,1},{1,2},{2,3},{3,4},{4,5},{5,6},{6,7},{7,0},{8,9},{9,10},{10,1... | collective-permute-start | bytes 491528 | tf_op jit(solution)/shard_map/ppermute | solution.py:401
  52.2 8.8 %collective-permute-start.6 = (bf16[128,640]{1,0:T(8,128)(2,1)}, bf16[128,640]{1,0:T(8,128)(2,1)S(1)}, u32[]{:S(2)}, u32[]{:S(2)}) collective-permute-start(bf16[128,640]{1,0:T(8,128)(2,1)} %collective-permute-done.5.refs_2_), channel_id=1, source_target_pairs={{0,7},{1,0},{2,1},{3,2},{4,3},{5,4},{6,5},{7,6},{8,15},{9,8},{10,9... | collective-permute-start | bytes 491528 | tf_op jit(solution)/shard_map/ppermute | solution.py:402
  58.2 8.7 %collective-permute-start.14 = (bf16[192,640]{1,0:T(8,128)(2,1)S(1)}, bf16[192,640]{1,0:T(8,128)(2,1)S(1)}, u32[]{:S(2)}, u32[]{:S(2)}) collective-permute-start(bf16[192,640]{1,0:T(8,128)(2,1)S(1)} %collective-permute-done.12.refs_1_), channel_id=1, source_target_pairs={{0,1},{1,2},{2,3},{3,4},{4,5},{5,6},{6,7},{7,0},{8,9},{9,10},{10,1... | collective-permute-start | bytes 737288 | tf_op jit(solution)/shard_map/ppermute | solution.py:401
  58.3 8.6 %collective-permute-start.15 = (bf16[192,640]{1,0:T(8,128)(2,1)S(1)}, bf16[192,640]{1,0:T(8,128)(2,1)S(1)}, u32[]{:S(2)}, u32[]{:S(2)}) collective-permute-start(bf16[192,640]{1,0:T(8,128)(2,1)S(1)} %collective-permute-done.13.refs_3_), channel_id=1, source_target_pairs={{0,7},{1,0},{2,1},{3,2},{4,3},{5,4},{6,5},{7,6},{8,15},{9,8},{10,9... | collective-permute-start | bytes 737288 | tf_op jit(solution)/shard_map/ppermute | solution.py:402
  61.7 10.4 %collective-permute-start.7 = (bf16[128,640]{1,0:T(8,128)(2,1)}, bf16[128,640]{1,0:T(8,128)(2,1)S(1)}, u32[]{:S(2)}, u32[]{:S(2)}) collective-permute-start(bf16[128,640]{1,0:T(8,128)(2,1)} %broadcast_select_fusion.2), channel_id=1, source_target_pairs={{0,1},{1,2},{2,3},{3,4},{4,5},{5,6},{6,7},{7,0},{8,15},{9,8},{10,9... | collective-permute-start | bytes 491528 | tf_op jit(solution)/shard_map/ppermute | solution.py:410
  67.0 5.1 %collective-permute-start.16 = (bf16[192,640]{1,0:T(8,128)(2,1)S(1)}, bf16[192,640]{1,0:T(8,128)(2,1)S(1)}, u32[]{:S(2)}, u32[]{:S(2)}) collective-permute-start(bf16[192,640]{1,0:T(8,128)(2,1)S(1)} %broadcast_select_fusion.1), channel_id=1, source_target_pairs={{0,1},{1,2},{2,3},{3,4},{4,5},{5,6},{6,7},{7,0},{8,15},{9,8},{10,9... | collective-permute-start | bytes 737288 | tf_op jit(solution)/shard_map/ppermute | solution.py:410
  67.4 4.7 %copy-start.1 = (bf16[128]{0:T(256)(128)(2,1)S(1)}, bf16[128]{0:T(256)(128)(2,1)}, u32[]{:S(2)}) copy-start(bf16[128]{0:T(256)(128)(2,1)} %param.19) | copy-start | bytes 772
  70.7 5.2 %copy-start.3 = (bf16[640]{0:T(1024)(128)(2,1)S(1)}, bf16[640]{0:T(1024)(128)(2,1)}, u32[]{:S(2)}) copy-start(bf16[640]{0:T(1024)(128)(2,1)} %param.17) | copy-start | bytes 3844
  73.5 5.5 %collective-permute-start.17 = (bf16[320,256]{1,0:T(8,128)(2,1)S(1)}, bf16[320,256]{1,0:T(8,128)(2,1)S(1)}, u32[]{:S(2)}, u32[]{:S(2)}) collective-permute-start(bf16[320,256]{1,0:T(8,128)(2,1)S(1)} %shard_map.106), channel_id=1, source_target_pairs={{0,16},{8,56},{16,0},{24,40},{32,48},{40,24},{48,32},{56,8},{64,80... | collective-permute-start | bytes 491528 | tf_op jit(solution)/shard_map/ppermute | solution.py:419
  75.9 3.2 %copy-start.4 = (s32[64]{0:T(128)S(1)}, s32[64]{0:T(128)}, u32[]{:S(2)}) copy-start(s32[64]{0:T(128)} %param.15) | copy-start | bytes 772
  79.0 9.5 %collective-permute-start.18 = (bf16[2,320,256]{2,1,0:T(8,128)(2,1)S(1)}, bf16[2,320,256]{2,1,0:T(8,128)(2,1)S(1)}, u32[]{:S(2)}, u32[]{:S(2)}) collective-permute-start(bf16[2,320,256]{2,1,0:T(8,128)(2,1)S(1)} %pad_maximum_fusion.refs_0_), channel_id=1, source_target_pairs={{0,48},{8,24},{16,32},{24,8},{32,16},{40,56},{48,0},{56,40},{64,11... | collective-permute-start | bytes 983048 | tf_op jit(solution)/shard_map/ppermute | solution.py:422
  79.5 14.9 %collective-permute-start.19 = (bf16[2,320,256]{2,1,0:T(8,128)(2,1)S(1)}, bf16[2,320,256]{2,1,0:T(8,128)(2,1)S(1)}, u32[]{:S(2)}, u32[]{:S(2)}) collective-permute-start(bf16[2,320,256]{2,1,0:T(8,128)(2,1)S(1)} %pad_maximum_fusion.refs_0_), channel_id=1, source_target_pairs={{0,8},{8,0},{16,24},{24,16},{32,40},{40,32},{48,56},{56,48},{64,72... | collective-permute-start | bytes 983048 | tf_op jit(solution)/shard_map/ppermute | solution.py:424
  88.5 7.2 %collective-permute-start.20 = (bf16[2,320,256]{2,1,0:T(8,128)(2,1)S(1)}, bf16[2,320,256]{2,1,0:T(8,128)(2,1)S(1)}, u32[]{:S(2)}, u32[]{:S(2)}) collective-permute-start(bf16[2,320,256]{2,1,0:T(8,128)(2,1)S(1)} %collective-permute-done.18.refs_1_), channel_id=1, source_target_pairs={{0,8},{8,0},{16,24},{24,16},{32,40},{40,32},{48,56},{56,48},{64,72... | collective-permute-start | bytes 983048 | tf_op jit(solution)/shard_map/ppermute | solution.py:424

commit v4 on v3

--- a/solution.py
+++ b/solution.py
@@ -250,8 +250,8 @@
     )(*in_hbm(candidates, clip_slot), group.reshape(1).astype(jnp.int32), sent)
 
 
-def attend_kernel(heads, clips, info_ref, q_ref, *refs):
-    o_ref, key_refs = refs[-1], refs[:-1]
+def attend_kernel(heads, clips, info_ref, q_ref, to_ref, *refs):
+    o_ref, out_ref, key_refs = refs[-2], refs[-1], refs[:-2]
     group, member = info_ref[0], info_ref[1]
     my_x, my_core = member // 2, member % 2
     scale = math.log2(math.e) / math.sqrt(HEAD)
@@ -325,26 +325,32 @@
         for h in range(heads):
             at = slice(h * HEAD, (h + 1) * HEAD)
             if part == clips:
-                o_ref[pl.ds(part * STEP, STEP), at] = out[h * STEP : (h + 1) * STEP]
+                out_ref[pl.ds(part * STEP, STEP), at] = out[h * STEP : (h + 1) * STEP]
                 continue
             for dy in range(GROUPS):
                 y = (group + GROUPS - dy) % GROUPS
                 to = pl.ds(pl.multiple_of(part * STEP + y * PART, PART), PART)
                 first = h * STEP + dy * PART
-                o_ref[to, at] = out[first : first + PART]
-
-
-def attend(info, q, pieces, heads, clips):
+                out_ref[to, at] = out[first : first + PART]
+    _, at = iotas((o_ref.shape[0], out_ref.shape[0]))
+    pick = one_hot(at == to_ref[...])
+    o_ref[...] = jnp.dot(pick, out_ref[...], preferred_element_type=jnp.float32).astype(
+        jnp.bfloat16
+    )
+
+
+def attend(info, q, to, pieces, heads, clips):
     return pl.pallas_call(
         functools.partial(attend_kernel, heads, clips),
         out_shape=jax.ShapeDtypeStruct(q.shape, jnp.bfloat16),
-        in_specs=[SMEM_SPEC] + [VMEM_SPEC] * (1 + len(pieces)),
+        in_specs=[SMEM_SPEC] + [VMEM_SPEC] * (2 + len(pieces)),
         out_specs=VMEM_SPEC,
+        scratch_shapes=[pltpu.VMEM(q.shape, jnp.bfloat16)],
         compiler_params=pltpu.CompilerParams(vmem_limit_bytes=MID_VMEM),
         cost_estimate=pl.CostEstimate(
             flops=1300000000, bytes_accessed=4000000, transcendentals=2500000
         ),
-    )(info, q, *pieces)
+    )(info, q, to, *pieces)
 
 
 def per_device(
@@ -384,7 +390,14 @@
         return (MEMBERS * (clip_idx + PART * y) + member).astype(jnp.int32).reshape(-1)
 
     cosine, sine = rope_tables(jnp.concatenate([text_at] + [clip_pos(dy) for dy in range(GROUPS)]))
-    sent, kv_flat, cosine, sine = lax.optimization_barrier((sent, kv_flat, cosine, sine))
+    blocks = block_order.shape[0]
+    block_len = (cands * clip_len + text_len) // blocks
+    sub = block_len // MEMBERS
+    send_from = sub * block_order.reshape(DEVICES, 1, 2) + jnp.arange(sub).reshape(1, sub, 1)
+    send_from = send_from.astype(jnp.int32).reshape(-1, 1)
+    sent, kv_flat, cosine, sine, send_from = lax.optimization_barrier(
+        (sent, kv_flat, cosine, sine, send_from)
+    )
 
     first, *others = unpack(candidates, clip_slot, group, sent, clips_here)
     arrived = [
@@ -424,16 +437,12 @@
     pieces = [near, off, lax.ppermute(near, "ctx", swap), lax.ppermute(off, "ctx", swap)]
 
     info = jnp.stack([group, member]).astype(jnp.int32)
-    out = attend(info, q, pieces, heads, cands)
-
-    blocks = block_order.shape[0]
-    block_len = (cands * clip_len + text_len) // blocks
-    sub = block_len // MEMBERS
-    send = jnp.take(out.reshape(blocks, sub, width), block_order, axis=0)
-    send = send.reshape(DEVICES, 2 * sub, width)
+    out = attend(info, q, send_from, pieces, heads, cands)
+
+    send = out.reshape(DEVICES, sub, 2, width)
     recv = lax.all_to_all(send, "ctx", 0, 0, tiled=True)
-    recv = recv.reshape(GROUPS, MEMBERS, 2, sub, width)
-    return recv.transpose(0, 2, 3, 1, 4).reshape(seqs, 2, block_len, width)
+    recv = recv.reshape(GROUPS, MEMBERS, sub, 2, width)
+    return recv.transpose(0, 3, 2, 1, 4).reshape(seqs, 2, block_len, width)
 
 
 def solution(mesh):

time: 120 us -> 117 us (0.975)
  blocking collectives: 16.4 us -> 13.8 us
    all_to_all x1, blocking collectives: 16.4 us -> 13.8 us  [per_device(): recv = lax.all_to_all(send, 'ctx', 0, 0, tiled=True)]
where the time goes in v4:
time: 117 us; the launch traced here: 116 us
  starting transfers between devices  50.9 us (44%)
  Pallas kernels  25.5 us (22%)
  waiting for transfers between devices  19.7 us (17%)
  blocking collectives  13.8 us (12%)
  local copies, waits for them, and re-layouts  3.94 us (3%)
  other arithmetic  1.98 us (2%)
    ppermute x6, starting transfers between devices, per_device(): bwd[h] = lax.ppermute(bwd[h], 'mp', shifted(PLANES, -1))  17.3 us
    all_to_all x1, blocking collectives, per_device(): recv = lax.all_to_all(send, 'ctx', 0, 0, tiled=True)  13.8 us
    pallas_call x4, Pallas kernels, add_products(): pl.pallas_call(functools.partial(products_kernel, groups, halves, sums is...  12.1 us
    all_to_all x1, waiting for transfers between devices, per_device(): sent = lax.all_to_all(sent, 'ctx', 0, 0, tiled=True)  10.3 us
    ppermute x1, starting transfers between devices, per_device(): lax.ppermute(near, 'ctx', swap)  8.96 us
    all_to_all x1, starting transfers between devices, per_device(): sent = lax.all_to_all(sent, 'ctx', 0, 0, tiled=True)  8.6 us
    ppermute x1, starting transfers between devices, per_device(): lax.ppermute(off, 'ctx', swap)  6.37 us
    pallas_call x1, Pallas kernels, attend(): pl.pallas_call(functools.partial(attend_kernel, heads, clips), out_shape=...  5.81 us
  transfers between devices with their start and end apart: 22, of which 8 were waited for; matrix products, arithmetic and copies ran while one was open for 4% of the time, Pallas kernels for 12%

profile of v4, /device:TPU:1, one launch (start us, length us, event | category | flops | bytes accessed | tf_op | source)
XLA Modules:
  0.0 116.3 jit_solution(519661105901835211)
XLA Ops:
  0.0 3.5 %shard_map.100 = bf16[32,16,768]{2,1,0:T(8,128)(2,1)} custom-call(s32[4,4]{1,0:T(4,128)} %cand_ref.3, s32[64]{0:T(128)} %slot_ref.3, s32[1]{0:T(128)} %bitcast.3.me_ref, bf16[2,512,640]{2,1,0:T(8,128)(2,1)} %clip_hbm.1, bf16[4,16,640]{2,1,0:T(8,128)(2,1)} %text_ref.1), custom_call_target="tpu_custom_call" | custom-call | tf_op jit(solution)/shard_map/pallas_call | solution.py:208
  3.5 8.6 %all-to-all-start = ((bf16[32,16,768]{2,1,0:T(8,128)(2,1)}), bf16[32,16,768]{2,1,0:T(8,128)(2,1)S(1)}, u32[]{:S(2)}, u32[]{:S(2)}) async-start(bf16[32,16,768]{2,1,0:T(8,128)(2,1)} %shard_map.100), calls=%async_computation | async-start | bytes 1572864 | tf_op jit(solution)/shard_map/all_to_all | solution.py:379
  13.1 1.9 %copy.19 = bf16[640,8,2,128]{3,1,2,0:T(8,128)(2,1)} copy(bf16[640,8,2,128]{3,2,1,0:T(2,128)(2,1)S(1)} %bitcast.31) | data formatting | bytes 5242880
  16.0 10.3 %all-to-all-done.sent_ref = bf16[32,16,768]{2,1,0:T(8,128)(2,1)S(1)} async-done(((bf16[32,16,768]{2,1,0:T(8,128)(2,1)}), bf16[32,16,768]{2,1,0:T(8,128)(2,1)S(1)}, u32[]{:S(2)}, u32[]{:S(2)}) %all-to-all-start) | async-done | bytes 786464 | tf_op jit(solution)/shard_map/all_to_all | solution.py:379
  26.3 1.0 shard_map.101
  27.4 1.7 %collective-permute-start.8 = (bf16[64,640]{1,0:T(8,128)(2,1)S(1)}, bf16[64,640]{1,0:T(8,128)(2,1)S(1)}, u32[]{:S(2)}, u32[]{:S(2)}) collective-permute-start(bf16[64,640]{1,0:T(8,128)(2,1)S(1)} %get-tuple-element.47), channel_id=1, source_target_pairs={{0,128},{8,136},{16,144},{24,152},{32,160},{40,168},{48,176},{56,1... | collective-permute-start | bytes 245768 | tf_op jit(solution)/shard_map/ppermute | solution.py:404
  29.1 1.6 %collective-permute-start.9 = (bf16[64,640]{1,0:T(8,128)(2,1)S(1)}, bf16[64,640]{1,0:T(8,128)(2,1)S(1)}, u32[]{:S(2)}, u32[]{:S(2)}) collective-permute-start(bf16[64,640]{1,0:T(8,128)(2,1)S(1)} %get-tuple-element.48), channel_id=1, source_target_pairs={{0,192},{8,200},{16,208},{24,216},{32,224},{40,232},{48,240},{56,2... | collective-permute-start | bytes 245768 | tf_op jit(solution)/shard_map/ppermute | solution.py:404
  30.7 3.4 %collective-permute-done = bf16[64,640]{1,0:T(8,128)(2,1)S(1)} collective-permute-done((bf16[64,640]{1,0:T(8,128)(2,1)S(1)}, bf16[64,640]{1,0:T(8,128)(2,1)S(1)}, u32[]{:S(2)}, u32[]{:S(2)}) %collective-permute-start) | collective-permute-done | bytes 81952 | tf_op jit(solution)/shard_map/ppermute | solution.py:404
  34.2 1.6 %collective-permute-start.1 = (bf16[128,640]{1,0:T(8,128)(2,1)S(1)}, bf16[128,640]{1,0:T(8,128)(2,1)S(1)}, u32[]{:S(2)}, u32[]{:S(2)}) collective-permute-start(bf16[128,640]{1,0:T(8,128)(2,1)S(1)} %get-tuple-element.45.refs_0_), channel_id=1, source_target_pairs={{0,1},{1,2},{2,3},{3,4},{4,5},{5,6},{6,7},{7,0},{8,9},{9,10},{10,1... | collective-permute-start | bytes 491528 | tf_op jit(solution)/shard_map/ppermute | solution.py:414
  35.8 3.9 %collective-permute-start.4 = (bf16[128,640]{1,0:T(8,128)(2,1)S(1)}, bf16[128,640]{1,0:T(8,128)(2,1)S(1)}, u32[]{:S(2)}, u32[]{:S(2)}) collective-permute-start(bf16[128,640]{1,0:T(8,128)(2,1)S(1)} %get-tuple-element.45.refs_0_), channel_id=1, source_target_pairs={{0,7},{1,0},{2,1},{3,2},{4,3},{5,4},{6,5},{7,6},{8,15},{9,8},{10,9... | collective-permute-start | bytes 491528 | tf_op jit(solution)/shard_map/ppermute | solution.py:415
  39.9 2.7 %collective-permute-start.11 = (bf16[192,640]{1,0:T(8,128)(2,1)S(1)}, bf16[192,640]{1,0:T(8,128)(2,1)S(1)}, u32[]{:S(2)}, u32[]{:S(2)}) collective-permute-start(bf16[192,640]{1,0:T(8,128)(2,1)S(1)} %constant_dynamic-update-slice_fusion.refs_1_), channel_id=1, source_target_pairs={{0,7},{1,0},{2,1},{3,2},{4,3},{5,4},{6,5},{7,6},{8,15},{9,8},{10,9... | collective-permute-start | bytes 737288 | tf_op jit(solution)/shard_map/ppermute | solution.py:415
  43.2 2.7 %collective-permute-start.5 = (bf16[128,640]{1,0:T(8,128)(2,1)S(1)}, bf16[128,640]{1,0:T(8,128)(2,1)}, u32[]{:S(2)}, u32[]{:S(2)}) collective-permute-start(bf16[128,640]{1,0:T(8,128)(2,1)S(1)} %collective-permute-done.4.refs_2_), channel_id=1, source_target_pairs={{0,7},{1,0},{2,1},{3,2},{4,3},{5,4},{6,5},{7,6},{8,15},{9,8},{10,9... | collective-permute-start | bytes 491528 | tf_op jit(solution)/shard_map/ppermute | solution.py:415
  46.0 1.9 %shard_map.102 = (f32[320,640]{1,0:T(8,128)S(1)}, f32[320,256]{1,0:T(8,128)S(1)}) custom-call(s32[1]{0:T(128)} %bitcast.4.owners_ref, bf16[5120,640]{1,0:T(8,128)(2,1)} %w_hbm.1, bf16[5120,256]{1,0:T(8,128)(2,1)} %bitcast.26, bf16[128,640]{1,0:T(8,128)(2,1)S(1)} %get-tuple-element.45.refs_0_, bf16[192,640]{1,0:T(8,128)(2,1)S(1)} %constant_dynamic-update-slice_fusion.refs_1_), custom_call_target="tpu_custom_call" | custom-call | flops 734003200 | bytes 1146880 | tf_op jit(solution)/shard_map/pallas_call | solution.py:100
  48.6 2.7 %collective-permute-start.13 = (bf16[192,640]{1,0:T(8,128)(2,1)S(1)}, bf16[192,640]{1,0:T(8,128)(2,1)S(1)}, u32[]{:S(2)}, u32[]{:S(2)}) collective-permute-start(bf16[192,640]{1,0:T(8,128)(2,1)S(1)} %collective-permute-done.11.refs_3_), channel_id=1, source_target_pairs={{0,7},{1,0},{2,1},{3,2},{4,3},{5,4},{6,5},{7,6},{8,15},{9,8},{10,9... | collective-permute-start | bytes 737288 | tf_op jit(solution)/shard_map/ppermute | solution.py:415
  51.3 0.9 collective-permute-done.2.refs_0_
  52.2 2.7 %collective-permute-start.6 = (bf16[128,640]{1,0:T(8,128)(2,1)}, bf16[128,640]{1,0:T(8,128)(2,1)S(1)}, u32[]{:S(2)}, u32[]{:S(2)}) collective-permute-start(bf16[128,640]{1,0:T(8,128)(2,1)} %collective-permute-done.5.refs_2_), channel_id=1, source_target_pairs={{0,7},{1,0},{2,1},{3,2},{4,3},{5,4},{6,5},{7,6},{8,15},{9,8},{10,9... | collective-permute-start | bytes 491528 | tf_op jit(solution)/shard_map/ppermute | solution.py:415
  54.9 3.2 %shard_map.103 = (f32[320,640]{1,0:T(8,128)S(1)}, f32[320,256]{1,0:T(8,128)S(1)}) custom-call(s32[2]{0:T(128)S(1)} %pad_add_fusion.1.owners_ref, bf16[5120,640]{1,0:T(8,128)(2,1)} %w_hbm.1, bf16[5120,256]{1,0:T(8,128)(2,1)} %bitcast.27, bf16[128,640]{1,0:T(8,128)(2,1)S(1)} %collective-permute-done.1.refs_0_, ...), custom_call_target="tpu_custom_call" | custom-call | flops 1468006400 | bytes 2293760 | tf_op jit(solution)/shard_map/pallas_call | solution.py:100
  58.3 2.7 %collective-permute-start.15 = (bf16[192,640]{1,0:T(8,128)(2,1)S(1)}, bf16[192,640]{1,0:T(8,128)(2,1)S(1)}, u32[]{:S(2)}, u32[]{:S(2)}) collective-permute-start(bf16[192,640]{1,0:T(8,128)(2,1)S(1)} %collective-permute-done.13.refs_3_), channel_id=1, source_target_pairs={{0,7},{1,0},{2,1},{3,2},{4,3},{5,4},{6,5},{7,6},{8,15},{9,8},{10,9... | collective-permute-start | bytes 737288 | tf_op jit(solution)/shard_map/ppermute | solution.py:415
  61.7 1.5 %collective-permute-start.7 = (bf16[128,640]{1,0:T(8,128)(2,1)}, bf16[128,640]{1,0:T(8,128)(2,1)S(1)}, u32[]{:S(2)}, u32[]{:S(2)}) collective-permute-start(bf16[128,640]{1,0:T(8,128)(2,1)} %broadcast_select_fusion.1), channel_id=1, source_target_pairs={{0,1},{1,2},{2,3},{3,4},{4,5},{5,6},{6,7},{7,0},{8,15},{9,8},{10,9... | collective-permute-start | bytes 491528 | tf_op jit(solution)/shard_map/ppermute | solution.py:423
  63.2 3.7 %shard_map.104 = (f32[320,640]{1,0:T(8,128)S(1)}, f32[320,256]{1,0:T(8,128)S(1)}) custom-call(s32[2]{0:T(128)S(1)} %pad_add_fusion.2.owners_ref, bf16[5120,640]{1,0:T(8,128)(2,1)} %w_hbm.1, bf16[5120,256]{1,0:T(8,128)(2,1)} %bitcast.28, bf16[128,640]{1,0:T(8,128)(2,1)} %collective-permute-done.2.refs_0_, ...), custom_call_target="tpu_custom_call" | custom-call | flops 1468006400 | bytes 2293760 | tf_op jit(solution)/shard_map/pallas_call | solution.py:100
  67.4 3.2 %shard_map.105 = (f32[320,640]{1,0:T(8,128)S(1)}, f32[320,256]{1,0:T(8,128)S(1)}) custom-call(s32[2]{0:T(128)S(1)} %pad_add_fusion.3.owners_ref, bf16[5120,640]{1,0:T(8,128)(2,1)} %w_hbm.1, bf16[5120,256]{1,0:T(8,128)(2,1)} %bitcast.29, bf16[128,640]{1,0:T(8,128)(2,1)S(1)} %collective-permute-done.3.refs_0_, ...), custom_call_target="tpu_custom_call" | custom-call | flops 1468006400 | bytes 2293760 | tf_op jit(solution)/shard_map/pallas_call | solution.py:100
  70.7 1.4 %collective-permute-done.16.refs_1_ = bf16[192,640]{1,0:T(8,128)(2,1)S(1)} collective-permute-done((bf16[192,640]{1,0:T(8,128)(2,1)S(1)}, bf16[192,640]{1,0:T(8,128)(2,1)S(1)}, u32[]{:S(2)}, u32[]{:S(2)}) %collective-permute-start.16) | collective-permute-done | bytes 245792 | tf_op jit(solution)/shard_map/ppermute | solution.py:423
  72.1 1.4 %shard_map.106 = bf16[320,256]{1,0:T(8,128)(2,1)S(1)} custom-call(s32[1]{0:T(128)} %bitcast.2.owner_ref, bf16[5120,256]{1,0:T(8,128)(2,1)} %bitcast.30, bf16[128,640]{1,0:T(8,128)(2,1)S(1)} %collective-permute-done.7.refs_0_, bf16[192,640]{1,0:T(8,128)(2,1)S(1)} %collective-permute-done.16.refs_1_, f32[320,256]{1,0:T(8,128)S(1)} %get-tuple-element.70.refs_2_, ...), custom_call_target="tpu_custom_call" | custom-call | flops 209715200 | bytes 2000000 | tf_op jit(solution)/shard_map/pallas_call | solution.py:149
  73.5 2.4 %collective-permute-start.17 = (bf16[320,256]{1,0:T(8,128)(2,1)S(1)}, bf16[320,256]{1,0:T(8,128)(2,1)S(1)}, u32[]{:S(2)}, u32[]{:S(2)}) collective-permute-start(bf16[320,256]{1,0:T(8,128)(2,1)S(1)} %shard_map.106), channel_id=1, source_target_pairs={{0,16},{8,56},{16,0},{24,40},{32,48},{40,24},{48,32},{56,8},{64,80... | collective-permute-start | bytes 491528 | tf_op jit(solution)/shard_map/ppermute | solution.py:432
  75.9 1.8 %shard_map.107.q_ref = bf16[320,640]{1,0:T(8,128)(2,1)S(1)} custom-call(s32[1]{0:T(128)} %bitcast.2.owner_ref, bf16[5120,640]{1,0:T(8,128)(2,1)} %w_hbm.1, bf16[128,640]{1,0:T(8,128)(2,1)S(1)} %collective-permute-done.7.refs_0_, bf16[192,640]{1,0:T(8,128)(2,1)S(1)} %collective-permute-done.16.refs_1_, f32[320,640]{1,0:T(8,128)S(1)} %get-tuple-element.73.refs_2_, ...), custom_call_target="tpu_custom_call" | custom-call | flops 524288000 | bytes 2000000 | tf_op jit(solution)/shard_map/pallas_call | solution.py:149
  77.7 1.2 %collective-permute-done.17 = bf16[320,256]{1,0:T(8,128)(2,1)S(1)} collective-permute-done((bf16[320,256]{1,0:T(8,128)(2,1)S(1)}, bf16[320,256]{1,0:T(8,128)(2,1)S(1)}, u32[]{:S(2)}, u32[]{:S(2)}) %collective-permute-start.17) | collective-permute-done | bytes 163872 | tf_op jit(solution)/shard_map/ppermute | solution.py:432
  79.1 9.0 %collective-permute-start.19 = (bf16[2,320,256]{2,1,0:T(8,128)(2,1)S(1)}, bf16[2,320,256]{2,1,0:T(8,128)(2,1)S(1)}, u32[]{:S(2)}, u32[]{:S(2)}) collective-permute-start(bf16[2,320,256]{2,1,0:T(8,128)(2,1)S(1)} %pad_maximum_fusion.refs_0_), channel_id=1, source_target_pairs={{0,8},{8,0},{16,24},{24,16},{32,40},{40,32},{48,56},{56,48},{64,72... | collective-permute-start | bytes 983048 | tf_op jit(solution)/shard_map/ppermute | solution.py:437
  88.0 6.4 %collective-permute-start.20 = (bf16[2,320,256]{2,1,0:T(8,128)(2,1)S(1)}, bf16[2,320,256]{2,1,0:T(8,128)(2,1)S(1)}, u32[]{:S(2)}, u32[]{:S(2)}) collective-permute-start(bf16[2,320,256]{2,1,0:T(8,128)(2,1)S(1)} %collective-permute-done.18.refs_1_), channel_id=1, source_target_pairs={{0,8},{8,0},{16,24},{24,16},{32,40},{40,32},{48,56},{56,48},{64,72... | collective-permute-start | bytes 983048 | tf_op jit(solution)/shard_map/ppermute | solution.py:437
  94.6 1.0 collective-permute-done.20.refs_3_
  95.7 5.8 %shard_map.108 = bf16[320,640]{1,0:T(8,128)(2,1)S(1)} custom-call(s32[2]{0:T(128)S(1)} %pad_add_fusion.info_ref, bf16[320,640]{1,0:T(8,128)(2,1)S(1)} %shard_map.107.q_ref, s32[320,1]{1,0:T(8,128)S(1)} %copy.14.to_ref, bf16[2,320,256]{2,1,0:T(8,128)(2,1)S(1)} %pad_maximum_fusion.refs_0_, bf16[2,320,256]{2,1,0:T(8,128)(2,1)S(1)} %collective-permute-done.18.refs_1_, ...), custom_call_target="tpu_custom_call" | custom-call | flops 1300000000 | bytes 4000000 | tf_op jit(solution)/shard_map/pallas_call | solution.py:343
  101.6 13.8 %all_to_all.10 = bf16[32,5,2,640]{3,2,1,0:T(2,128)(2,1)S(1)} all-to-all(bf16[32,5,2,640]{3,2,1,0:T(2,128)(2,1)S(1)} %reshape.163), channel_id=1, replica_groups=mesh['ctx'=32,'mp'=8] {'ctx'}, dimensions={0} | all-to-all | bytes 819200 | tf_op jit(solution)/shard_map/all_to_all | solution.py:443
  115.5 0.8 copy.20
  (65 shorter events, 5.4 us)
Async XLA Ops:
  0.0 12.7 %copy-start = (s32[4,512]{1,0:T(4,128)S(1)}, s32[4,512]{1,0:T(4,128)}, u32[]{:S(2)}) copy-start(s32[4,512]{1,0:T(4,128)} %param.14) | copy-start | bytes 24580
  0.0 12.3 %copy-start.4 = (s32[64]{0:T(128)S(1)}, s32[64]{0:T(128)}, u32[]{:S(2)}) copy-start(s32[64]{0:T(128)} %param.15) | copy-start | bytes 772
  0.0 13.1 %copy-start.2 = (bf16[5120,2,128]{2,1,0:T(2,128)(2,1)S(1)}, bf16[5120,2,128]{2,1,0:T(2,128)(2,1)}, u32[]{:S(2)}) copy-start(bf16[5120,2,128]{2,1,0:T(2,128)(2,1)} %param.18) | copy-start | bytes 7864324
  3.5 22.8 %all-to-all-start = ((bf16[32,16,768]{2,1,0:T(8,128)(2,1)}), bf16[32,16,768]{2,1,0:T(8,128)(2,1)S(1)}, u32[]{:S(2)}, u32[]{:S(2)}) async-start(bf16[32,16,768]{2,1,0:T(8,128)(2,1)} %shard_map.100), calls=%async_computation | async-start | bytes 1572864 | tf_op jit(solution)/shard_map/all_to_all | solution.py:379
  27.3 6.8 %collective-permute-start = (bf16[64,640]{1,0:T(8,128)(2,1)S(1)}, bf16[64,640]{1,0:T(8,128)(2,1)S(1)}, u32[]{:S(2)}, u32[]{:S(2)}) collective-permute-start(bf16[64,640]{1,0:T(8,128)(2,1)S(1)} %get-tuple-element.44), channel_id=1, source_target_pairs={{0,64},{8,72},{16,80},{24,88},{32,96},{40,104},{48,112},{56,120},{... | collective-permute-start | bytes 245768 | tf_op jit(solution)/shard_map/ppermute | solution.py:404
  27.4 12.3 %collective-permute-start.8 = (bf16[64,640]{1,0:T(8,128)(2,1)S(1)}, bf16[64,640]{1,0:T(8,128)(2,1)S(1)}, u32[]{:S(2)}, u32[]{:S(2)}) collective-permute-start(bf16[64,640]{1,0:T(8,128)(2,1)S(1)} %get-tuple-element.47), channel_id=1, source_target_pairs={{0,128},{8,136},{16,144},{24,152},{32,160},{40,168},{48,176},{56,1... | collective-permute-start | bytes 245768 | tf_op jit(solution)/shard_map/ppermute | solution.py:404
  29.1 10.7 %collective-permute-start.9 = (bf16[64,640]{1,0:T(8,128)(2,1)S(1)}, bf16[64,640]{1,0:T(8,128)(2,1)S(1)}, u32[]{:S(2)}, u32[]{:S(2)}) collective-permute-start(bf16[64,640]{1,0:T(8,128)(2,1)S(1)} %get-tuple-element.48), channel_id=1, source_target_pairs={{0,192},{8,200},{16,208},{24,216},{32,224},{40,232},{48,240},{56,2... | collective-permute-start | bytes 245768 | tf_op jit(solution)/shard_map/ppermute | solution.py:404
  34.2 9.0 %collective-permute-start.1 = (bf16[128,640]{1,0:T(8,128)(2,1)S(1)}, bf16[128,640]{1,0:T(8,128)(2,1)S(1)}, u32[]{:S(2)}, u32[]{:S(2)}) collective-permute-start(bf16[128,640]{1,0:T(8,128)(2,1)S(1)} %get-tuple-element.45.refs_0_), channel_id=1, source_target_pairs={{0,1},{1,2},{2,3},{3,4},{4,5},{5,6},{6,7},{7,0},{8,9},{9,10},{10,1... | collective-permute-start | bytes 491528 | tf_op jit(solution)/shard_map/ppermute | solution.py:414
  35.8 7.4 %collective-permute-start.4 = (bf16[128,640]{1,0:T(8,128)(2,1)S(1)}, bf16[128,640]{1,0:T(8,128)(2,1)S(1)}, u32[]{:S(2)}, u32[]{:S(2)}) collective-permute-start(bf16[128,640]{1,0:T(8,128)(2,1)S(1)} %get-tuple-element.45.refs_0_), channel_id=1, source_target_pairs={{0,7},{1,0},{2,1},{3,2},{4,3},{5,4},{6,5},{7,6},{8,15},{9,8},{10,9... | collective-permute-start | bytes 491528 | tf_op jit(solution)/shard_map/ppermute | solution.py:415
  39.8 8.8 %collective-permute-start.10 = (bf16[192,640]{1,0:T(8,128)(2,1)S(1)}, bf16[192,640]{1,0:T(8,128)(2,1)S(1)}, u32[]{:S(2)}, u32[]{:S(2)}) collective-permute-start(bf16[192,640]{1,0:T(8,128)(2,1)S(1)} %constant_dynamic-update-slice_fusion.refs_1_), channel_id=1, source_target_pairs={{0,1},{1,2},{2,3},{3,4},{4,5},{5,6},{6,7},{7,0},{8,9},{9,10},{10,1... | collective-permute-start | bytes 737288 | tf_op jit(solution)/shard_map/ppermute | solution.py:414
  39.9 8.7 %collective-permute-start.11 = (bf16[192,640]{1,0:T(8,128)(2,1)S(1)}, bf16[192,640]{1,0:T(8,128)(2,1)S(1)}, u32[]{:S(2)}, u32[]{:S(2)}) collective-permute-start(bf16[192,640]{1,0:T(8,128)(2,1)S(1)} %constant_dynamic-update-slice_fusion.refs_1_), channel_id=1, source_target_pairs={{0,7},{1,0},{2,1},{3,2},{4,3},{5,4},{6,5},{7,6},{8,15},{9,8},{10,9... | collective-permute-start | bytes 737288 | tf_op jit(solution)/shard_map/ppermute | solution.py:415
  43.2 9.0 %collective-permute-start.2 = (bf16[128,640]{1,0:T(8,128)(2,1)S(1)}, bf16[128,640]{1,0:T(8,128)(2,1)}, u32[]{:S(2)}, u32[]{:S(2)}) collective-permute-start(bf16[128,640]{1,0:T(8,128)(2,1)S(1)} %collective-permute-done.1.refs_0_), channel_id=1, source_target_pairs={{0,1},{1,2},{2,3},{3,4},{4,5},{5,6},{6,7},{7,0},{8,9},{9,10},{10,1... | collective-permute-start | bytes 491528 | tf_op jit(solution)/shard_map/ppermute | solution.py:414
  43.2 9.0 %collective-permute-start.5 = (bf16[128,640]{1,0:T(8,128)(2,1)S(1)}, bf16[128,640]{1,0:T(8,128)(2,1)}, u32[]{:S(2)}, u32[]{:S(2)}) collective-permute-start(bf16[128,640]{1,0:T(8,128)(2,1)S(1)} %collective-permute-done.4.refs_2_), channel_id=1, source_target_pairs={{0,7},{1,0},{2,1},{3,2},{4,3},{5,4},{6,5},{7,6},{8,15},{9,8},{10,9... | collective-permute-start | bytes 491528 | tf_op jit(solution)/shard_map/ppermute | solution.py:415
  48.6 9.6 %collective-permute-start.12 = (bf16[192,640]{1,0:T(8,128)(2,1)S(1)}, bf16[192,640]{1,0:T(8,128)(2,1)S(1)}, u32[]{:S(2)}, u32[]{:S(2)}) collective-permute-start(bf16[192,640]{1,0:T(8,128)(2,1)S(1)} %collective-permute-done.10.refs_1_), channel_id=1, source_target_pairs={{0,1},{1,2},{2,3},{3,4},{4,5},{5,6},{6,7},{7,0},{8,9},{9,10},{10,1... | collective-permute-start | bytes 737288 | tf_op jit(solution)/shard_map/ppermute | solution.py:414
  48.6 9.6 %collective-permute-start.13 = (bf16[192,640]{1,0:T(8,128)(2,1)S(1)}, bf16[192,640]{1,0:T(8,128)(2,1)S(1)}, u32[]{:S(2)}, u32[]{:S(2)}) collective-permute-start(bf16[192,640]{1,0:T(8,128)(2,1)S(1)} %collective-permute-done.11.refs_3_), channel_id=1, source_target_pairs={{0,7},{1,0},{2,1},{3,2},{4,3},{5,4},{6,5},{7,6},{8,15},{9,8},{10,9... | collective-permute-start | bytes 737288 | tf_op jit(solution)/shard_map/ppermute | solution.py:415
  52.2 8.8 %collective-permute-start.3 = (bf16[128,640]{1,0:T(8,128)(2,1)}, bf16[128,640]{1,0:T(8,128)(2,1)S(1)}, u32[]{:S(2)}, u32[]{:S(2)}) collective-permute-start(bf16[128,640]{1,0:T(8,128)(2,1)} %collective-permute-done.2.refs_0_), channel_id=1, source_target_pairs={{0,1},{1,2},{2,3},{3,4},{4,5},{5,6},{6,7},{7,0},{8,9},{9,10},{10,1... | collective-permute-start | bytes 491528 | tf_op jit(solution)/shard_map/ppermute | solution.py:414
  52.2 8.8 %collective-permute-start.6 = (bf16[128,640]{1,0:T(8,128)(2,1)}, bf16[128,640]{1,0:T(8,128)(2,1)S(1)}, u32[]{:S(2)}, u32[]{:S(2)}) collective-permute-start(bf16[128,640]{1,0:T(8,128)(2,1)} %collective-permute-done.5.refs_2_), channel_id=1, source_target_pairs={{0,7},{1,0},{2,1},{3,2},{4,3},{5,4},{6,5},{7,6},{8,15},{9,8},{10,9... | collective-permute-start | bytes 491528 | tf_op jit(solution)/shard_map/ppermute | solution.py:415
  58.2 8.7 %collective-permute-start.14 = (bf16[192,640]{1,0:T(8,128)(2,1)S(1)}, bf16[192,640]{1,0:T(8,128)(2,1)S(1)}, u32[]{:S(2)}, u32[]{:S(2)}) collective-permute-start(bf16[192,640]{1,0:T(8,128)(2,1)S(1)} %collective-permute-done.12.refs_1_), channel_id=1, source_target_pairs={{0,1},{1,2},{2,3},{3,4},{4,5},{5,6},{6,7},{7,0},{8,9},{9,10},{10,1... | collective-permute-start | bytes 737288 | tf_op jit(solution)/shard_map/ppermute | solution.py:414
  58.3 8.6 %collective-permute-start.15 = (bf16[192,640]{1,0:T(8,128)(2,1)S(1)}, bf16[192,640]{1,0:T(8,128)(2,1)S(1)}, u32[]{:S(2)}, u32[]{:S(2)}) collective-permute-start(bf16[192,640]{1,0:T(8,128)(2,1)S(1)} %collective-permute-done.13.refs_3_), channel_id=1, source_target_pairs={{0,7},{1,0},{2,1},{3,2},{4,3},{5,4},{6,5},{7,6},{8,15},{9,8},{10,9... | collective-permute-start | bytes 737288 | tf_op jit(solution)/shard_map/ppermute | solution.py:415
  61.7 10.4 %collective-permute-start.7 = (bf16[128,640]{1,0:T(8,128)(2,1)}, bf16[128,640]{1,0:T(8,128)(2,1)S(1)}, u32[]{:S(2)}, u32[]{:S(2)}) collective-permute-start(bf16[128,640]{1,0:T(8,128)(2,1)} %broadcast_select_fusion.1), channel_id=1, source_target_pairs={{0,1},{1,2},{2,3},{3,4},{4,5},{5,6},{6,7},{7,0},{8,15},{9,8},{10,9... | collective-permute-start | bytes 491528 | tf_op jit(solution)/shard_map/ppermute | solution.py:423
  67.0 5.1 %collective-permute-start.16 = (bf16[192,640]{1,0:T(8,128)(2,1)S(1)}, bf16[192,640]{1,0:T(8,128)(2,1)S(1)}, u32[]{:S(2)}, u32[]{:S(2)}) collective-permute-start(bf16[192,640]{1,0:T(8,128)(2,1)S(1)} %broadcast_select_fusion), channel_id=1, source_target_pairs={{0,1},{1,2},{2,3},{3,4},{4,5},{5,6},{6,7},{7,0},{8,15},{9,8},{10,9... | collective-permute-start | bytes 737288 | tf_op jit(solution)/shard_map/ppermute | solution.py:423
  67.4 4.7 %copy-start.1 = (bf16[128]{0:T(256)(128)(2,1)S(1)}, bf16[128]{0:T(256)(128)(2,1)}, u32[]{:S(2)}) copy-start(bf16[128]{0:T(256)(128)(2,1)} %param.19) | copy-start | bytes 772
  70.7 5.2 %copy-start.3 = (bf16[640]{0:T(1024)(128)(2,1)S(1)}, bf16[640]{0:T(1024)(128)(2,1)}, u32[]{:S(2)}) copy-start(bf16[640]{0:T(1024)(128)(2,1)} %param.17) | copy-start | bytes 3844
  73.5 5.5 %collective-permute-start.17 = (bf16[320,256]{1,0:T(8,128)(2,1)S(1)}, bf16[320,256]{1,0:T(8,128)(2,1)S(1)}, u32[]{:S(2)}, u32[]{:S(2)}) collective-permute-start(bf16[320,256]{1,0:T(8,128)(2,1)S(1)} %shard_map.106), channel_id=1, source_target_pairs={{0,16},{8,56},{16,0},{24,40},{32,48},{40,24},{48,32},{56,8},{64,80... | collective-permute-start | bytes 491528 | tf_op jit(solution)/shard_map/ppermute | solution.py:432
  79.0 9.1 %collective-permute-start.18 = (bf16[2,320,256]{2,1,0:T(8,128)(2,1)S(1)}, bf16[2,320,256]{2,1,0:T(8,128)(2,1)S(1)}, u32[]{:S(2)}, u32[]{:S(2)}) collective-permute-start(bf16[2,320,256]{2,1,0:T(8,128)(2,1)S(1)} %pad_maximum_fusion.refs_0_), channel_id=1, source_target_pairs={{0,48},{8,24},{16,32},{24,8},{32,16},{40,56},{48,0},{56,40},{64,11... | collective-permute-start | bytes 983048 | tf_op jit(solution)/shard_map/ppermute | solution.py:435
  79.1 15.6 %collective-permute-start.19 = (bf16[2,320,256]{2,1,0:T(8,128)(2,1)S(1)}, bf16[2,320,256]{2,1,0:T(8,128)(2,1)S(1)}, u32[]{:S(2)}, u32[]{:S(2)}) collective-permute-start(bf16[2,320,256]{2,1,0:T(8,128)(2,1)S(1)} %pad_maximum_fusion.refs_0_), channel_id=1, source_target_pairs={{0,8},{8,0},{16,24},{24,16},{32,40},{40,32},{48,56},{56,48},{64,72... | collective-permute-start | bytes 983048 | tf_op jit(solution)/shard_map/ppermute | solution.py:437
  88.0 7.6 %collective-permute-start.20 = (bf16[2,320,256]{2,1,0:T(8,128)(2,1)S(1)}, bf16[2,320,256]{2,1,0:T(8,128)(2,1)S(1)}, u32[]{:S(2)}, u32[]{:S(2)}) collective-permute-start(bf16[2,320,256]{2,1,0:T(8,128)(2,1)S(1)} %collective-permute-done.18.refs_1_), channel_id=1, source_target_pairs={{0,8},{8,0},{16,24},{24,16},{32,40},{40,32},{48,56},{56,48},{64,72... | collective-permute-start | bytes 983048 | tf_op jit(solution)/shard_map/ppermute | solution.py:437

commit v5 on v4

--- a/solution.py
+++ b/solution.py
@@ -40,10 +40,6 @@
         y, x, c = move(i // MEMBERS, (i // 2) % 4, i % 2)
         pairs.append((i, (y % 4) * MEMBERS + (x % 4) * 2 + c))
     return pairs
-
-
-def across(first):
-    return ctx_pairs(lambda y, x, c: (y, x ^ (1 if (c == 0) == first else 3), c))
 
 
 def far_pairs():
@@ -270,17 +266,15 @@
     lane = lax.broadcasted_iota(jnp.int32, (STEP, keys_step), 1)
     row = lax.broadcasted_iota(jnp.int32, (STEP, keys_step), 0)
     slot = lane // STEP
-    core = (my_core + slot // 4) % 2
-    by_near, by_far = jnp.where(core == 0, 1, 3), jnp.where(core == 0, 3, 1)
-    x = my_x ^ jnp.where(slot % 2 == 1, by_near, 0) ^ jnp.where((slot // 2) % 2 == 1, by_far, 0)
-    k_mem = 2 * x + core
+    pair = slot // 2
+    off = jnp.where(pair == 0, 0, jnp.where(pair == 1, 3, pair - 1))
+    k_mem = 2 * ((my_x + off) % 4) + (my_core + slot) % 2
 
     def gather(part, at):
         return jnp.concatenate(
             [
-                ref[piece, pl.ds(first, n), at : at + HEAD]
+                ref[pl.ds(first, n), at : at + HEAD]
                 for ref in key_refs
-                for piece in range(2)
                 for first, n in spans(part)
             ],
             axis=0,
@@ -404,7 +398,7 @@
         lax.ppermute(out, "ctx", ctx_pairs(lambda y, x, c, dy=dy: (y + dy, x, c)))
         for dy, out in enumerate(others, 1)
     ]
-    first, arrived[0] = lax.optimization_barrier((first, arrived[0]))
+    first, arrived[1] = lax.optimization_barrier((first, arrived[1]))
     own = [first, jnp.concatenate(arrived, 0)]
 
     fwd, bwd = list(own), list(own)
@@ -429,12 +423,17 @@
     kv = finish(True, sums[1], far, opposite, kv_flat, cosine, sine, value_offset_bias)
     q = finish(False, sums[0], far, opposite, w_query, cosine, sine, b_query)
 
-    beside = lax.ppermute(kv, "ctx", across(True))
-    beside, q = lax.optimization_barrier((beside, q))
-    near = jnp.stack([kv, beside])
-    off = lax.ppermute(near, "ctx", across(False))
+    below = lax.ppermute(kv, "ctx", ctx_pairs(lambda y, x, c: (y, x + 1, c)))
+    above = lax.ppermute(kv, "ctx", ctx_pairs(lambda y, x, c: (y, x - 1, c)))
+    above, q = lax.optimization_barrier((above, q))
+    beyond = lax.ppermute(
+        jnp.where(core == 0, above, below), "ctx",
+        ctx_pairs(lambda y, x, c: (y, x + (-1 if c == 0 else 1), c)),
+    )
     swap = ctx_pairs(lambda y, x, c: (y, x, 1 - c))
-    pieces = [near, off, lax.ppermute(near, "ctx", swap), lax.ppermute(off, "ctx", swap)]
+    pieces = []
+    for piece in (kv, below, above, beyond):
+        pieces += [piece, lax.ppermute(piece, "ctx", swap)]
 
     info = jnp.stack([group, member]).astype(jnp.int32)
     out = attend(info, q, send_from, pieces, heads, cands)

time: 117 us -> 116 us (level)
    ppermute x3, waiting for transfers between devices: 3.44 us -> 0.87 us  [per_device(): lax.ppermute(out, 'ctx', ctx_pairs(lambda y, x, c, dy=dy: (y + dy, x, c)))]
    ppermute x4 -> x7, waiting for transfers between devices: 2.27 us -> 4.36 us  [the longest x1 3.12 us: per_device(): below = lax.ppermute(kv, 'ctx', ctx_pairs(lambda y, x, c: (y, x + 1, c)))]
    ppermute x4 -> x7, starting transfers between devices: 17.9 us -> 15.8 us  [the longest x4 13.2 us: per_device(): pieces += [piece, lax.ppermute(piece, 'ctx', swap)]]
  transfers between devices with their start and end apart: 22 -> 25, of which waited for: 8 -> 8; matrix products, arithmetic and copies ran while one was open for 4% -> 4% of each run, Pallas kernels for 12% -> 12%
where the time goes in v5:
time: 116 us; the launch traced here: 115 us
  starting transfers between devices  50 us (43%)
  Pallas kernels  25.5 us (22%)
  waiting for transfers between devices  19.1 us (16%)
  blocking collectives  14.1 us (12%)
  local copies, waits for them, and re-layouts  3.93 us (3%)
  other arithmetic  1.96 us (2%)
    ppermute x6, starting transfers between devices, per_device(): bwd[h] = lax.ppermute(bwd[h], 'mp', shifted(PLANES, -1))  17.4 us
    all_to_all x1, blocking collectives, per_device(): recv = lax.all_to_all(send, 'ctx', 0, 0, tiled=True)  14.1 us
    ppermute x4, starting transfers between devices, per_device(): pieces += [piece, lax.ppermute(piece, 'ctx', swap)]  13.2 us
    pallas_call x4, Pallas kernels, add_products(): pl.pallas_call(functools.partial(products_kernel, groups, halves, sums is...  12.1 us
    all_to_all x1, waiting for transfers between devices, per_device(): sent = lax.all_to_all(sent, 'ctx', 0, 0, tiled=True)  10.3 us
    all_to_all x1, starting transfers between devices, per_device(): sent = lax.all_to_all(sent, 'ctx', 0, 0, tiled=True)  8.6 us
    pallas_call x1, Pallas kernels, attend(): pl.pallas_call(functools.partial(attend_kernel, heads, clips), out_shape=...  5.8 us
    ppermute x3, starting transfers between devices, per_device(): lax.ppermute(out, 'ctx', ctx_pairs(lambda y, x, c, dy=dy: (y + dy, x, c)))  4.01 us
  transfers between devices with their start and end apart: 25, of which 8 were waited for; matrix products, arithmetic and copies ran while one was open for 4% of the time, Pallas kernels for 12%

profile of v5, /device:TPU:1, one launch (start us, length us, event | category | flops | bytes accessed | tf_op | source)
XLA Modules:
  0.0 115.1 jit_solution(15324475650301907790)
XLA Ops:
  0.0 3.5 %shard_map.100 = bf16[32,16,768]{2,1,0:T(8,128)(2,1)} custom-call(s32[4,4]{1,0:T(4,128)} %cand_ref.3, s32[64]{0:T(128)} %slot_ref.3, s32[1]{0:T(128)} %bitcast.3.me_ref, bf16[2,512,640]{2,1,0:T(8,128)(2,1)} %clip_hbm.1, bf16[4,16,640]{2,1,0:T(8,128)(2,1)} %text_ref.1), custom_call_target="tpu_custom_call" | custom-call | tf_op jit(solution)/shard_map/pallas_call | solution.py:204
  3.5 8.6 %all-to-all-start = ((bf16[32,16,768]{2,1,0:T(8,128)(2,1)}), bf16[32,16,768]{2,1,0:T(8,128)(2,1)S(1)}, u32[]{:S(2)}, u32[]{:S(2)}) async-start(bf16[32,16,768]{2,1,0:T(8,128)(2,1)} %shard_map.100), calls=%async_computation | async-start | bytes 1572864 | tf_op jit(solution)/shard_map/all_to_all | solution.py:373
  13.1 1.9 %copy.19 = bf16[640,8,2,128]{3,1,2,0:T(8,128)(2,1)} copy(bf16[640,8,2,128]{3,2,1,0:T(2,128)(2,1)S(1)} %bitcast.28) | data formatting | bytes 5242880
  16.0 10.3 %all-to-all-done.sent_ref = bf16[32,16,768]{2,1,0:T(8,128)(2,1)S(1)} async-done(((bf16[32,16,768]{2,1,0:T(8,128)(2,1)}), bf16[32,16,768]{2,1,0:T(8,128)(2,1)S(1)}, u32[]{:S(2)}, u32[]{:S(2)}) %all-to-all-start) | async-done | bytes 786464 | tf_op jit(solution)/shard_map/all_to_all | solution.py:373
  26.3 1.0 shard_map.101
  27.3 1.3 %collective-permute-start = (bf16[64,640]{1,0:T(8,128)(2,1)S(1)}, bf16[64,640]{1,0:T(8,128)(2,1)S(1)}, u32[]{:S(2)}, u32[]{:S(2)}) collective-permute-start(bf16[64,640]{1,0:T(8,128)(2,1)S(1)} %get-tuple-element.44), channel_id=1, source_target_pairs={{0,128},{8,136},{16,144},{24,152},{32,160},{40,168},{48,176},{56,1... | collective-permute-start | bytes 245768 | tf_op jit(solution)/shard_map/ppermute | solution.py:398
  28.6 2.7 %collective-permute-start.9 = (bf16[64,640]{1,0:T(8,128)(2,1)S(1)}, bf16[64,640]{1,0:T(8,128)(2,1)S(1)}, u32[]{:S(2)}, u32[]{:S(2)}) collective-permute-start(bf16[64,640]{1,0:T(8,128)(2,1)S(1)} %get-tuple-element.48), channel_id=1, source_target_pairs={{0,192},{8,200},{16,208},{24,216},{32,224},{40,232},{48,240},{56,2... | collective-permute-start | bytes 245768 | tf_op jit(solution)/shard_map/ppermute | solution.py:398
  31.3 0.9 collective-permute-done
  32.2 1.6 %collective-permute-start.1 = (bf16[128,640]{1,0:T(8,128)(2,1)S(1)}, bf16[128,640]{1,0:T(8,128)(2,1)S(1)}, u32[]{:S(2)}, u32[]{:S(2)}) collective-permute-start(bf16[128,640]{1,0:T(8,128)(2,1)S(1)} %get-tuple-element.45.refs_0_), channel_id=1, source_target_pairs={{0,1},{1,2},{2,3},{3,4},{4,5},{5,6},{6,7},{7,0},{8,9},{9,10},{10,1... | collective-permute-start | bytes 491528 | tf_op jit(solution)/shard_map/ppermute | solution.py:408
  33.8 3.9 %collective-permute-start.4 = (bf16[128,640]{1,0:T(8,128)(2,1)S(1)}, bf16[128,640]{1,0:T(8,128)(2,1)S(1)}, u32[]{:S(2)}, u32[]{:S(2)}) collective-permute-start(bf16[128,640]{1,0:T(8,128)(2,1)S(1)} %get-tuple-element.45.refs_0_), channel_id=1, source_target_pairs={{0,7},{1,0},{2,1},{3,2},{4,3},{5,4},{6,5},{7,6},{8,15},{9,8},{10,9... | collective-permute-start | bytes 491528 | tf_op jit(solution)/shard_map/ppermute | solution.py:409
  37.9 2.8 %collective-permute-start.11 = (bf16[192,640]{1,0:T(8,128)(2,1)S(1)}, bf16[192,640]{1,0:T(8,128)(2,1)S(1)}, u32[]{:S(2)}, u32[]{:S(2)}) collective-permute-start(bf16[192,640]{1,0:T(8,128)(2,1)S(1)} %constant_dynamic-update-slice_fusion.refs_1_), channel_id=1, source_target_pairs={{0,7},{1,0},{2,1},{3,2},{4,3},{5,4},{6,5},{7,6},{8,15},{9,8},{10,9... | collective-permute-start | bytes 737288 | tf_op jit(solution)/shard_map/ppermute | solution.py:409
  40.7 2.7 %collective-permute-start.5 = (bf16[128,640]{1,0:T(8,128)(2,1)S(1)}, bf16[128,640]{1,0:T(8,128)(2,1)}, u32[]{:S(2)}, u32[]{:S(2)}) collective-permute-start(bf16[128,640]{1,0:T(8,128)(2,1)S(1)} %collective-permute-done.4.refs_2_), channel_id=1, source_target_pairs={{0,7},{1,0},{2,1},{3,2},{4,3},{5,4},{6,5},{7,6},{8,15},{9,8},{10,9... | collective-permute-start | bytes 491528 | tf_op jit(solution)/shard_map/ppermute | solution.py:409
  43.5 1.9 %shard_map.102 = (f32[320,640]{1,0:T(8,128)S(1)}, f32[320,256]{1,0:T(8,128)S(1)}) custom-call(s32[1]{0:T(128)} %bitcast.4.owners_ref, bf16[5120,640]{1,0:T(8,128)(2,1)} %w_hbm.1, bf16[5120,256]{1,0:T(8,128)(2,1)} %bitcast.23, bf16[128,640]{1,0:T(8,128)(2,1)S(1)} %get-tuple-element.45.refs_0_, bf16[192,640]{1,0:T(8,128)(2,1)S(1)} %constant_dynamic-update-slice_fusion.refs_1_), custom_call_target="tpu_custom_call" | custom-call | flops 734003200 | bytes 1146880 | tf_op jit(solution)/shard_map/pallas_call | solution.py:96
  45.4 1.8 %collective-permute-done.10.refs_1_ = bf16[192,640]{1,0:T(8,128)(2,1)S(1)} collective-permute-done((bf16[192,640]{1,0:T(8,128)(2,1)S(1)}, bf16[192,640]{1,0:T(8,128)(2,1)S(1)}, u32[]{:S(2)}, u32[]{:S(2)}) %collective-permute-start.10) | collective-permute-done | bytes 245792 | tf_op jit(solution)/shard_map/ppermute | solution.py:408
  47.1 2.7 %collective-permute-start.13 = (bf16[192,640]{1,0:T(8,128)(2,1)S(1)}, bf16[192,640]{1,0:T(8,128)(2,1)S(1)}, u32[]{:S(2)}, u32[]{:S(2)}) collective-permute-start(bf16[192,640]{1,0:T(8,128)(2,1)S(1)} %collective-permute-done.11.refs_3_), channel_id=1, source_target_pairs={{0,7},{1,0},{2,1},{3,2},{4,3},{5,4},{6,5},{7,6},{8,15},{9,8},{10,9... | collective-permute-start | bytes 737288 | tf_op jit(solution)/shard_map/ppermute | solution.py:409
  49.8 0.9 collective-permute-done.2.refs_0_
  50.8 2.7 %collective-permute-start.6 = (bf16[128,640]{1,0:T(8,128)(2,1)}, bf16[128,640]{1,0:T(8,128)(2,1)S(1)}, u32[]{:S(2)}, u32[]{:S(2)}) collective-permute-start(bf16[128,640]{1,0:T(8,128)(2,1)} %collective-permute-done.5.refs_2_), channel_id=1, source_target_pairs={{0,7},{1,0},{2,1},{3,2},{4,3},{5,4},{6,5},{7,6},{8,15},{9,8},{10,9... | collective-permute-start | bytes 491528 | tf_op jit(solution)/shard_map/ppermute | solution.py:409
  53.5 3.2 %shard_map.103 = (f32[320,640]{1,0:T(8,128)S(1)}, f32[320,256]{1,0:T(8,128)S(1)}) custom-call(s32[2]{0:T(128)S(1)} %pad_add_fusion.1.owners_ref, bf16[5120,640]{1,0:T(8,128)(2,1)} %w_hbm.1, bf16[5120,256]{1,0:T(8,128)(2,1)} %bitcast.24, bf16[128,640]{1,0:T(8,128)(2,1)S(1)} %collective-permute-done.1.refs_0_, ...), custom_call_target="tpu_custom_call" | custom-call | flops 1468006400 | bytes 2293760 | tf_op jit(solution)/shard_map/pallas_call | solution.py:96
  56.9 2.7 %collective-permute-start.15 = (bf16[192,640]{1,0:T(8,128)(2,1)S(1)}, bf16[192,640]{1,0:T(8,128)(2,1)S(1)}, u32[]{:S(2)}, u32[]{:S(2)}) collective-permute-start(bf16[192,640]{1,0:T(8,128)(2,1)S(1)} %collective-permute-done.13.refs_3_), channel_id=1, source_target_pairs={{0,7},{1,0},{2,1},{3,2},{4,3},{5,4},{6,5},{7,6},{8,15},{9,8},{10,9... | collective-permute-start | bytes 737288 | tf_op jit(solution)/shard_map/ppermute | solution.py:409
  60.2 1.2 %collective-permute-start.7 = (bf16[128,640]{1,0:T(8,128)(2,1)}, bf16[128,640]{1,0:T(8,128)(2,1)S(1)}, u32[]{:S(2)}, u32[]{:S(2)}) collective-permute-start(bf16[128,640]{1,0:T(8,128)(2,1)} %broadcast_select_fusion.2), channel_id=1, source_target_pairs={{0,1},{1,2},{2,3},{3,4},{4,5},{5,6},{6,7},{7,0},{8,15},{9,8},{10,9... | collective-permute-start | bytes 491528 | tf_op jit(solution)/shard_map/ppermute | solution.py:417
  61.4 3.7 %shard_map.104 = (f32[320,640]{1,0:T(8,128)S(1)}, f32[320,256]{1,0:T(8,128)S(1)}) custom-call(s32[2]{0:T(128)S(1)} %pad_add_fusion.2.owners_ref, bf16[5120,640]{1,0:T(8,128)(2,1)} %w_hbm.1, bf16[5120,256]{1,0:T(8,128)(2,1)} %bitcast.25, bf16[128,640]{1,0:T(8,128)(2,1)} %collective-permute-done.2.refs_0_, ...), custom_call_target="tpu_custom_call" | custom-call | flops 1468006400 | bytes 2293760 | tf_op jit(solution)/shard_map/pallas_call | solution.py:96
  65.2 1.2 %collective-permute-start.16 = (bf16[192,640]{1,0:T(8,128)(2,1)S(1)}, bf16[192,640]{1,0:T(8,128)(2,1)S(1)}, u32[]{:S(2)}, u32[]{:S(2)}) collective-permute-start(bf16[192,640]{1,0:T(8,128)(2,1)S(1)} %broadcast_select_fusion), channel_id=1, source_target_pairs={{0,1},{1,2},{2,3},{3,4},{4,5},{5,6},{6,7},{7,0},{8,15},{9,8},{10,9... | collective-permute-start | bytes 737288 | tf_op jit(solution)/shard_map/ppermute | solution.py:417
  66.5 3.2 %shard_map.105 = (f32[320,640]{1,0:T(8,128)S(1)}, f32[320,256]{1,0:T(8,128)S(1)}) custom-call(s32[2]{0:T(128)S(1)} %pad_add_fusion.3.owners_ref, bf16[5120,640]{1,0:T(8,128)(2,1)} %w_hbm.1, bf16[5120,256]{1,0:T(8,128)(2,1)} %bitcast.26, bf16[128,640]{1,0:T(8,128)(2,1)S(1)} %collective-permute-done.3.refs_0_, ...), custom_call_target="tpu_custom_call" | custom-call | flops 1468006400 | bytes 2293760 | tf_op jit(solution)/shard_map/pallas_call | solution.py:96
  69.7 0.9 collective-permute-done.16.refs_1_
  70.6 1.4 %shard_map.106.refs_0_ = bf16[320,256]{1,0:T(8,128)(2,1)S(1)} custom-call(s32[1]{0:T(128)} %bitcast.2.owner_ref, bf16[5120,256]{1,0:T(8,128)(2,1)} %bitcast.27, bf16[128,640]{1,0:T(8,128)(2,1)S(1)} %collective-permute-done.7.refs_0_, bf16[192,640]{1,0:T(8,128)(2,1)S(1)} %collective-permute-done.16.refs_1_, f32[320,256]{1,0:T(8,128)S(1)} %get-tuple-element.70.refs_2_, ...), custom_call_target="tpu_custom_call" | custom-call | flops 209715200 | bytes 2000000 | tf_op jit(solution)/shard_map/pallas_call | solution.py:145
  72.0 2.5 %collective-permute-start.17 = (bf16[320,256]{1,0:T(8,128)(2,1)S(1)}, bf16[320,256]{1,0:T(8,128)(2,1)S(1)}, u32[]{:S(2)}, u32[]{:S(2)}) collective-permute-start(bf16[320,256]{1,0:T(8,128)(2,1)S(1)} %shard_map.106.refs_0_), channel_id=1, source_target_pairs={{0,48},{8,56},{16,0},{24,8},{32,16},{40,24},{48,32},{56,40},{64,11... | collective-permute-start | bytes 491528 | tf_op jit(solution)/shard_map/ppermute | solution.py:427
  74.5 1.8 %shard_map.107.q_ref = bf16[320,640]{1,0:T(8,128)(2,1)S(1)} custom-call(s32[1]{0:T(128)} %bitcast.2.owner_ref, bf16[5120,640]{1,0:T(8,128)(2,1)} %w_hbm.1, bf16[128,640]{1,0:T(8,128)(2,1)S(1)} %collective-permute-done.7.refs_0_, bf16[192,640]{1,0:T(8,128)(2,1)S(1)} %collective-permute-done.16.refs_1_, f32[320,640]{1,0:T(8,128)S(1)} %get-tuple-element.73.refs_2_, ...), custom_call_target="tpu_custom_call" | custom-call | flops 524288000 | bytes 2000000 | tf_op jit(solution)/shard_map/pallas_call | solution.py:145
  76.7 3.1 %collective-permute-done.19.refs_2_ = bf16[320,256]{1,0:T(8,128)(2,1)S(1)} collective-permute-done((bf16[320,256]{1,0:T(8,128)(2,1)S(1)}, bf16[320,256]{1,0:T(8,128)(2,1)S(1)}, u32[]{:S(2)}, u32[]{:S(2)}) %collective-permute-start.19) | collective-permute-done | bytes 163872 | tf_op jit(solution)/shard_map/ppermute | solution.py:426
  79.9 8.0 %collective-permute-start.18 = (bf16[320,256]{1,0:T(8,128)(2,1)S(1)}, bf16[320,256]{1,0:T(8,128)(2,1)S(1)}, u32[]{:S(2)}, u32[]{:S(2)}) collective-permute-start(bf16[320,256]{1,0:T(8,128)(2,1)S(1)} %shard_map.106.refs_0_), channel_id=1, source_target_pairs={{0,8},{8,0},{16,24},{24,16},{32,40},{40,32},{48,56},{56,48},{64,72... | collective-permute-start | bytes 491528 | tf_op jit(solution)/shard_map/ppermute | solution.py:436
  88.5 4.7 %collective-permute-start.23 = (bf16[320,256]{1,0:T(8,128)(2,1)S(1)}, bf16[320,256]{1,0:T(8,128)(2,1)S(1)}, u32[]{:S(2)}, u32[]{:S(2)}) collective-permute-start(bf16[320,256]{1,0:T(8,128)(2,1)S(1)} %collective-permute-done.22.refs_6_), channel_id=1, source_target_pairs={{0,8},{8,0},{16,24},{24,16},{32,40},{40,32},{48,56},{56,48},{64,72... | collective-permute-start | bytes 491528 | tf_op jit(solution)/shard_map/ppermute | solution.py:436
  94.2 5.8 %shard_map.108 = bf16[320,640]{1,0:T(8,128)(2,1)S(1)} custom-call(s32[2]{0:T(128)S(1)} %pad_add_fusion.info_ref, bf16[320,640]{1,0:T(8,128)(2,1)S(1)} %shard_map.107.q_ref, s32[320,1]{1,0:T(8,128)S(1)} %copy.14.to_ref, bf16[320,256]{1,0:T(8,128)(2,1)S(1)} %shard_map.106.refs_0_, bf16[320,256]{1,0:T(8,128)(2,1)S(1)} %collective-permute-done.18.refs_1_, ...), custom_call_target="tpu_custom_call" | custom-call | flops 1300000000 | bytes 4000000 | tf_op jit(solution)/shard_map/pallas_call | solution.py:337
  100.2 14.1 %all_to_all.10 = bf16[32,5,2,640]{3,2,1,0:T(2,128)(2,1)S(1)} all-to-all(bf16[32,5,2,640]{3,2,1,0:T(2,128)(2,1)S(1)} %reshape.163), channel_id=1, replica_groups=mesh['ctx'=32,'mp'=8] {'ctx'}, dimensions={0} | all-to-all | bytes 819200 | tf_op jit(solution)/shard_map/all_to_all | solution.py:442
  (71 shorter events, 6.1 us)
Async XLA Ops:
  0.0 12.7 %copy-start = (s32[4,512]{1,0:T(4,128)S(1)}, s32[4,512]{1,0:T(4,128)}, u32[]{:S(2)}) copy-start(s32[4,512]{1,0:T(4,128)} %param.14) | copy-start | bytes 24580
  0.0 12.3 %copy-start.4 = (s32[64]{0:T(128)S(1)}, s32[64]{0:T(128)}, u32[]{:S(2)}) copy-start(s32[64]{0:T(128)} %param.15) | copy-start | bytes 772
  0.0 13.0 %copy-start.2 = (bf16[5120,2,128]{2,1,0:T(2,128)(2,1)S(1)}, bf16[5120,2,128]{2,1,0:T(2,128)(2,1)}, u32[]{:S(2)}) copy-start(bf16[5120,2,128]{2,1,0:T(2,128)(2,1)} %param.18) | copy-start | bytes 7864324
  3.5 22.8 %all-to-all-start = ((bf16[32,16,768]{2,1,0:T(8,128)(2,1)}), bf16[32,16,768]{2,1,0:T(8,128)(2,1)S(1)}, u32[]{:S(2)}, u32[]{:S(2)}) async-start(bf16[32,16,768]{2,1,0:T(8,128)(2,1)} %shard_map.100), calls=%async_computation | async-start | bytes 1572864 | tf_op jit(solution)/shard_map/all_to_all | solution.py:373
  27.3 4.9 %collective-permute-start = (bf16[64,640]{1,0:T(8,128)(2,1)S(1)}, bf16[64,640]{1,0:T(8,128)(2,1)S(1)}, u32[]{:S(2)}, u32[]{:S(2)}) collective-permute-start(bf16[64,640]{1,0:T(8,128)(2,1)S(1)} %get-tuple-element.44), channel_id=1, source_target_pairs={{0,128},{8,136},{16,144},{24,152},{32,160},{40,168},{48,176},{56,1... | collective-permute-start | bytes 245768 | tf_op jit(solution)/shard_map/ppermute | solution.py:398
  28.6 9.1 %collective-permute-start.8 = (bf16[64,640]{1,0:T(8,128)(2,1)S(1)}, bf16[64,640]{1,0:T(8,128)(2,1)S(1)}, u32[]{:S(2)}, u32[]{:S(2)}) collective-permute-start(bf16[64,640]{1,0:T(8,128)(2,1)S(1)} %get-tuple-element.46), channel_id=1, source_target_pairs={{0,64},{8,72},{16,80},{24,88},{32,96},{40,104},{48,112},{56,120},{... | collective-permute-start | bytes 245768 | tf_op jit(solution)/shard_map/ppermute | solution.py:398
  28.6 9.2 %collective-permute-start.9 = (bf16[64,640]{1,0:T(8,128)(2,1)S(1)}, bf16[64,640]{1,0:T(8,128)(2,1)S(1)}, u32[]{:S(2)}, u32[]{:S(2)}) collective-permute-start(bf16[64,640]{1,0:T(8,128)(2,1)S(1)} %get-tuple-element.48), channel_id=1, source_target_pairs={{0,192},{8,200},{16,208},{24,216},{32,224},{40,232},{48,240},{56,2... | collective-permute-start | bytes 245768 | tf_op jit(solution)/shard_map/ppermute | solution.py:398
  32.2 8.5 %collective-permute-start.1 = (bf16[128,640]{1,0:T(8,128)(2,1)S(1)}, bf16[128,640]{1,0:T(8,128)(2,1)S(1)}, u32[]{:S(2)}, u32[]{:S(2)}) collective-permute-start(bf16[128,640]{1,0:T(8,128)(2,1)S(1)} %get-tuple-element.45.refs_0_), channel_id=1, source_target_pairs={{0,1},{1,2},{2,3},{3,4},{4,5},{5,6},{6,7},{7,0},{8,9},{9,10},{10,1... | collective-permute-start | bytes 491528 | tf_op jit(solution)/shard_map/ppermute | solution.py:408
  33.8 6.9 %collective-permute-start.4 = (bf16[128,640]{1,0:T(8,128)(2,1)S(1)}, bf16[128,640]{1,0:T(8,128)(2,1)S(1)}, u32[]{:S(2)}, u32[]{:S(2)}) collective-permute-start(bf16[128,640]{1,0:T(8,128)(2,1)S(1)} %get-tuple-element.45.refs_0_), channel_id=1, source_target_pairs={{0,7},{1,0},{2,1},{3,2},{4,3},{5,4},{6,5},{7,6},{8,15},{9,8},{10,9... | collective-permute-start | bytes 491528 | tf_op jit(solution)/shard_map/ppermute | solution.py:409
  37.8 9.3 %collective-permute-start.10 = (bf16[192,640]{1,0:T(8,128)(2,1)S(1)}, bf16[192,640]{1,0:T(8,128)(2,1)S(1)}, u32[]{:S(2)}, u32[]{:S(2)}) collective-permute-start(bf16[192,640]{1,0:T(8,128)(2,1)S(1)} %constant_dynamic-update-slice_fusion.refs_1_), channel_id=1, source_target_pairs={{0,1},{1,2},{2,3},{3,4},{4,5},{5,6},{6,7},{7,0},{8,9},{9,10},{10,1... | collective-permute-start | bytes 737288 | tf_op jit(solution)/shard_map/ppermute | solution.py:408
  37.9 9.2 %collective-permute-start.11 = (bf16[192,640]{1,0:T(8,128)(2,1)S(1)}, bf16[192,640]{1,0:T(8,128)(2,1)S(1)}, u32[]{:S(2)}, u32[]{:S(2)}) collective-permute-start(bf16[192,640]{1,0:T(8,128)(2,1)S(1)} %constant_dynamic-update-slice_fusion.refs_1_), channel_id=1, source_target_pairs={{0,7},{1,0},{2,1},{3,2},{4,3},{5,4},{6,5},{7,6},{8,15},{9,8},{10,9... | collective-permute-start | bytes 737288 | tf_op jit(solution)/shard_map/ppermute | solution.py:409
  40.7 10.0 %collective-permute-start.2 = (bf16[128,640]{1,0:T(8,128)(2,1)S(1)}, bf16[128,640]{1,0:T(8,128)(2,1)}, u32[]{:S(2)}, u32[]{:S(2)}) collective-permute-start(bf16[128,640]{1,0:T(8,128)(2,1)S(1)} %collective-permute-done.1.refs_0_), channel_id=1, source_target_pairs={{0,1},{1,2},{2,3},{3,4},{4,5},{5,6},{6,7},{7,0},{8,9},{9,10},{10,1... | collective-permute-start | bytes 491528 | tf_op jit(solution)/shard_map/ppermute | solution.py:408
  40.7 10.0 %collective-permute-start.5 = (bf16[128,640]{1,0:T(8,128)(2,1)S(1)}, bf16[128,640]{1,0:T(8,128)(2,1)}, u32[]{:S(2)}, u32[]{:S(2)}) collective-permute-start(bf16[128,640]{1,0:T(8,128)(2,1)S(1)} %collective-permute-done.4.refs_2_), channel_id=1, source_target_pairs={{0,7},{1,0},{2,1},{3,2},{4,3},{5,4},{6,5},{7,6},{8,15},{9,8},{10,9... | collective-permute-start | bytes 491528 | tf_op jit(solution)/shard_map/ppermute | solution.py:409
  47.1 9.6 %collective-permute-start.12 = (bf16[192,640]{1,0:T(8,128)(2,1)S(1)}, bf16[192,640]{1,0:T(8,128)(2,1)S(1)}, u32[]{:S(2)}, u32[]{:S(2)}) collective-permute-start(bf16[192,640]{1,0:T(8,128)(2,1)S(1)} %collective-permute-done.10.refs_1_), channel_id=1, source_target_pairs={{0,1},{1,2},{2,3},{3,4},{4,5},{5,6},{6,7},{7,0},{8,9},{9,10},{10,1... | collective-permute-start | bytes 737288 | tf_op jit(solution)/shard_map/ppermute | solution.py:408
  47.1 9.6 %collective-permute-start.13 = (bf16[192,640]{1,0:T(8,128)(2,1)S(1)}, bf16[192,640]{1,0:T(8,128)(2,1)S(1)}, u32[]{:S(2)}, u32[]{:S(2)}) collective-permute-start(bf16[192,640]{1,0:T(8,128)(2,1)S(1)} %collective-permute-done.11.refs_3_), channel_id=1, source_target_pairs={{0,7},{1,0},{2,1},{3,2},{4,3},{5,4},{6,5},{7,6},{8,15},{9,8},{10,9... | collective-permute-start | bytes 737288 | tf_op jit(solution)/shard_map/ppermute | solution.py:409
  50.8 8.8 %collective-permute-start.3 = (bf16[128,640]{1,0:T(8,128)(2,1)}, bf16[128,640]{1,0:T(8,128)(2,1)S(1)}, u32[]{:S(2)}, u32[]{:S(2)}) collective-permute-start(bf16[128,640]{1,0:T(8,128)(2,1)} %collective-permute-done.2.refs_0_), channel_id=1, source_target_pairs={{0,1},{1,2},{2,3},{3,4},{4,5},{5,6},{6,7},{7,0},{8,9},{9,10},{10,1... | collective-permute-start | bytes 491528 | tf_op jit(solution)/shard_map/ppermute | solution.py:408
  50.8 8.8 %collective-permute-start.6 = (bf16[128,640]{1,0:T(8,128)(2,1)}, bf16[128,640]{1,0:T(8,128)(2,1)S(1)}, u32[]{:S(2)}, u32[]{:S(2)}) collective-permute-start(bf16[128,640]{1,0:T(8,128)(2,1)} %collective-permute-done.5.refs_2_), channel_id=1, source_target_pairs={{0,7},{1,0},{2,1},{3,2},{4,3},{5,4},{6,5},{7,6},{8,15},{9,8},{10,9... | collective-permute-start | bytes 491528 | tf_op jit(solution)/shard_map/ppermute | solution.py:409
  56.8 8.3 %collective-permute-start.14 = (bf16[192,640]{1,0:T(8,128)(2,1)S(1)}, bf16[192,640]{1,0:T(8,128)(2,1)S(1)}, u32[]{:S(2)}, u32[]{:S(2)}) collective-permute-start(bf16[192,640]{1,0:T(8,128)(2,1)S(1)} %collective-permute-done.12.refs_1_), channel_id=1, source_target_pairs={{0,1},{1,2},{2,3},{3,4},{4,5},{5,6},{6,7},{7,0},{8,9},{9,10},{10,1... | collective-permute-start | bytes 737288 | tf_op jit(solution)/shard_map/ppermute | solution.py:408
  56.9 8.3 %collective-permute-start.15 = (bf16[192,640]{1,0:T(8,128)(2,1)S(1)}, bf16[192,640]{1,0:T(8,128)(2,1)S(1)}, u32[]{:S(2)}, u32[]{:S(2)}) collective-permute-start(bf16[192,640]{1,0:T(8,128)(2,1)S(1)} %collective-permute-done.13.refs_3_), channel_id=1, source_target_pairs={{0,7},{1,0},{2,1},{3,2},{4,3},{5,4},{6,5},{7,6},{8,15},{9,8},{10,9... | collective-permute-start | bytes 737288 | tf_op jit(solution)/shard_map/ppermute | solution.py:409
  60.2 10.4 %collective-permute-start.7 = (bf16[128,640]{1,0:T(8,128)(2,1)}, bf16[128,640]{1,0:T(8,128)(2,1)S(1)}, u32[]{:S(2)}, u32[]{:S(2)}) collective-permute-start(bf16[128,640]{1,0:T(8,128)(2,1)} %broadcast_select_fusion.2), channel_id=1, source_target_pairs={{0,1},{1,2},{2,3},{3,4},{4,5},{5,6},{6,7},{7,0},{8,15},{9,8},{10,9... | collective-permute-start | bytes 491528 | tf_op jit(solution)/shard_map/ppermute | solution.py:417
  65.2 5.4 %collective-permute-start.16 = (bf16[192,640]{1,0:T(8,128)(2,1)S(1)}, bf16[192,640]{1,0:T(8,128)(2,1)S(1)}, u32[]{:S(2)}, u32[]{:S(2)}) collective-permute-start(bf16[192,640]{1,0:T(8,128)(2,1)S(1)} %broadcast_select_fusion), channel_id=1, source_target_pairs={{0,1},{1,2},{2,3},{3,4},{4,5},{5,6},{6,7},{7,0},{8,15},{9,8},{10,9... | collective-permute-start | bytes 737288 | tf_op jit(solution)/shard_map/ppermute | solution.py:417
  66.5 4.1 %copy-start.1 = (bf16[128]{0:T(256)(128)(2,1)S(1)}, bf16[128]{0:T(256)(128)(2,1)}, u32[]{:S(2)}) copy-start(bf16[128]{0:T(256)(128)(2,1)} %param.19) | copy-start | bytes 772
  69.7 4.7 %copy-start.3 = (bf16[640]{0:T(1024)(128)(2,1)S(1)}, bf16[640]{0:T(1024)(128)(2,1)}, u32[]{:S(2)}) copy-start(bf16[640]{0:T(1024)(128)(2,1)} %param.17) | copy-start | bytes 3844
  72.0 4.7 %collective-permute-start.17 = (bf16[320,256]{1,0:T(8,128)(2,1)S(1)}, bf16[320,256]{1,0:T(8,128)(2,1)S(1)}, u32[]{:S(2)}, u32[]{:S(2)}) collective-permute-start(bf16[320,256]{1,0:T(8,128)(2,1)S(1)} %shard_map.106.refs_0_), channel_id=1, source_target_pairs={{0,48},{8,56},{16,0},{24,8},{32,16},{40,24},{48,32},{56,40},{64,11... | collective-permute-start | bytes 491528 | tf_op jit(solution)/shard_map/ppermute | solution.py:427
  74.4 5.4 %collective-permute-start.19 = (bf16[320,256]{1,0:T(8,128)(2,1)S(1)}, bf16[320,256]{1,0:T(8,128)(2,1)S(1)}, u32[]{:S(2)}, u32[]{:S(2)}) collective-permute-start(bf16[320,256]{1,0:T(8,128)(2,1)S(1)} %shard_map.106.refs_0_), channel_id=1, source_target_pairs={{0,16},{8,24},{16,32},{24,40},{32,48},{40,56},{48,0},{56,8},{64,80... | collective-permute-start | bytes 491528 | tf_op jit(solution)/shard_map/ppermute | solution.py:426
  79.8 8.6 %collective-permute-start.22 = (bf16[320,256]{1,0:T(8,128)(2,1)S(1)}, bf16[320,256]{1,0:T(8,128)(2,1)S(1)}, u32[]{:S(2)}, u32[]{:S(2)}) collective-permute-start(bf16[320,256]{1,0:T(8,128)(2,1)S(1)} %broadcast_select_fusion.1), channel_id=1, source_target_pairs={{0,48},{8,24},{16,0},{24,40},{32,16},{40,56},{48,32},{56,8},{64,11... | collective-permute-start | bytes 491528 | tf_op jit(solution)/shard_map/ppermute | solution.py:429
  79.9 13.5 %collective-permute-start.18 = (bf16[320,256]{1,0:T(8,128)(2,1)S(1)}, bf16[320,256]{1,0:T(8,128)(2,1)S(1)}, u32[]{:S(2)}, u32[]{:S(2)}) collective-permute-start(bf16[320,256]{1,0:T(8,128)(2,1)S(1)} %shard_map.106.refs_0_), channel_id=1, source_target_pairs={{0,8},{8,0},{16,24},{24,16},{32,40},{40,32},{48,56},{56,48},{64,72... | collective-permute-start | bytes 491528 | tf_op jit(solution)/shard_map/ppermute | solution.py:436
  87.9 5.5 %collective-permute-start.21 = (bf16[320,256]{1,0:T(8,128)(2,1)S(1)}, bf16[320,256]{1,0:T(8,128)(2,1)S(1)}, u32[]{:S(2)}, u32[]{:S(2)}) collective-permute-start(bf16[320,256]{1,0:T(8,128)(2,1)S(1)} %collective-permute-done.17.refs_4_), channel_id=1, source_target_pairs={{0,8},{8,0},{16,24},{24,16},{32,40},{40,32},{48,56},{56,48},{64,72... | collective-permute-start | bytes 491528 | tf_op jit(solution)/shard_map/ppermute | solution.py:436
  88.0 5.4 %collective-permute-start.20 = (bf16[320,256]{1,0:T(8,128)(2,1)S(1)}, bf16[320,256]{1,0:T(8,128)(2,1)S(1)}, u32[]{:S(2)}, u32[]{:S(2)}) collective-permute-start(bf16[320,256]{1,0:T(8,128)(2,1)S(1)} %collective-permute-done.19.refs_2_), channel_id=1, source_target_pairs={{0,8},{8,0},{16,24},{24,16},{32,40},{40,32},{48,56},{56,48},{64,72... | collective-permute-start | bytes 491528 | tf_op jit(solution)/shard_map/ppermute | solution.py:436
  88.5 5.7 %collective-permute-start.23 = (bf16[320,256]{1,0:T(8,128)(2,1)S(1)}, bf16[320,256]{1,0:T(8,128)(2,1)S(1)}, u32[]{:S(2)}, u32[]{:S(2)}) collective-permute-start(bf16[320,256]{1,0:T(8,128)(2,1)S(1)} %collective-permute-done.22.refs_6_), channel_id=1, source_target_pairs={{0,8},{8,0},{16,24},{24,16},{32,40},{40,32},{48,56},{56,48},{64,72... | collective-permute-start | bytes 491528 | tf_op jit(solution)/shard_map/ppermute | solution.py:436

commit v6 on v5

--- a/solution.py
+++ b/solution.py
@@ -119,7 +119,26 @@
     return (x * cosine + pltpu.roll(x, HEAD // 2, 1) * sine).astype(jnp.bfloat16)
 
 
-def finish_kernel(halves, keys, owner_ref, w_hbm, *refs):
+def keys_kernel(halves, *refs):
+    w_ref, sum_ref, cos_ref, sin_ref, bias_ref, o_ref = refs[halves:]
+    rows = rows_of(refs[:halves])
+    out = sum_ref[...] + jnp.dot(rows, w_ref[...], preferred_element_type=jnp.float32)
+    o_ref[:, :HEAD] = rotated(out[:, :HEAD], cos_ref[...], sin_ref[...])
+    o_ref[:, HEAD:] = (out[:, HEAD:] + bias_ref[...].astype(jnp.float32)).astype(jnp.bfloat16)
+
+
+def finish_keys(total, far, weight, cosine, sine, bias):
+    args = [*far, weight, total, cosine, sine, bias.reshape(1, -1)]
+    return pl.pallas_call(
+        functools.partial(keys_kernel, len(far)),
+        in_specs=[VMEM_SPEC] * len(args),
+        out_specs=VMEM_SPEC,
+        out_shape=jax.ShapeDtypeStruct(total.shape, jnp.bfloat16),
+        compiler_params=pltpu.CompilerParams(vmem_limit_bytes=SMALL_VMEM),
+    )(*args)
+
+
+def finish_kernel(halves, owner_ref, w_hbm, *refs):
     sum_ref, cos_ref, sin_ref, bias_ref, o_ref, w_ref, sem = refs[halves:]
     feat = w_ref.shape[0]
     at = pl.ds(pl.multiple_of(owner_ref[0] * feat, feat), feat)
@@ -128,22 +147,17 @@
     rows = rows_of(refs[:halves])
     copy.wait()
     out = sum_ref[...] + jnp.dot(rows, w_ref[...], preferred_element_type=jnp.float32)
-    bias = bias_ref[...].astype(jnp.float32)
-    if keys:
-        o_ref[:, :HEAD] = rotated(out[:, :HEAD], cos_ref[...], sin_ref[...])
-        o_ref[:, HEAD:] = (out[:, HEAD:] + bias).astype(jnp.bfloat16)
-        return
-    out = out + bias
+    out = out + bias_ref[...].astype(jnp.float32)
     for h in range(out.shape[1] // HEAD):
         at = slice(h * HEAD, (h + 1) * HEAD)
         o_ref[:, at] = rotated(out[:, at], cos_ref[...], sin_ref[...])
 
 
-def finish(keys, total, far, owner, weight, cosine, sine, bias):
+def finish_queries(total, far, owner, weight, cosine, sine, bias):
     (count, cols), feat = total.shape, far[0].shape[1]
     args = [*far, total, cosine, sine, bias.reshape(1, -1)]
     return pl.pallas_call(
-        functools.partial(finish_kernel, len(far), keys),
+        functools.partial(finish_kernel, len(far)),
         in_specs=[SMEM_SPEC, HBM_SPEC] + [VMEM_SPEC] * len(args),
         out_specs=VMEM_SPEC,
         out_shape=jax.ShapeDtypeStruct((count, cols), jnp.bfloat16),
@@ -373,6 +387,8 @@
     sent = lax.all_to_all(sent, "ctx", 0, 0, tiled=True)
 
     kv_flat = key_value_weight.reshape(key_value_weight.shape[0], -1)
+    opposite = (plane + PLANES // 2) % PLANES
+    kv_opposite = lax.dynamic_slice_in_dim(kv_flat, opposite * feat, feat, 0)
     text_at = lax.dynamic_index_in_dim(
         lax.dynamic_index_in_dim(text_positions, group, 0, keepdims=False).reshape(-1, MEMBERS),
         member, 1, keepdims=False,
@@ -389,8 +405,8 @@
     sub = block_len // MEMBERS
     send_from = sub * block_order.reshape(DEVICES, 1, 2) + jnp.arange(sub).reshape(1, sub, 1)
     send_from = send_from.astype(jnp.int32).reshape(-1, 1)
-    sent, kv_flat, cosine, sine, send_from = lax.optimization_barrier(
-        (sent, kv_flat, cosine, sine, send_from)
+    sent, kv_flat, kv_opposite, cosine, sine, send_from = lax.optimization_barrier(
+        (sent, kv_flat, kv_opposite, cosine, sine, send_from)
     )
 
     first, *others = unpack(candidates, clip_slot, group, sent, clips_here)
@@ -419,20 +435,20 @@
     ]
     sums = add_products(sums, parts, owners, w_query, kv_flat)
     far[-1], sums = lax.optimization_barrier((far[-1], sums))
-    opposite = (plane + PLANES // 2) % PLANES
-    kv = finish(True, sums[1], far, opposite, kv_flat, cosine, sine, value_offset_bias)
-    q = finish(False, sums[0], far, opposite, w_query, cosine, sine, b_query)
+    kv = finish_keys(sums[1], far, kv_opposite, cosine, sine, value_offset_bias)
+    q = finish_queries(sums[0], far, opposite, w_query, cosine, sine, b_query)
 
     below = lax.ppermute(kv, "ctx", ctx_pairs(lambda y, x, c: (y, x + 1, c)))
     above = lax.ppermute(kv, "ctx", ctx_pairs(lambda y, x, c: (y, x - 1, c)))
-    above, q = lax.optimization_barrier((above, q))
+    swap = ctx_pairs(lambda y, x, c: (y, x, 1 - c))
+    beside = lax.ppermute(kv, "ctx", swap)
+    above, beside, q = lax.optimization_barrier((above, beside, q))
     beyond = lax.ppermute(
         jnp.where(core == 0, above, below), "ctx",
         ctx_pairs(lambda y, x, c: (y, x + (-1 if c == 0 else 1), c)),
     )
-    swap = ctx_pairs(lambda y, x, c: (y, x, 1 - c))
-    pieces = []
-    for piece in (kv, below, above, beyond):
+    pieces = [kv, beside]
+    for piece in (below, above, beyond):
         pieces += [piece, lax.ppermute(piece, "ctx", swap)]
 
     info = jnp.stack([group, member]).astype(jnp.int32)

time: 116 us -> 114 us (0.983)
  starting transfers between devices: 50 us -> 44.8 us
  waiting for transfers between devices: 19.1 us -> 22 us
  local copies, waits for them, and re-layouts: 3.93 us -> 6.68 us
    ppermute x4 -> x3, starting transfers between devices: 13.2 us -> 1.7 us  [per_device(): pieces += [piece, lax.ppermute(piece, 'ctx', swap)]]
    ppermute x0 -> x1, starting transfers between devices: none -> 5.8 us  [per_device(): beside = lax.ppermute(kv, 'ctx', swap)]
    ppermute x1, waiting for transfers between devices: 0.01 us -> 4.39 us  [per_device(): lax.ppermute(jnp.where(core == 0, above, below), 'ctx', ctx_pairs(lambda...]
    all_to_all x1, waiting for transfers between devices: 10.3 us -> 7.55 us  [per_device(): sent = lax.all_to_all(sent, 'ctx', 0, 0, tiled=True)]
    ppermute x1, waiting for transfers between devices: 3.12 us -> 5.18 us  [per_device(): below = lax.ppermute(kv, 'ctx', ctx_pairs(lambda y, x, c: (y, x + 1, c)))]
    unnamed x13 -> x11, local copies, waits for them, and re-layouts: 1.89 us -> 3.65 us
  transfers between devices with their start and end apart: 25 -> 25, of which waited for: 8 -> 8; matrix products, arithmetic and copies ran while one was open for 4% -> 6% of each run, Pallas kernels for 12% -> 12%
where the time goes in v6:
time: 114 us
  starting transfers between devices  44.8 us (39%)
  Pallas kernels  24.4 us (21%)
  waiting for transfers between devices  22 us (19%)
  blocking collectives  14 us (12%)
  local copies, waits for them, and re-layouts  6.68 us (6%)
  other arithmetic  1.29 us (1%)
    ppermute x6, starting transfers between devices, per_device(): bwd[h] = lax.ppermute(bwd[h], 'mp', shifted(PLANES, -1))  17.4 us
    all_to_all x1, blocking collectives, per_device(): recv = lax.all_to_all(send, 'ctx', 0, 0, tiled=True)  14 us
    pallas_call x4, Pallas kernels, add_products(): pl.pallas_call(functools.partial(products_kernel, groups, halves, sums is...  12.1 us
    all_to_all x1, starting transfers between devices, per_device(): sent = lax.all_to_all(sent, 'ctx', 0, 0, tiled=True)  8.6 us
    all_to_all x1, waiting for transfers between devices, per_device(): sent = lax.all_to_all(sent, 'ctx', 0, 0, tiled=True)  7.55 us
    ppermute x1, starting transfers between devices, per_device(): beside = lax.ppermute(kv, 'ctx', swap)  5.8 us
    pallas_call x1, Pallas kernels, attend(): pl.pallas_call(functools.partial(attend_kernel, heads, clips), out_shape=...  5.79 us
    ppermute x1, waiting for transfers between devices, per_device(): below = lax.ppermute(kv, 'ctx', ctx_pairs(lambda y, x, c: (y, x + 1, c)))  5.18 us
  transfers between devices with their start and end apart: 25, of which 8 were waited for; matrix products, arithmetic and copies ran while one was open for 6% of the time, Pallas kernels for 12%

profile of v6, /device:TPU:1, one launch (start us, length us, event | category | flops | bytes accessed | tf_op | source)
XLA Modules:
  0.0 113.6 jit_solution(10043233317069569291)
XLA Ops:
  0.0 3.3 %shard_map.100 = bf16[32,16,768]{2,1,0:T(8,128)(2,1)} custom-call(s32[4,4]{1,0:T(4,128)} %cand_ref.3, s32[64]{0:T(128)} %slot_ref.3, s32[1]{0:T(128)} %bitcast.2.me_ref, bf16[2,512,640]{2,1,0:T(8,128)(2,1)} %clip_hbm.1, bf16[4,16,640]{2,1,0:T(8,128)(2,1)} %text_ref.1), custom_call_target="tpu_custom_call" | custom-call | tf_op jit(solution)/shard_map/pallas_call | solution.py:218
  3.4 8.6 %all-to-all-start = ((bf16[32,16,768]{2,1,0:T(8,128)(2,1)}), bf16[32,16,768]{2,1,0:T(8,128)(2,1)S(1)}, u32[]{:S(2)}, u32[]{:S(2)}) async-start(bf16[32,16,768]{2,1,0:T(8,128)(2,1)} %shard_map.100), calls=%async_computation | async-start | bytes 1572864 | tf_op jit(solution)/shard_map/all_to_all | solution.py:387
  12.9 3.6 %copy.19 = bf16[640,8,2,128]{3,1,2,0:T(8,128)(2,1)} copy(bf16[640,8,2,128]{3,2,1,0:T(2,128)(2,1)} %bitcast.28) | data formatting | bytes 5242880
  16.8 1.0 constant_dynamic-slice_fusion.refs_2_
  18.6 7.5 %all-to-all-done.sent_ref = bf16[32,16,768]{2,1,0:T(8,128)(2,1)S(1)} async-done(((bf16[32,16,768]{2,1,0:T(8,128)(2,1)}), bf16[32,16,768]{2,1,0:T(8,128)(2,1)S(1)}, u32[]{:S(2)}, u32[]{:S(2)}) %all-to-all-start) | async-done | bytes 786464 | tf_op jit(solution)/shard_map/all_to_all | solution.py:387
  26.2 1.0 shard_map.101
  27.2 1.3 %collective-permute-start = (bf16[64,640]{1,0:T(8,128)(2,1)S(1)}, bf16[64,640]{1,0:T(8,128)(2,1)S(1)}, u32[]{:S(2)}, u32[]{:S(2)}) collective-permute-start(bf16[64,640]{1,0:T(8,128)(2,1)S(1)} %get-tuple-element.45), channel_id=1, source_target_pairs={{0,128},{8,136},{16,144},{24,152},{32,160},{40,168},{48,176},{56,1... | collective-permute-start | bytes 245768 | tf_op jit(solution)/shard_map/ppermute | solution.py:414
  28.5 2.7 %collective-permute-start.9 = (bf16[64,640]{1,0:T(8,128)(2,1)S(1)}, bf16[64,640]{1,0:T(8,128)(2,1)S(1)}, u32[]{:S(2)}, u32[]{:S(2)}) collective-permute-start(bf16[64,640]{1,0:T(8,128)(2,1)S(1)} %get-tuple-element.49), channel_id=1, source_target_pairs={{0,192},{8,200},{16,208},{24,216},{32,224},{40,232},{48,240},{56,2... | collective-permute-start | bytes 245768 | tf_op jit(solution)/shard_map/ppermute | solution.py:414
  31.2 0.9 collective-permute-done
  32.1 1.6 %collective-permute-start.1 = (bf16[128,640]{1,0:T(8,128)(2,1)S(1)}, bf16[128,640]{1,0:T(8,128)(2,1)S(1)}, u32[]{:S(2)}, u32[]{:S(2)}) collective-permute-start(bf16[128,640]{1,0:T(8,128)(2,1)S(1)} %get-tuple-element.46.refs_0_), channel_id=1, source_target_pairs={{0,1},{1,2},{2,3},{3,4},{4,5},{5,6},{6,7},{7,0},{8,9},{9,10},{10,1... | collective-permute-start | bytes 491528 | tf_op jit(solution)/shard_map/ppermute | solution.py:424
  33.7 3.9 %collective-permute-start.4 = (bf16[128,640]{1,0:T(8,128)(2,1)S(1)}, bf16[128,640]{1,0:T(8,128)(2,1)S(1)}, u32[]{:S(2)}, u32[]{:S(2)}) collective-permute-start(bf16[128,640]{1,0:T(8,128)(2,1)S(1)} %get-tuple-element.46.refs_0_), channel_id=1, source_target_pairs={{0,7},{1,0},{2,1},{3,2},{4,3},{5,4},{6,5},{7,6},{8,15},{9,8},{10,9... | collective-permute-start | bytes 491528 | tf_op jit(solution)/shard_map/ppermute | solution.py:425
  37.8 2.8 %collective-permute-start.11 = (bf16[192,640]{1,0:T(8,128)(2,1)S(1)}, bf16[192,640]{1,0:T(8,128)(2,1)S(1)}, u32[]{:S(2)}, u32[]{:S(2)}) collective-permute-start(bf16[192,640]{1,0:T(8,128)(2,1)S(1)} %constant_dynamic-update-slice_fusion.refs_1_), channel_id=1, source_target_pairs={{0,7},{1,0},{2,1},{3,2},{4,3},{5,4},{6,5},{7,6},{8,15},{9,8},{10,9... | collective-permute-start | bytes 737288 | tf_op jit(solution)/shard_map/ppermute | solution.py:425
  40.6 2.7 %collective-permute-start.5 = (bf16[128,640]{1,0:T(8,128)(2,1)S(1)}, bf16[128,640]{1,0:T(8,128)(2,1)}, u32[]{:S(2)}, u32[]{:S(2)}) collective-permute-start(bf16[128,640]{1,0:T(8,128)(2,1)S(1)} %collective-permute-done.4.refs_2_), channel_id=1, source_target_pairs={{0,7},{1,0},{2,1},{3,2},{4,3},{5,4},{6,5},{7,6},{8,15},{9,8},{10,9... | collective-permute-start | bytes 491528 | tf_op jit(solution)/shard_map/ppermute | solution.py:425
  43.3 1.9 %shard_map.102 = (f32[320,640]{1,0:T(8,128)S(1)}, f32[320,256]{1,0:T(8,128)S(1)}) custom-call(s32[1]{0:T(128)} %bitcast.3.owners_ref, bf16[5120,640]{1,0:T(8,128)(2,1)} %w_hbm.1, bf16[5120,256]{1,0:T(8,128)(2,1)} %bitcast.24, bf16[128,640]{1,0:T(8,128)(2,1)S(1)} %get-tuple-element.46.refs_0_, bf16[192,640]{1,0:T(8,128)(2,1)S(1)} %constant_dynamic-update-slice_fusion.refs_1_), custom_call_target="tpu_custom_call" | custom-call | flops 734003200 | bytes 1146880 | tf_op jit(solution)/shard_map/pallas_call | solution.py:96
  45.2 1.8 %collective-permute-done.10.refs_1_ = bf16[192,640]{1,0:T(8,128)(2,1)S(1)} collective-permute-done((bf16[192,640]{1,0:T(8,128)(2,1)S(1)}, bf16[192,640]{1,0:T(8,128)(2,1)S(1)}, u32[]{:S(2)}, u32[]{:S(2)}) %collective-permute-start.10) | collective-permute-done | bytes 245792 | tf_op jit(solution)/shard_map/ppermute | solution.py:424
  47.0 2.7 %collective-permute-start.13 = (bf16[192,640]{1,0:T(8,128)(2,1)S(1)}, bf16[192,640]{1,0:T(8,128)(2,1)S(1)}, u32[]{:S(2)}, u32[]{:S(2)}) collective-permute-start(bf16[192,640]{1,0:T(8,128)(2,1)S(1)} %collective-permute-done.11.refs_3_), channel_id=1, source_target_pairs={{0,7},{1,0},{2,1},{3,2},{4,3},{5,4},{6,5},{7,6},{8,15},{9,8},{10,9... | collective-permute-start | bytes 737288 | tf_op jit(solution)/shard_map/ppermute | solution.py:425
  49.7 0.9 collective-permute-done.2.refs_0_
  50.6 2.7 %collective-permute-start.6 = (bf16[128,640]{1,0:T(8,128)(2,1)}, bf16[128,640]{1,0:T(8,128)(2,1)S(1)}, u32[]{:S(2)}, u32[]{:S(2)}) collective-permute-start(bf16[128,640]{1,0:T(8,128)(2,1)} %collective-permute-done.5.refs_2_), channel_id=1, source_target_pairs={{0,7},{1,0},{2,1},{3,2},{4,3},{5,4},{6,5},{7,6},{8,15},{9,8},{10,9... | collective-permute-start | bytes 491528 | tf_op jit(solution)/shard_map/ppermute | solution.py:425
  53.4 3.2 %shard_map.103 = (f32[320,640]{1,0:T(8,128)S(1)}, f32[320,256]{1,0:T(8,128)S(1)}) custom-call(s32[2]{0:T(128)S(1)} %pad_add_fusion.1.owners_ref, bf16[5120,640]{1,0:T(8,128)(2,1)} %w_hbm.1, bf16[5120,256]{1,0:T(8,128)(2,1)} %bitcast.25, bf16[128,640]{1,0:T(8,128)(2,1)S(1)} %collective-permute-done.1.refs_0_, ...), custom_call_target="tpu_custom_call" | custom-call | flops 1468006400 | bytes 2293760 | tf_op jit(solution)/shard_map/pallas_call | solution.py:96
  56.7 2.7 %collective-permute-start.15 = (bf16[192,640]{1,0:T(8,128)(2,1)S(1)}, bf16[192,640]{1,0:T(8,128)(2,1)S(1)}, u32[]{:S(2)}, u32[]{:S(2)}) collective-permute-start(bf16[192,640]{1,0:T(8,128)(2,1)S(1)} %collective-permute-done.13.refs_3_), channel_id=1, source_target_pairs={{0,7},{1,0},{2,1},{3,2},{4,3},{5,4},{6,5},{7,6},{8,15},{9,8},{10,9... | collective-permute-start | bytes 737288 | tf_op jit(solution)/shard_map/ppermute | solution.py:425
  59.4 1.3 %collective-permute-start.7 = (bf16[128,640]{1,0:T(8,128)(2,1)S(1)}, bf16[128,640]{1,0:T(8,128)(2,1)S(1)}, u32[]{:S(2)}, u32[]{:S(2)}) collective-permute-start(bf16[128,640]{1,0:T(8,128)(2,1)S(1)} %broadcast_select_fusion.2), channel_id=1, source_target_pairs={{0,1},{1,2},{2,3},{3,4},{4,5},{5,6},{6,7},{7,0},{8,15},{9,8},{10,9... | collective-permute-start | bytes 491528 | tf_op jit(solution)/shard_map/ppermute | solution.py:433
  60.7 3.7 %shard_map.104 = (f32[320,640]{1,0:T(8,128)S(1)}, f32[320,256]{1,0:T(8,128)S(1)}) custom-call(s32[2]{0:T(128)S(1)} %pad_add_fusion.2.owners_ref, bf16[5120,640]{1,0:T(8,128)(2,1)} %w_hbm.1, bf16[5120,256]{1,0:T(8,128)(2,1)} %bitcast.26, bf16[128,640]{1,0:T(8,128)(2,1)} %collective-permute-done.2.refs_0_, ...), custom_call_target="tpu_custom_call" | custom-call | flops 1468006400 | bytes 2293760 | tf_op jit(solution)/shard_map/pallas_call | solution.py:96
  64.5 1.8 %collective-permute-start.16 = (bf16[192,640]{1,0:T(8,128)(2,1)S(1)}, bf16[192,640]{1,0:T(8,128)(2,1)S(1)}, u32[]{:S(2)}, u32[]{:S(2)}) collective-permute-start(bf16[192,640]{1,0:T(8,128)(2,1)S(1)} %broadcast_select_fusion), channel_id=1, source_target_pairs={{0,1},{1,2},{2,3},{3,4},{4,5},{5,6},{6,7},{7,0},{8,15},{9,8},{10,9... | collective-permute-start | bytes 737288 | tf_op jit(solution)/shard_map/ppermute | solution.py:433
  66.3 3.2 %shard_map.105 = (f32[320,640]{1,0:T(8,128)S(1)}, f32[320,256]{1,0:T(8,128)S(1)}) custom-call(s32[2]{0:T(128)S(1)} %pad_add_fusion.3.owners_ref, bf16[5120,640]{1,0:T(8,128)(2,1)} %w_hbm.1, bf16[5120,256]{1,0:T(8,128)(2,1)} %bitcast.27, bf16[128,640]{1,0:T(8,128)(2,1)S(1)} %collective-permute-done.3.refs_0_, ...), custom_call_target="tpu_custom_call" | custom-call | flops 1468006400 | bytes 2293760 | tf_op jit(solution)/shard_map/pallas_call | solution.py:96
  70.4 2.3 %collective-permute-start.17 = (bf16[320,256]{1,0:T(8,128)(2,1)S(1)}, bf16[320,256]{1,0:T(8,128)(2,1)S(1)}, u32[]{:S(2)}, u32[]{:S(2)}) collective-permute-start(bf16[320,256]{1,0:T(8,128)(2,1)S(1)} %shard_map.106.refs_0_), channel_id=1, source_target_pairs={{0,48},{8,56},{16,0},{24,8},{32,16},{40,24},{48,32},{56,40},{64,11... | collective-permute-start | bytes 491528 | tf_op jit(solution)/shard_map/ppermute | solution.py:442
  72.7 5.8 %collective-permute-start.18 = (bf16[320,256]{1,0:T(8,128)(2,1)S(1)}, bf16[320,256]{1,0:T(8,128)(2,1)S(1)}, u32[]{:S(2)}, u32[]{:S(2)}) collective-permute-start(bf16[320,256]{1,0:T(8,128)(2,1)S(1)} %shard_map.106.refs_0_), channel_id=1, source_target_pairs={{0,8},{8,0},{16,24},{24,16},{32,40},{40,32},{48,56},{56,48},{64,72... | collective-permute-start | bytes 491528 | tf_op jit(solution)/shard_map/ppermute | solution.py:444
  78.6 1.8 %shard_map.107.q_ref = bf16[320,640]{1,0:T(8,128)(2,1)S(1)} custom-call(s32[1]{0:T(128)} %bitcast.11.owner_ref, bf16[5120,640]{1,0:T(8,128)(2,1)} %w_hbm.1, bf16[128,640]{1,0:T(8,128)(2,1)S(1)} %collective-permute-done.7.refs_0_, bf16[192,640]{1,0:T(8,128)(2,1)S(1)} %collective-permute-done.16.refs_1_, f32[320,640]{1,0:T(8,128)S(1)} %get-tuple-element.76.refs_2_, ...), custom_call_target="tpu_custom_call" | custom-call | flops 524288000 | bytes 2000000 | tf_op jit(solution)/shard_map/pallas_call | solution.py:159
  80.4 5.2 %collective-permute-done.19.refs_2_ = bf16[320,256]{1,0:T(8,128)(2,1)S(1)} collective-permute-done((bf16[320,256]{1,0:T(8,128)(2,1)S(1)}, bf16[320,256]{1,0:T(8,128)(2,1)S(1)}, u32[]{:S(2)}, u32[]{:S(2)}) %collective-permute-start.19) | collective-permute-done | bytes 163872 | tf_op jit(solution)/shard_map/ppermute | solution.py:441
  85.7 0.9 collective-permute-start.21
  86.7 4.4 %collective-permute-done.22.refs_6_ = bf16[320,256]{1,0:T(8,128)(2,1)S(1)} collective-permute-done((bf16[320,256]{1,0:T(8,128)(2,1)S(1)}, bf16[320,256]{1,0:T(8,128)(2,1)S(1)}, u32[]{:S(2)}, u32[]{:S(2)}) %collective-permute-start.22) | collective-permute-done | bytes 163872 | tf_op jit(solution)/shard_map/ppermute | solution.py:446
  92.8 5.8 %shard_map.108 = bf16[320,640]{1,0:T(8,128)(2,1)S(1)} custom-call(s32[2]{0:T(128)S(1)} %pad_add_fusion.info_ref, bf16[320,640]{1,0:T(8,128)(2,1)S(1)} %shard_map.107.q_ref, s32[320,1]{1,0:T(8,128)S(1)} %copy.14.to_ref, bf16[320,256]{1,0:T(8,128)(2,1)S(1)} %shard_map.106.refs_0_, bf16[320,256]{1,0:T(8,128)(2,1)S(1)} %collective-permute-done.18.refs_1_, ...), custom_call_target="tpu_custom_call" | custom-call | flops 1300000000 | bytes 4000000 | tf_op jit(solution)/shard_map/pallas_call | solution.py:351
  98.8 14.0 %all_to_all.10 = bf16[32,5,2,640]{3,2,1,0:T(2,128)(2,1)S(1)} all-to-all(bf16[32,5,2,640]{3,2,1,0:T(2,128)(2,1)S(1)} %reshape.162), channel_id=1, replica_groups=mesh['ctx'=32,'mp'=8] {'ctx'}, dimensions={0} | all-to-all | bytes 819200 | tf_op jit(solution)/shard_map/all_to_all | solution.py:458
  (70 shorter events, 6.1 us)
Async XLA Ops:
  0.0 12.5 %copy-start = (s32[4,512]{1,0:T(4,128)S(1)}, s32[4,512]{1,0:T(4,128)}, u32[]{:S(2)}) copy-start(s32[4,512]{1,0:T(4,128)} %param.14) | copy-start | bytes 24580
  3.4 22.8 %all-to-all-start = ((bf16[32,16,768]{2,1,0:T(8,128)(2,1)}), bf16[32,16,768]{2,1,0:T(8,128)(2,1)S(1)}, u32[]{:S(2)}, u32[]{:S(2)}) async-start(bf16[32,16,768]{2,1,0:T(8,128)(2,1)} %shard_map.100), calls=%async_computation | async-start | bytes 1572864 | tf_op jit(solution)/shard_map/all_to_all | solution.py:387
  12.9 3.6 %copy-start.3 = (s32[64]{0:T(128)S(1)}, s32[64]{0:T(128)}, u32[]{:S(2)}) copy-start(s32[64]{0:T(128)} %param.15) | copy-start | bytes 772
  27.2 4.9 %collective-permute-start = (bf16[64,640]{1,0:T(8,128)(2,1)S(1)}, bf16[64,640]{1,0:T(8,128)(2,1)S(1)}, u32[]{:S(2)}, u32[]{:S(2)}) collective-permute-start(bf16[64,640]{1,0:T(8,128)(2,1)S(1)} %get-tuple-element.45), channel_id=1, source_target_pairs={{0,128},{8,136},{16,144},{24,152},{32,160},{40,168},{48,176},{56,1... | collective-permute-start | bytes 245768 | tf_op jit(solution)/shard_map/ppermute | solution.py:414
  28.5 9.1 %collective-permute-start.8 = (bf16[64,640]{1,0:T(8,128)(2,1)S(1)}, bf16[64,640]{1,0:T(8,128)(2,1)S(1)}, u32[]{:S(2)}, u32[]{:S(2)}) collective-permute-start(bf16[64,640]{1,0:T(8,128)(2,1)S(1)} %get-tuple-element.47), channel_id=1, source_target_pairs={{0,64},{8,72},{16,80},{24,88},{32,96},{40,104},{48,112},{56,120},{... | collective-permute-start | bytes 245768 | tf_op jit(solution)/shard_map/ppermute | solution.py:414
  28.5 9.2 %collective-permute-start.9 = (bf16[64,640]{1,0:T(8,128)(2,1)S(1)}, bf16[64,640]{1,0:T(8,128)(2,1)S(1)}, u32[]{:S(2)}, u32[]{:S(2)}) collective-permute-start(bf16[64,640]{1,0:T(8,128)(2,1)S(1)} %get-tuple-element.49), channel_id=1, source_target_pairs={{0,192},{8,200},{16,208},{24,216},{32,224},{40,232},{48,240},{56,2... | collective-permute-start | bytes 245768 | tf_op jit(solution)/shard_map/ppermute | solution.py:414
  32.1 8.5 %collective-permute-start.1 = (bf16[128,640]{1,0:T(8,128)(2,1)S(1)}, bf16[128,640]{1,0:T(8,128)(2,1)S(1)}, u32[]{:S(2)}, u32[]{:S(2)}) collective-permute-start(bf16[128,640]{1,0:T(8,128)(2,1)S(1)} %get-tuple-element.46.refs_0_), channel_id=1, source_target_pairs={{0,1},{1,2},{2,3},{3,4},{4,5},{5,6},{6,7},{7,0},{8,9},{9,10},{10,1... | collective-permute-start | bytes 491528 | tf_op jit(solution)/shard_map/ppermute | solution.py:424
  33.7 6.9 %collective-permute-start.4 = (bf16[128,640]{1,0:T(8,128)(2,1)S(1)}, bf16[128,640]{1,0:T(8,128)(2,1)S(1)}, u32[]{:S(2)}, u32[]{:S(2)}) collective-permute-start(bf16[128,640]{1,0:T(8,128)(2,1)S(1)} %get-tuple-element.46.refs_0_), channel_id=1, source_target_pairs={{0,7},{1,0},{2,1},{3,2},{4,3},{5,4},{6,5},{7,6},{8,15},{9,8},{10,9... | collective-permute-start | bytes 491528 | tf_op jit(solution)/shard_map/ppermute | solution.py:425
  37.7 9.3 %collective-permute-start.10 = (bf16[192,640]{1,0:T(8,128)(2,1)S(1)}, bf16[192,640]{1,0:T(8,128)(2,1)S(1)}, u32[]{:S(2)}, u32[]{:S(2)}) collective-permute-start(bf16[192,640]{1,0:T(8,128)(2,1)S(1)} %constant_dynamic-update-slice_fusion.refs_1_), channel_id=1, source_target_pairs={{0,1},{1,2},{2,3},{3,4},{4,5},{5,6},{6,7},{7,0},{8,9},{9,10},{10,1... | collective-permute-start | bytes 737288 | tf_op jit(solution)/shard_map/ppermute | solution.py:424
  37.8 9.2 %collective-permute-start.11 = (bf16[192,640]{1,0:T(8,128)(2,1)S(1)}, bf16[192,640]{1,0:T(8,128)(2,1)S(1)}, u32[]{:S(2)}, u32[]{:S(2)}) collective-permute-start(bf16[192,640]{1,0:T(8,128)(2,1)S(1)} %constant_dynamic-update-slice_fusion.refs_1_), channel_id=1, source_target_pairs={{0,7},{1,0},{2,1},{3,2},{4,3},{5,4},{6,5},{7,6},{8,15},{9,8},{10,9... | collective-permute-start | bytes 737288 | tf_op jit(solution)/shard_map/ppermute | solution.py:425
  40.6 10.0 %collective-permute-start.2 = (bf16[128,640]{1,0:T(8,128)(2,1)S(1)}, bf16[128,640]{1,0:T(8,128)(2,1)}, u32[]{:S(2)}, u32[]{:S(2)}) collective-permute-start(bf16[128,640]{1,0:T(8,128)(2,1)S(1)} %collective-permute-done.1.refs_0_), channel_id=1, source_target_pairs={{0,1},{1,2},{2,3},{3,4},{4,5},{5,6},{6,7},{7,0},{8,9},{9,10},{10,1... | collective-permute-start | bytes 491528 | tf_op jit(solution)/shard_map/ppermute | solution.py:424
  40.6 10.0 %collective-permute-start.5 = (bf16[128,640]{1,0:T(8,128)(2,1)S(1)}, bf16[128,640]{1,0:T(8,128)(2,1)}, u32[]{:S(2)}, u32[]{:S(2)}) collective-permute-start(bf16[128,640]{1,0:T(8,128)(2,1)S(1)} %collective-permute-done.4.refs_2_), channel_id=1, source_target_pairs={{0,7},{1,0},{2,1},{3,2},{4,3},{5,4},{6,5},{7,6},{8,15},{9,8},{10,9... | collective-permute-start | bytes 491528 | tf_op jit(solution)/shard_map/ppermute | solution.py:425
  47.0 9.6 %collective-permute-start.12 = (bf16[192,640]{1,0:T(8,128)(2,1)S(1)}, bf16[192,640]{1,0:T(8,128)(2,1)S(1)}, u32[]{:S(2)}, u32[]{:S(2)}) collective-permute-start(bf16[192,640]{1,0:T(8,128)(2,1)S(1)} %collective-permute-done.10.refs_1_), channel_id=1, source_target_pairs={{0,1},{1,2},{2,3},{3,4},{4,5},{5,6},{6,7},{7,0},{8,9},{9,10},{10,1... | collective-permute-start | bytes 737288 | tf_op jit(solution)/shard_map/ppermute | solution.py:424
  47.0 9.6 %collective-permute-start.13 = (bf16[192,640]{1,0:T(8,128)(2,1)S(1)}, bf16[192,640]{1,0:T(8,128)(2,1)S(1)}, u32[]{:S(2)}, u32[]{:S(2)}) collective-permute-start(bf16[192,640]{1,0:T(8,128)(2,1)S(1)} %collective-permute-done.11.refs_3_), channel_id=1, source_target_pairs={{0,7},{1,0},{2,1},{3,2},{4,3},{5,4},{6,5},{7,6},{8,15},{9,8},{10,9... | collective-permute-start | bytes 737288 | tf_op jit(solution)/shard_map/ppermute | solution.py:425
  50.6 8.8 %collective-permute-start.3 = (bf16[128,640]{1,0:T(8,128)(2,1)}, bf16[128,640]{1,0:T(8,128)(2,1)S(1)}, u32[]{:S(2)}, u32[]{:S(2)}) collective-permute-start(bf16[128,640]{1,0:T(8,128)(2,1)} %collective-permute-done.2.refs_0_), channel_id=1, source_target_pairs={{0,1},{1,2},{2,3},{3,4},{4,5},{5,6},{6,7},{7,0},{8,9},{9,10},{10,1... | collective-permute-start | bytes 491528 | tf_op jit(solution)/shard_map/ppermute | solution.py:424
  50.6 8.8 %collective-permute-start.6 = (bf16[128,640]{1,0:T(8,128)(2,1)}, bf16[128,640]{1,0:T(8,128)(2,1)S(1)}, u32[]{:S(2)}, u32[]{:S(2)}) collective-permute-start(bf16[128,640]{1,0:T(8,128)(2,1)} %collective-permute-done.5.refs_2_), channel_id=1, source_target_pairs={{0,7},{1,0},{2,1},{3,2},{4,3},{5,4},{6,5},{7,6},{8,15},{9,8},{10,9... | collective-permute-start | bytes 491528 | tf_op jit(solution)/shard_map/ppermute | solution.py:425
  56.6 7.8 %collective-permute-start.14 = (bf16[192,640]{1,0:T(8,128)(2,1)S(1)}, bf16[192,640]{1,0:T(8,128)(2,1)S(1)}, u32[]{:S(2)}, u32[]{:S(2)}) collective-permute-start(bf16[192,640]{1,0:T(8,128)(2,1)S(1)} %collective-permute-done.12.refs_1_), channel_id=1, source_target_pairs={{0,1},{1,2},{2,3},{3,4},{4,5},{5,6},{6,7},{7,0},{8,9},{9,10},{10,1... | collective-permute-start | bytes 737288 | tf_op jit(solution)/shard_map/ppermute | solution.py:424
  56.7 7.7 %collective-permute-start.15 = (bf16[192,640]{1,0:T(8,128)(2,1)S(1)}, bf16[192,640]{1,0:T(8,128)(2,1)S(1)}, u32[]{:S(2)}, u32[]{:S(2)}) collective-permute-start(bf16[192,640]{1,0:T(8,128)(2,1)S(1)} %collective-permute-done.13.refs_3_), channel_id=1, source_target_pairs={{0,7},{1,0},{2,1},{3,2},{4,3},{5,4},{6,5},{7,6},{8,15},{9,8},{10,9... | collective-permute-start | bytes 737288 | tf_op jit(solution)/shard_map/ppermute | solution.py:425
  59.4 10.6 %collective-permute-start.7 = (bf16[128,640]{1,0:T(8,128)(2,1)S(1)}, bf16[128,640]{1,0:T(8,128)(2,1)S(1)}, u32[]{:S(2)}, u32[]{:S(2)}) collective-permute-start(bf16[128,640]{1,0:T(8,128)(2,1)S(1)} %broadcast_select_fusion.2), channel_id=1, source_target_pairs={{0,1},{1,2},{2,3},{3,4},{4,5},{5,6},{6,7},{7,0},{8,15},{9,8},{10,9... | collective-permute-start | bytes 491528 | tf_op jit(solution)/shard_map/ppermute | solution.py:433
  64.5 5.6 %collective-permute-start.16 = (bf16[192,640]{1,0:T(8,128)(2,1)S(1)}, bf16[192,640]{1,0:T(8,128)(2,1)S(1)}, u32[]{:S(2)}, u32[]{:S(2)}) collective-permute-start(bf16[192,640]{1,0:T(8,128)(2,1)S(1)} %broadcast_select_fusion), channel_id=1, source_target_pairs={{0,1},{1,2},{2,3},{3,4},{4,5},{5,6},{6,7},{7,0},{8,15},{9,8},{10,9... | collective-permute-start | bytes 737288 | tf_op jit(solution)/shard_map/ppermute | solution.py:433
  66.3 3.7 %copy-start.1 = (bf16[128]{0:T(256)(128)(2,1)S(1)}, bf16[128]{0:T(256)(128)(2,1)}, u32[]{:S(2)}) copy-start(bf16[128]{0:T(256)(128)(2,1)} %param.19) | copy-start | bytes 772
  66.3 12.2 %copy-start.2 = (bf16[640]{0:T(1024)(128)(2,1)S(1)}, bf16[640]{0:T(1024)(128)(2,1)}, u32[]{:S(2)}) copy-start(bf16[640]{0:T(1024)(128)(2,1)} %param.17) | copy-start | bytes 3844
  70.4 9.9 %collective-permute-start.17 = (bf16[320,256]{1,0:T(8,128)(2,1)S(1)}, bf16[320,256]{1,0:T(8,128)(2,1)S(1)}, u32[]{:S(2)}, u32[]{:S(2)}) collective-permute-start(bf16[320,256]{1,0:T(8,128)(2,1)S(1)} %shard_map.106.refs_0_), channel_id=1, source_target_pairs={{0,48},{8,56},{16,0},{24,8},{32,16},{40,24},{48,32},{56,40},{64,11... | collective-permute-start | bytes 491528 | tf_op jit(solution)/shard_map/ppermute | solution.py:442
  72.7 7.6 %collective-permute-start.18 = (bf16[320,256]{1,0:T(8,128)(2,1)S(1)}, bf16[320,256]{1,0:T(8,128)(2,1)S(1)}, u32[]{:S(2)}, u32[]{:S(2)}) collective-permute-start(bf16[320,256]{1,0:T(8,128)(2,1)S(1)} %shard_map.106.refs_0_), channel_id=1, source_target_pairs={{0,8},{8,0},{16,24},{24,16},{32,40},{40,32},{48,56},{56,48},{64,72... | collective-permute-start | bytes 491528 | tf_op jit(solution)/shard_map/ppermute | solution.py:444
  78.5 7.0 %collective-permute-start.19 = (bf16[320,256]{1,0:T(8,128)(2,1)S(1)}, bf16[320,256]{1,0:T(8,128)(2,1)S(1)}, u32[]{:S(2)}, u32[]{:S(2)}) collective-permute-start(bf16[320,256]{1,0:T(8,128)(2,1)S(1)} %shard_map.106.refs_0_), channel_id=1, source_target_pairs={{0,16},{8,24},{16,32},{24,40},{32,48},{40,56},{48,0},{56,8},{64,80... | collective-permute-start | bytes 491528 | tf_op jit(solution)/shard_map/ppermute | solution.py:441
  85.6 5.5 %collective-permute-start.22 = (bf16[320,256]{1,0:T(8,128)(2,1)S(1)}, bf16[320,256]{1,0:T(8,128)(2,1)S(1)}, u32[]{:S(2)}, u32[]{:S(2)}) collective-permute-start(bf16[320,256]{1,0:T(8,128)(2,1)S(1)} %broadcast_select_fusion.1), channel_id=1, source_target_pairs={{0,48},{8,24},{16,0},{24,40},{32,16},{40,56},{48,32},{56,8},{64,11... | collective-permute-start | bytes 491528 | tf_op jit(solution)/shard_map/ppermute | solution.py:446
  85.7 6.3 %collective-permute-start.21 = (bf16[320,256]{1,0:T(8,128)(2,1)S(1)}, bf16[320,256]{1,0:T(8,128)(2,1)S(1)}, u32[]{:S(2)}, u32[]{:S(2)}) collective-permute-start(bf16[320,256]{1,0:T(8,128)(2,1)S(1)} %collective-permute-done.17.refs_4_), channel_id=1, source_target_pairs={{0,8},{8,0},{16,24},{24,16},{32,40},{40,32},{48,56},{56,48},{64,72... | collective-permute-start | bytes 491528 | tf_op jit(solution)/shard_map/ppermute | solution.py:452
  86.6 5.5 %collective-permute-start.20 = (bf16[320,256]{1,0:T(8,128)(2,1)S(1)}, bf16[320,256]{1,0:T(8,128)(2,1)S(1)}, u32[]{:S(2)}, u32[]{:S(2)}) collective-permute-start(bf16[320,256]{1,0:T(8,128)(2,1)S(1)} %collective-permute-done.19.refs_2_), channel_id=1, source_target_pairs={{0,8},{8,0},{16,24},{24,16},{32,40},{40,32},{48,56},{56,48},{64,72... | collective-permute-start | bytes 491528 | tf_op jit(solution)/shard_map/ppermute | solution.py:452
  91.0 1.8 %collective-permute-start.23 = (bf16[320,256]{1,0:T(8,128)(2,1)S(1)}, bf16[320,256]{1,0:T(8,128)(2,1)S(1)}, u32[]{:S(2)}, u32[]{:S(2)}) collective-permute-start(bf16[320,256]{1,0:T(8,128)(2,1)S(1)} %collective-permute-done.22.refs_6_), channel_id=1, source_target_pairs={{0,8},{8,0},{16,24},{24,16},{32,40},{40,32},{48,56},{56,48},{64,72... | collective-permute-start | bytes 491528 | tf_op jit(solution)/shard_map/ppermute | solution.py:452

commit v7 on v6

--- a/solution.py
+++ b/solution.py
@@ -442,7 +442,7 @@
     above = lax.ppermute(kv, "ctx", ctx_pairs(lambda y, x, c: (y, x - 1, c)))
     swap = ctx_pairs(lambda y, x, c: (y, x, 1 - c))
     beside = lax.ppermute(kv, "ctx", swap)
-    above, beside, q = lax.optimization_barrier((above, beside, q))
+    above, q = lax.optimization_barrier((above, q))
     beyond = lax.ppermute(
         jnp.where(core == 0, above, below), "ctx",
         ctx_pairs(lambda y, x, c: (y, x + (-1 if c == 0 else 1), c)),

time: 114 us -> 114 us (level)
  waiting for transfers between devices: 22 us -> 16 us
  starting transfers between devices: 44.8 us -> 50.5 us
    ppermute x1, waiting for transfers between devices: 4.39 us -> 0.01 us  [per_device(): lax.ppermute(jnp.where(core == 0, above, below), 'ctx', ctx_pairs(lambda...]
    ppermute x3, starting transfers between devices: 1.7 us -> 5.21 us  [per_device(): pieces += [piece, lax.ppermute(piece, 'ctx', swap)]]
    ppermute x1, starting transfers between devices: 5.8 us -> 8.01 us  [per_device(): beside = lax.ppermute(kv, 'ctx', swap)]
    ppermute x1, waiting for transfers between devices: 5.18 us -> 3.12 us  [per_device(): below = lax.ppermute(kv, 'ctx', ctx_pairs(lambda y, x, c: (y, x + 1, c)))]
where the time goes in v7:
time: 114 us; the launch traced here: 113 us
  starting transfers between devices  50.5 us (44%)
  Pallas kernels  24.4 us (21%)
  waiting for transfers between devices  16 us (14%)
  blocking collectives  14.1 us (12%)
  local copies, waits for them, and re-layouts  6.68 us (6%)
  other arithmetic  1.29 us (1%)
    ppermute x6, starting transfers between devices, per_device(): bwd[h] = lax.ppermute(bwd[h], 'mp', shifted(PLANES, -1))  17.4 us
    all_to_all x1, blocking collectives, per_device(): recv = lax.all_to_all(send, 'ctx', 0, 0, tiled=True)  14.1 us
    pallas_call x4, Pallas kernels, add_products(): pl.pallas_call(functools.partial(products_kernel, groups, halves, sums is...  12.1 us
    all_to_all x1, starting transfers between devices, per_device(): sent = lax.all_to_all(sent, 'ctx', 0, 0, tiled=True)  8.6 us
    ppermute x1, starting transfers between devices, per_device(): beside = lax.ppermute(kv, 'ctx', swap)  8.01 us
    all_to_all x1, waiting for transfers between devices, per_device(): sent = lax.all_to_all(sent, 'ctx', 0, 0, tiled=True)  7.55 us
    pallas_call x1, Pallas kernels, attend(): pl.pallas_call(functools.partial(attend_kernel, heads, clips), out_shape=...  5.79 us
    ppermute x3, starting transfers between devices, per_device(): pieces += [piece, lax.ppermute(piece, 'ctx', swap)]  5.21 us
  transfers between devices with their start and end apart: 25, of which 8 were waited for; matrix products, arithmetic and copies ran while one was open for 6% of the time, Pallas kernels for 12%

profile of v7, /device:TPU:1, one launch (start us, length us, event | category | flops | bytes accessed | tf_op | source)
XLA Modules:
  0.0 113.4 jit_solution(9590386780813906744)
XLA Ops:
  0.0 3.3 %shard_map.100 = bf16[32,16,768]{2,1,0:T(8,128)(2,1)} custom-call(s32[4,4]{1,0:T(4,128)} %cand_ref.3, s32[64]{0:T(128)} %slot_ref.3, s32[1]{0:T(128)} %bitcast.2.me_ref, bf16[2,512,640]{2,1,0:T(8,128)(2,1)} %clip_hbm.1, bf16[4,16,640]{2,1,0:T(8,128)(2,1)} %text_ref.1), custom_call_target="tpu_custom_call" | custom-call | tf_op jit(solution)/shard_map/pallas_call | solution.py:218
  3.4 8.6 %all-to-all-start = ((bf16[32,16,768]{2,1,0:T(8,128)(2,1)}), bf16[32,16,768]{2,1,0:T(8,128)(2,1)S(1)}, u32[]{:S(2)}, u32[]{:S(2)}) async-start(bf16[32,16,768]{2,1,0:T(8,128)(2,1)} %shard_map.100), calls=%async_computation | async-start | bytes 1572864 | tf_op jit(solution)/shard_map/all_to_all | solution.py:387
  12.9 3.6 %copy.19 = bf16[640,8,2,128]{3,1,2,0:T(8,128)(2,1)} copy(bf16[640,8,2,128]{3,2,1,0:T(2,128)(2,1)} %bitcast.28) | data formatting | bytes 5242880
  16.8 1.0 constant_dynamic-slice_fusion.refs_2_
  18.6 7.5 %all-to-all-done.sent_ref = bf16[32,16,768]{2,1,0:T(8,128)(2,1)S(1)} async-done(((bf16[32,16,768]{2,1,0:T(8,128)(2,1)}), bf16[32,16,768]{2,1,0:T(8,128)(2,1)S(1)}, u32[]{:S(2)}, u32[]{:S(2)}) %all-to-all-start) | async-done | bytes 786464 | tf_op jit(solution)/shard_map/all_to_all | solution.py:387
  26.2 1.0 shard_map.101
  27.2 1.3 %collective-permute-start = (bf16[64,640]{1,0:T(8,128)(2,1)S(1)}, bf16[64,640]{1,0:T(8,128)(2,1)S(1)}, u32[]{:S(2)}, u32[]{:S(2)}) collective-permute-start(bf16[64,640]{1,0:T(8,128)(2,1)S(1)} %get-tuple-element.44), channel_id=1, source_target_pairs={{0,128},{8,136},{16,144},{24,152},{32,160},{40,168},{48,176},{56,1... | collective-permute-start | bytes 245768 | tf_op jit(solution)/shard_map/ppermute | solution.py:414
  28.5 2.7 %collective-permute-start.9 = (bf16[64,640]{1,0:T(8,128)(2,1)S(1)}, bf16[64,640]{1,0:T(8,128)(2,1)S(1)}, u32[]{:S(2)}, u32[]{:S(2)}) collective-permute-start(bf16[64,640]{1,0:T(8,128)(2,1)S(1)} %get-tuple-element.48), channel_id=1, source_target_pairs={{0,192},{8,200},{16,208},{24,216},{32,224},{40,232},{48,240},{56,2... | collective-permute-start | bytes 245768 | tf_op jit(solution)/shard_map/ppermute | solution.py:414
  31.2 0.9 collective-permute-done
  32.1 1.6 %collective-permute-start.1 = (bf16[128,640]{1,0:T(8,128)(2,1)S(1)}, bf16[128,640]{1,0:T(8,128)(2,1)S(1)}, u32[]{:S(2)}, u32[]{:S(2)}) collective-permute-start(bf16[128,640]{1,0:T(8,128)(2,1)S(1)} %get-tuple-element.45.refs_0_), channel_id=1, source_target_pairs={{0,1},{1,2},{2,3},{3,4},{4,5},{5,6},{6,7},{7,0},{8,9},{9,10},{10,1... | collective-permute-start | bytes 491528 | tf_op jit(solution)/shard_map/ppermute | solution.py:424
  33.7 3.9 %collective-permute-start.4 = (bf16[128,640]{1,0:T(8,128)(2,1)S(1)}, bf16[128,640]{1,0:T(8,128)(2,1)S(1)}, u32[]{:S(2)}, u32[]{:S(2)}) collective-permute-start(bf16[128,640]{1,0:T(8,128)(2,1)S(1)} %get-tuple-element.45.refs_0_), channel_id=1, source_target_pairs={{0,7},{1,0},{2,1},{3,2},{4,3},{5,4},{6,5},{7,6},{8,15},{9,8},{10,9... | collective-permute-start | bytes 491528 | tf_op jit(solution)/shard_map/ppermute | solution.py:425
  37.8 2.8 %collective-permute-start.11 = (bf16[192,640]{1,0:T(8,128)(2,1)S(1)}, bf16[192,640]{1,0:T(8,128)(2,1)S(1)}, u32[]{:S(2)}, u32[]{:S(2)}) collective-permute-start(bf16[192,640]{1,0:T(8,128)(2,1)S(1)} %constant_dynamic-update-slice_fusion.refs_1_), channel_id=1, source_target_pairs={{0,7},{1,0},{2,1},{3,2},{4,3},{5,4},{6,5},{7,6},{8,15},{9,8},{10,9... | collective-permute-start | bytes 737288 | tf_op jit(solution)/shard_map/ppermute | solution.py:425
  40.6 2.7 %collective-permute-start.5 = (bf16[128,640]{1,0:T(8,128)(2,1)S(1)}, bf16[128,640]{1,0:T(8,128)(2,1)}, u32[]{:S(2)}, u32[]{:S(2)}) collective-permute-start(bf16[128,640]{1,0:T(8,128)(2,1)S(1)} %collective-permute-done.4.refs_2_), channel_id=1, source_target_pairs={{0,7},{1,0},{2,1},{3,2},{4,3},{5,4},{6,5},{7,6},{8,15},{9,8},{10,9... | collective-permute-start | bytes 491528 | tf_op jit(solution)/shard_map/ppermute | solution.py:425
  43.3 1.9 %shard_map.102 = (f32[320,640]{1,0:T(8,128)S(1)}, f32[320,256]{1,0:T(8,128)S(1)}) custom-call(s32[1]{0:T(128)} %bitcast.3.owners_ref, bf16[5120,640]{1,0:T(8,128)(2,1)} %w_hbm.1, bf16[5120,256]{1,0:T(8,128)(2,1)} %bitcast.24, bf16[128,640]{1,0:T(8,128)(2,1)S(1)} %get-tuple-element.45.refs_0_, bf16[192,640]{1,0:T(8,128)(2,1)S(1)} %constant_dynamic-update-slice_fusion.refs_1_), custom_call_target="tpu_custom_call" | custom-call | flops 734003200 | bytes 1146880 | tf_op jit(solution)/shard_map/pallas_call | solution.py:96
  45.2 1.8 %collective-permute-done.10.refs_1_ = bf16[192,640]{1,0:T(8,128)(2,1)S(1)} collective-permute-done((bf16[192,640]{1,0:T(8,128)(2,1)S(1)}, bf16[192,640]{1,0:T(8,128)(2,1)S(1)}, u32[]{:S(2)}, u32[]{:S(2)}) %collective-permute-start.10) | collective-permute-done | bytes 245792 | tf_op jit(solution)/shard_map/ppermute | solution.py:424
  47.0 2.7 %collective-permute-start.13 = (bf16[192,640]{1,0:T(8,128)(2,1)S(1)}, bf16[192,640]{1,0:T(8,128)(2,1)S(1)}, u32[]{:S(2)}, u32[]{:S(2)}) collective-permute-start(bf16[192,640]{1,0:T(8,128)(2,1)S(1)} %collective-permute-done.11.refs_3_), channel_id=1, source_target_pairs={{0,7},{1,0},{2,1},{3,2},{4,3},{5,4},{6,5},{7,6},{8,15},{9,8},{10,9... | collective-permute-start | bytes 737288 | tf_op jit(solution)/shard_map/ppermute | solution.py:425
  49.7 0.9 collective-permute-done.2.refs_0_
  50.6 2.7 %collective-permute-start.6 = (bf16[128,640]{1,0:T(8,128)(2,1)}, bf16[128,640]{1,0:T(8,128)(2,1)S(1)}, u32[]{:S(2)}, u32[]{:S(2)}) collective-permute-start(bf16[128,640]{1,0:T(8,128)(2,1)} %collective-permute-done.5.refs_2_), channel_id=1, source_target_pairs={{0,7},{1,0},{2,1},{3,2},{4,3},{5,4},{6,5},{7,6},{8,15},{9,8},{10,9... | collective-permute-start | bytes 491528 | tf_op jit(solution)/shard_map/ppermute | solution.py:425
  53.4 3.2 %shard_map.103 = (f32[320,640]{1,0:T(8,128)S(1)}, f32[320,256]{1,0:T(8,128)S(1)}) custom-call(s32[2]{0:T(128)S(1)} %pad_add_fusion.1.owners_ref, bf16[5120,640]{1,0:T(8,128)(2,1)} %w_hbm.1, bf16[5120,256]{1,0:T(8,128)(2,1)} %bitcast.25, bf16[128,640]{1,0:T(8,128)(2,1)S(1)} %collective-permute-done.1.refs_0_, ...), custom_call_target="tpu_custom_call" | custom-call | flops 1468006400 | bytes 2293760 | tf_op jit(solution)/shard_map/pallas_call | solution.py:96
  56.7 2.7 %collective-permute-start.15 = (bf16[192,640]{1,0:T(8,128)(2,1)S(1)}, bf16[192,640]{1,0:T(8,128)(2,1)S(1)}, u32[]{:S(2)}, u32[]{:S(2)}) collective-permute-start(bf16[192,640]{1,0:T(8,128)(2,1)S(1)} %collective-permute-done.13.refs_3_), channel_id=1, source_target_pairs={{0,7},{1,0},{2,1},{3,2},{4,3},{5,4},{6,5},{7,6},{8,15},{9,8},{10,9... | collective-permute-start | bytes 737288 | tf_op jit(solution)/shard_map/ppermute | solution.py:425
  59.4 1.3 %collective-permute-start.7 = (bf16[128,640]{1,0:T(8,128)(2,1)S(1)}, bf16[128,640]{1,0:T(8,128)(2,1)S(1)}, u32[]{:S(2)}, u32[]{:S(2)}) collective-permute-start(bf16[128,640]{1,0:T(8,128)(2,1)S(1)} %broadcast_select_fusion.2), channel_id=1, source_target_pairs={{0,1},{1,2},{2,3},{3,4},{4,5},{5,6},{6,7},{7,0},{8,15},{9,8},{10,9... | collective-permute-start | bytes 491528 | tf_op jit(solution)/shard_map/ppermute | solution.py:433
  60.7 3.7 %shard_map.104 = (f32[320,640]{1,0:T(8,128)S(1)}, f32[320,256]{1,0:T(8,128)S(1)}) custom-call(s32[2]{0:T(128)S(1)} %pad_add_fusion.2.owners_ref, bf16[5120,640]{1,0:T(8,128)(2,1)} %w_hbm.1, bf16[5120,256]{1,0:T(8,128)(2,1)} %bitcast.26, bf16[128,640]{1,0:T(8,128)(2,1)} %collective-permute-done.2.refs_0_, ...), custom_call_target="tpu_custom_call" | custom-call | flops 1468006400 | bytes 2293760 | tf_op jit(solution)/shard_map/pallas_call | solution.py:96
  64.5 1.8 %collective-permute-start.16 = (bf16[192,640]{1,0:T(8,128)(2,1)S(1)}, bf16[192,640]{1,0:T(8,128)(2,1)S(1)}, u32[]{:S(2)}, u32[]{:S(2)}) collective-permute-start(bf16[192,640]{1,0:T(8,128)(2,1)S(1)} %broadcast_select_fusion), channel_id=1, source_target_pairs={{0,1},{1,2},{2,3},{3,4},{4,5},{5,6},{6,7},{7,0},{8,15},{9,8},{10,9... | collective-permute-start | bytes 737288 | tf_op jit(solution)/shard_map/ppermute | solution.py:433
  66.3 3.2 %shard_map.105 = (f32[320,640]{1,0:T(8,128)S(1)}, f32[320,256]{1,0:T(8,128)S(1)}) custom-call(s32[2]{0:T(128)S(1)} %pad_add_fusion.3.owners_ref, bf16[5120,640]{1,0:T(8,128)(2,1)} %w_hbm.1, bf16[5120,256]{1,0:T(8,128)(2,1)} %bitcast.27, bf16[128,640]{1,0:T(8,128)(2,1)S(1)} %collective-permute-done.3.refs_0_, ...), custom_call_target="tpu_custom_call" | custom-call | flops 1468006400 | bytes 2293760 | tf_op jit(solution)/shard_map/pallas_call | solution.py:96
  70.4 2.3 %collective-permute-start.17 = (bf16[320,256]{1,0:T(8,128)(2,1)S(1)}, bf16[320,256]{1,0:T(8,128)(2,1)S(1)}, u32[]{:S(2)}, u32[]{:S(2)}) collective-permute-start(bf16[320,256]{1,0:T(8,128)(2,1)S(1)} %shard_map.106.refs_0_), channel_id=1, source_target_pairs={{0,48},{8,56},{16,0},{24,8},{32,16},{40,24},{48,32},{56,40},{64,11... | collective-permute-start | bytes 491528 | tf_op jit(solution)/shard_map/ppermute | solution.py:442
  72.7 1.8 %shard_map.107.q_ref = bf16[320,640]{1,0:T(8,128)(2,1)S(1)} custom-call(s32[1]{0:T(128)} %bitcast.11.owner_ref, bf16[5120,640]{1,0:T(8,128)(2,1)} %w_hbm.1, bf16[128,640]{1,0:T(8,128)(2,1)S(1)} %collective-permute-done.7.refs_0_, bf16[192,640]{1,0:T(8,128)(2,1)S(1)} %collective-permute-done.16.refs_1_, f32[320,640]{1,0:T(8,128)S(1)} %get-tuple-element.75.refs_2_, ...), custom_call_target="tpu_custom_call" | custom-call | flops 524288000 | bytes 2000000 | tf_op jit(solution)/shard_map/pallas_call | solution.py:159
  75.0 3.1 %collective-permute-done.19.refs_2_ = bf16[320,256]{1,0:T(8,128)(2,1)S(1)} collective-permute-done((bf16[320,256]{1,0:T(8,128)(2,1)S(1)}, bf16[320,256]{1,0:T(8,128)(2,1)S(1)}, u32[]{:S(2)}, u32[]{:S(2)}) %collective-permute-start.19) | collective-permute-done | bytes 163872 | tf_op jit(solution)/shard_map/ppermute | solution.py:441
  78.2 8.0 %collective-permute-start.18 = (bf16[320,256]{1,0:T(8,128)(2,1)S(1)}, bf16[320,256]{1,0:T(8,128)(2,1)S(1)}, u32[]{:S(2)}, u32[]{:S(2)}) collective-permute-start(bf16[320,256]{1,0:T(8,128)(2,1)S(1)} %shard_map.106.refs_0_), channel_id=1, source_target_pairs={{0,8},{8,0},{16,24},{24,16},{32,40},{40,32},{48,56},{56,48},{64,72... | collective-permute-start | bytes 491528 | tf_op jit(solution)/shard_map/ppermute | solution.py:444
  86.7 4.7 %collective-permute-start.23 = (bf16[320,256]{1,0:T(8,128)(2,1)S(1)}, bf16[320,256]{1,0:T(8,128)(2,1)S(1)}, u32[]{:S(2)}, u32[]{:S(2)}) collective-permute-start(bf16[320,256]{1,0:T(8,128)(2,1)S(1)} %collective-permute-done.22.refs_6_), channel_id=1, source_target_pairs={{0,8},{8,0},{16,24},{24,16},{32,40},{40,32},{48,56},{56,48},{64,72... | collective-permute-start | bytes 491528 | tf_op jit(solution)/shard_map/ppermute | solution.py:452
  92.5 5.8 %shard_map.108 = bf16[320,640]{1,0:T(8,128)(2,1)S(1)} custom-call(s32[2]{0:T(128)S(1)} %pad_add_fusion.info_ref, bf16[320,640]{1,0:T(8,128)(2,1)S(1)} %shard_map.107.q_ref, s32[320,1]{1,0:T(8,128)S(1)} %copy.14.to_ref, bf16[320,256]{1,0:T(8,128)(2,1)S(1)} %shard_map.106.refs_0_, bf16[320,256]{1,0:T(8,128)(2,1)S(1)} %collective-permute-done.18.refs_1_, ...), custom_call_target="tpu_custom_call" | custom-call | flops 1300000000 | bytes 4000000 | tf_op jit(solution)/shard_map/pallas_call | solution.py:351
  98.4 14.1 %all_to_all.10 = bf16[32,5,2,640]{3,2,1,0:T(2,128)(2,1)S(1)} all-to-all(bf16[32,5,2,640]{3,2,1,0:T(2,128)(2,1)S(1)} %reshape.162), channel_id=1, replica_groups=mesh['ctx'=32,'mp'=8] {'ctx'}, dimensions={0} | all-to-all | bytes 819200 | tf_op jit(solution)/shard_map/all_to_all | solution.py:458
  112.6 0.8 copy.20
  (70 shorter events, 5.4 us)
Async XLA Ops:
  0.0 12.5 %copy-start = (s32[4,512]{1,0:T(4,128)S(1)}, s32[4,512]{1,0:T(4,128)}, u32[]{:S(2)}) copy-start(s32[4,512]{1,0:T(4,128)} %param.14) | copy-start | bytes 24580
  3.4 22.8 %all-to-all-start = ((bf16[32,16,768]{2,1,0:T(8,128)(2,1)}), bf16[32,16,768]{2,1,0:T(8,128)(2,1)S(1)}, u32[]{:S(2)}, u32[]{:S(2)}) async-start(bf16[32,16,768]{2,1,0:T(8,128)(2,1)} %shard_map.100), calls=%async_computation | async-start | bytes 1572864 | tf_op jit(solution)/shard_map/all_to_all | solution.py:387
  12.9 3.6 %copy-start.3 = (s32[64]{0:T(128)S(1)}, s32[64]{0:T(128)}, u32[]{:S(2)}) copy-start(s32[64]{0:T(128)} %param.15) | copy-start | bytes 772
  27.2 4.9 %collective-permute-start = (bf16[64,640]{1,0:T(8,128)(2,1)S(1)}, bf16[64,640]{1,0:T(8,128)(2,1)S(1)}, u32[]{:S(2)}, u32[]{:S(2)}) collective-permute-start(bf16[64,640]{1,0:T(8,128)(2,1)S(1)} %get-tuple-element.44), channel_id=1, source_target_pairs={{0,128},{8,136},{16,144},{24,152},{32,160},{40,168},{48,176},{56,1... | collective-permute-start | bytes 245768 | tf_op jit(solution)/shard_map/ppermute | solution.py:414
  28.5 9.1 %collective-permute-start.8 = (bf16[64,640]{1,0:T(8,128)(2,1)S(1)}, bf16[64,640]{1,0:T(8,128)(2,1)S(1)}, u32[]{:S(2)}, u32[]{:S(2)}) collective-permute-start(bf16[64,640]{1,0:T(8,128)(2,1)S(1)} %get-tuple-element.46), channel_id=1, source_target_pairs={{0,64},{8,72},{16,80},{24,88},{32,96},{40,104},{48,112},{56,120},{... | collective-permute-start | bytes 245768 | tf_op jit(solution)/shard_map/ppermute | solution.py:414
  28.5 9.2 %collective-permute-start.9 = (bf16[64,640]{1,0:T(8,128)(2,1)S(1)}, bf16[64,640]{1,0:T(8,128)(2,1)S(1)}, u32[]{:S(2)}, u32[]{:S(2)}) collective-permute-start(bf16[64,640]{1,0:T(8,128)(2,1)S(1)} %get-tuple-element.48), channel_id=1, source_target_pairs={{0,192},{8,200},{16,208},{24,216},{32,224},{40,232},{48,240},{56,2... | collective-permute-start | bytes 245768 | tf_op jit(solution)/shard_map/ppermute | solution.py:414
  32.1 8.5 %collective-permute-start.1 = (bf16[128,640]{1,0:T(8,128)(2,1)S(1)}, bf16[128,640]{1,0:T(8,128)(2,1)S(1)}, u32[]{:S(2)}, u32[]{:S(2)}) collective-permute-start(bf16[128,640]{1,0:T(8,128)(2,1)S(1)} %get-tuple-element.45.refs_0_), channel_id=1, source_target_pairs={{0,1},{1,2},{2,3},{3,4},{4,5},{5,6},{6,7},{7,0},{8,9},{9,10},{10,1... | collective-permute-start | bytes 491528 | tf_op jit(solution)/shard_map/ppermute | solution.py:424
  33.7 6.9 %collective-permute-start.4 = (bf16[128,640]{1,0:T(8,128)(2,1)S(1)}, bf16[128,640]{1,0:T(8,128)(2,1)S(1)}, u32[]{:S(2)}, u32[]{:S(2)}) collective-permute-start(bf16[128,640]{1,0:T(8,128)(2,1)S(1)} %get-tuple-element.45.refs_0_), channel_id=1, source_target_pairs={{0,7},{1,0},{2,1},{3,2},{4,3},{5,4},{6,5},{7,6},{8,15},{9,8},{10,9... | collective-permute-start | bytes 491528 | tf_op jit(solution)/shard_map/ppermute | solution.py:425
  37.7 9.3 %collective-permute-start.10 = (bf16[192,640]{1,0:T(8,128)(2,1)S(1)}, bf16[192,640]{1,0:T(8,128)(2,1)S(1)}, u32[]{:S(2)}, u32[]{:S(2)}) collective-permute-start(bf16[192,640]{1,0:T(8,128)(2,1)S(1)} %constant_dynamic-update-slice_fusion.refs_1_), channel_id=1, source_target_pairs={{0,1},{1,2},{2,3},{3,4},{4,5},{5,6},{6,7},{7,0},{8,9},{9,10},{10,1... | collective-permute-start | bytes 737288 | tf_op jit(solution)/shard_map/ppermute | solution.py:424
  37.8 9.2 %collective-permute-start.11 = (bf16[192,640]{1,0:T(8,128)(2,1)S(1)}, bf16[192,640]{1,0:T(8,128)(2,1)S(1)}, u32[]{:S(2)}, u32[]{:S(2)}) collective-permute-start(bf16[192,640]{1,0:T(8,128)(2,1)S(1)} %constant_dynamic-update-slice_fusion.refs_1_), channel_id=1, source_target_pairs={{0,7},{1,0},{2,1},{3,2},{4,3},{5,4},{6,5},{7,6},{8,15},{9,8},{10,9... | collective-permute-start | bytes 737288 | tf_op jit(solution)/shard_map/ppermute | solution.py:425
  40.6 10.0 %collective-permute-start.2 = (bf16[128,640]{1,0:T(8,128)(2,1)S(1)}, bf16[128,640]{1,0:T(8,128)(2,1)}, u32[]{:S(2)}, u32[]{:S(2)}) collective-permute-start(bf16[128,640]{1,0:T(8,128)(2,1)S(1)} %collective-permute-done.1.refs_0_), channel_id=1, source_target_pairs={{0,1},{1,2},{2,3},{3,4},{4,5},{5,6},{6,7},{7,0},{8,9},{9,10},{10,1... | collective-permute-start | bytes 491528 | tf_op jit(solution)/shard_map/ppermute | solution.py:424
  40.6 10.0 %collective-permute-start.5 = (bf16[128,640]{1,0:T(8,128)(2,1)S(1)}, bf16[128,640]{1,0:T(8,128)(2,1)}, u32[]{:S(2)}, u32[]{:S(2)}) collective-permute-start(bf16[128,640]{1,0:T(8,128)(2,1)S(1)} %collective-permute-done.4.refs_2_), channel_id=1, source_target_pairs={{0,7},{1,0},{2,1},{3,2},{4,3},{5,4},{6,5},{7,6},{8,15},{9,8},{10,9... | collective-permute-start | bytes 491528 | tf_op jit(solution)/shard_map/ppermute | solution.py:425
  47.0 9.6 %collective-permute-start.12 = (bf16[192,640]{1,0:T(8,128)(2,1)S(1)}, bf16[192,640]{1,0:T(8,128)(2,1)S(1)}, u32[]{:S(2)}, u32[]{:S(2)}) collective-permute-start(bf16[192,640]{1,0:T(8,128)(2,1)S(1)} %collective-permute-done.10.refs_1_), channel_id=1, source_target_pairs={{0,1},{1,2},{2,3},{3,4},{4,5},{5,6},{6,7},{7,0},{8,9},{9,10},{10,1... | collective-permute-start | bytes 737288 | tf_op jit(solution)/shard_map/ppermute | solution.py:424
  47.0 9.6 %collective-permute-start.13 = (bf16[192,640]{1,0:T(8,128)(2,1)S(1)}, bf16[192,640]{1,0:T(8,128)(2,1)S(1)}, u32[]{:S(2)}, u32[]{:S(2)}) collective-permute-start(bf16[192,640]{1,0:T(8,128)(2,1)S(1)} %collective-permute-done.11.refs_3_), channel_id=1, source_target_pairs={{0,7},{1,0},{2,1},{3,2},{4,3},{5,4},{6,5},{7,6},{8,15},{9,8},{10,9... | collective-permute-start | bytes 737288 | tf_op jit(solution)/shard_map/ppermute | solution.py:425
  50.6 8.8 %collective-permute-start.3 = (bf16[128,640]{1,0:T(8,128)(2,1)}, bf16[128,640]{1,0:T(8,128)(2,1)S(1)}, u32[]{:S(2)}, u32[]{:S(2)}) collective-permute-start(bf16[128,640]{1,0:T(8,128)(2,1)} %collective-permute-done.2.refs_0_), channel_id=1, source_target_pairs={{0,1},{1,2},{2,3},{3,4},{4,5},{5,6},{6,7},{7,0},{8,9},{9,10},{10,1... | collective-permute-start | bytes 491528 | tf_op jit(solution)/shard_map/ppermute | solution.py:424
  50.6 8.8 %collective-permute-start.6 = (bf16[128,640]{1,0:T(8,128)(2,1)}, bf16[128,640]{1,0:T(8,128)(2,1)S(1)}, u32[]{:S(2)}, u32[]{:S(2)}) collective-permute-start(bf16[128,640]{1,0:T(8,128)(2,1)} %collective-permute-done.5.refs_2_), channel_id=1, source_target_pairs={{0,7},{1,0},{2,1},{3,2},{4,3},{5,4},{6,5},{7,6},{8,15},{9,8},{10,9... | collective-permute-start | bytes 491528 | tf_op jit(solution)/shard_map/ppermute | solution.py:425
  56.6 7.8 %collective-permute-start.14 = (bf16[192,640]{1,0:T(8,128)(2,1)S(1)}, bf16[192,640]{1,0:T(8,128)(2,1)S(1)}, u32[]{:S(2)}, u32[]{:S(2)}) collective-permute-start(bf16[192,640]{1,0:T(8,128)(2,1)S(1)} %collective-permute-done.12.refs_1_), channel_id=1, source_target_pairs={{0,1},{1,2},{2,3},{3,4},{4,5},{5,6},{6,7},{7,0},{8,9},{9,10},{10,1... | collective-permute-start | bytes 737288 | tf_op jit(solution)/shard_map/ppermute | solution.py:424
  56.7 7.7 %collective-permute-start.15 = (bf16[192,640]{1,0:T(8,128)(2,1)S(1)}, bf16[192,640]{1,0:T(8,128)(2,1)S(1)}, u32[]{:S(2)}, u32[]{:S(2)}) collective-permute-start(bf16[192,640]{1,0:T(8,128)(2,1)S(1)} %collective-permute-done.13.refs_3_), channel_id=1, source_target_pairs={{0,7},{1,0},{2,1},{3,2},{4,3},{5,4},{6,5},{7,6},{8,15},{9,8},{10,9... | collective-permute-start | bytes 737288 | tf_op jit(solution)/shard_map/ppermute | solution.py:425
  59.4 10.6 %collective-permute-start.7 = (bf16[128,640]{1,0:T(8,128)(2,1)S(1)}, bf16[128,640]{1,0:T(8,128)(2,1)S(1)}, u32[]{:S(2)}, u32[]{:S(2)}) collective-permute-start(bf16[128,640]{1,0:T(8,128)(2,1)S(1)} %broadcast_select_fusion.2), channel_id=1, source_target_pairs={{0,1},{1,2},{2,3},{3,4},{4,5},{5,6},{6,7},{7,0},{8,15},{9,8},{10,9... | collective-permute-start | bytes 491528 | tf_op jit(solution)/shard_map/ppermute | solution.py:433
  64.5 5.6 %collective-permute-start.16 = (bf16[192,640]{1,0:T(8,128)(2,1)S(1)}, bf16[192,640]{1,0:T(8,128)(2,1)S(1)}, u32[]{:S(2)}, u32[]{:S(2)}) collective-permute-start(bf16[192,640]{1,0:T(8,128)(2,1)S(1)} %broadcast_select_fusion), channel_id=1, source_target_pairs={{0,1},{1,2},{2,3},{3,4},{4,5},{5,6},{6,7},{7,0},{8,15},{9,8},{10,9... | collective-permute-start | bytes 737288 | tf_op jit(solution)/shard_map/ppermute | solution.py:433
  66.3 3.7 %copy-start.1 = (bf16[128]{0:T(256)(128)(2,1)S(1)}, bf16[128]{0:T(256)(128)(2,1)}, u32[]{:S(2)}) copy-start(bf16[128]{0:T(256)(128)(2,1)} %param.19) | copy-start | bytes 772
  66.3 6.4 %copy-start.2 = (bf16[640]{0:T(1024)(128)(2,1)S(1)}, bf16[640]{0:T(1024)(128)(2,1)}, u32[]{:S(2)}) copy-start(bf16[640]{0:T(1024)(128)(2,1)} %param.17) | copy-start | bytes 3844
  70.4 4.6 %collective-permute-start.17 = (bf16[320,256]{1,0:T(8,128)(2,1)S(1)}, bf16[320,256]{1,0:T(8,128)(2,1)S(1)}, u32[]{:S(2)}, u32[]{:S(2)}) collective-permute-start(bf16[320,256]{1,0:T(8,128)(2,1)S(1)} %shard_map.106.refs_0_), channel_id=1, source_target_pairs={{0,48},{8,56},{16,0},{24,8},{32,16},{40,24},{48,32},{56,40},{64,11... | collective-permute-start | bytes 491528 | tf_op jit(solution)/shard_map/ppermute | solution.py:442
  72.7 5.4 %collective-permute-start.19 = (bf16[320,256]{1,0:T(8,128)(2,1)S(1)}, bf16[320,256]{1,0:T(8,128)(2,1)S(1)}, u32[]{:S(2)}, u32[]{:S(2)}) collective-permute-start(bf16[320,256]{1,0:T(8,128)(2,1)S(1)} %shard_map.106.refs_0_), channel_id=1, source_target_pairs={{0,16},{8,24},{16,32},{24,40},{32,48},{40,56},{48,0},{56,8},{64,80... | collective-permute-start | bytes 491528 | tf_op jit(solution)/shard_map/ppermute | solution.py:441
  78.1 8.6 %collective-permute-start.22 = (bf16[320,256]{1,0:T(8,128)(2,1)S(1)}, bf16[320,256]{1,0:T(8,128)(2,1)S(1)}, u32[]{:S(2)}, u32[]{:S(2)}) collective-permute-start(bf16[320,256]{1,0:T(8,128)(2,1)S(1)} %broadcast_select_fusion.1), channel_id=1, source_target_pairs={{0,48},{8,24},{16,0},{24,40},{32,16},{40,56},{48,32},{56,8},{64,11... | collective-permute-start | bytes 491528 | tf_op jit(solution)/shard_map/ppermute | solution.py:446
  78.2 13.5 %collective-permute-start.18 = (bf16[320,256]{1,0:T(8,128)(2,1)S(1)}, bf16[320,256]{1,0:T(8,128)(2,1)S(1)}, u32[]{:S(2)}, u32[]{:S(2)}) collective-permute-start(bf16[320,256]{1,0:T(8,128)(2,1)S(1)} %shard_map.106.refs_0_), channel_id=1, source_target_pairs={{0,8},{8,0},{16,24},{24,16},{32,40},{40,32},{48,56},{56,48},{64,72... | collective-permute-start | bytes 491528 | tf_op jit(solution)/shard_map/ppermute | solution.py:444
  86.2 5.5 %collective-permute-start.21 = (bf16[320,256]{1,0:T(8,128)(2,1)S(1)}, bf16[320,256]{1,0:T(8,128)(2,1)S(1)}, u32[]{:S(2)}, u32[]{:S(2)}) collective-permute-start(bf16[320,256]{1,0:T(8,128)(2,1)S(1)} %collective-permute-done.17.refs_4_), channel_id=1, source_target_pairs={{0,8},{8,0},{16,24},{24,16},{32,40},{40,32},{48,56},{56,48},{64,72... | collective-permute-start | bytes 491528 | tf_op jit(solution)/shard_map/ppermute | solution.py:452
  86.3 5.4 %collective-permute-start.20 = (bf16[320,256]{1,0:T(8,128)(2,1)S(1)}, bf16[320,256]{1,0:T(8,128)(2,1)S(1)}, u32[]{:S(2)}, u32[]{:S(2)}) collective-permute-start(bf16[320,256]{1,0:T(8,128)(2,1)S(1)} %collective-permute-done.19.refs_2_), channel_id=1, source_target_pairs={{0,8},{8,0},{16,24},{24,16},{32,40},{40,32},{48,56},{56,48},{64,72... | collective-permute-start | bytes 491528 | tf_op jit(solution)/shard_map/ppermute | solution.py:452
  86.7 5.7 %collective-permute-start.23 = (bf16[320,256]{1,0:T(8,128)(2,1)S(1)}, bf16[320,256]{1,0:T(8,128)(2,1)S(1)}, u32[]{:S(2)}, u32[]{:S(2)}) collective-permute-start(bf16[320,256]{1,0:T(8,128)(2,1)S(1)} %collective-permute-done.22.refs_6_), channel_id=1, source_target_pairs={{0,8},{8,0},{16,24},{24,16},{32,40},{40,32},{48,56},{56,48},{64,72... | collective-permute-start | bytes 491528 | tf_op jit(solution)/shard_map/ppermute | solution.py:452
